TPU v7x, 32 devices: a whole 2x2x4 slice. The times are simulated.
32 devices in a mesh: row: 8 (over z, x), col: 4 (over y, core).
Axes of the slice: x: 2, y: 2, z: 4, core: 2. Of those that a mesh axis runs over, the one named last changes fastest.
Arguments:
- potential: float32 [16, 16, 512], P('row', 'col'), may hold values from -6 to 6
- basis: bfloat16 [16, 16, 384, 512], P('row', 'col'), may hold values from -6 to 6
- hamiltonian: bfloat16 [3072, 3072], P('row', 'col'), may hold values from -0.109375 to 0.109375
- density: bfloat16 [2, 3072, 3072], P(None, 'row', 'col'), may hold values from -6 to 6
- hmask: int32 [24, 24], replicated, may hold values from 0 to 1, as said below
- pmask: int32 [24, 24], replicated, may hold values from 0 to 1, as said below
Outputs:
- propagated: bfloat16 [2, 3072, 3072], P(None, 'row', 'col')
Inputs may be any that keep to these rules, and one draw needn't show every extreme that they name: hmask[I, I] is always 1; every other block is 1 with probability 1/2, independently. pmask follows the same law as hmask, drawn independently.
All inputs are finite; a program needn't handle non-finite values.
Results may differ from a plain program's by a relative error of at most 0.0062.
Values may be sent and summed in bfloat16 or wider, within the bound.
No kernel may reach another device: no remote copies, remote signals or barrier semaphores. Data moves between devices by JAX's collectives and lax.ppermute only.
A program may use at most 64 MiB of HBM per device.

v0:
```python
import jax
import jax.numpy as jnp
from jax import lax
from jax.sharding import PartitionSpec as P

BLK = 128


KAPPA = 0.4
TIME_STEP = 0.5


def extended_2(block, sides, width):
    for axis, dim in sides:
        count = lax.axis_size(axis)
        forward = [(i, i + 1) for i in range(count - 1)]
        backward = [(target, source) for source, target in forward]
        low = lax.ppermute(
            lax.slice_in_dim(block, block.shape[dim] - width, None, axis=dim), axis, forward
        )
        high = lax.ppermute(lax.slice_in_dim(block, 0, width, axis=dim), axis, backward)
        block = jnp.concatenate([low, block, high], axis=dim)
    return block


def shards(potential, basis, hamiltonian, density, hmask, pmask):
    width_x, width_y, depth_z = potential.shape
    extended = extended_2(potential, (("row", 0), ("col", 1)), 1)
    padded = jnp.pad(extended, ((0, 0), (0, 0), (1, 1)))
    beside = padded[2:, 1:-1, 1:-1] + padded[:-2, 1:-1, 1:-1]
    beside = beside + padded[1:-1, 2:, 1:-1] + padded[1:-1, :-2, 1:-1]
    beside = beside + padded[1:-1, 1:-1, 2:] + padded[1:-1, 1:-1, :-2]
    effective = potential + KAPPA * (beside - 6.0 * potential)
    blocks_here = basis.shape[2] // BLK
    weighted = (basis * effective[:, :, None, :]).astype(jnp.bfloat16)
    partial_blocks = jnp.einsum(
        "xykaz,xykbz->kab",
        weighted.reshape(width_x, width_y, blocks_here, BLK, depth_z),
        basis.reshape(width_x, width_y, blocks_here, BLK, depth_z),
        preferred_element_type=jnp.float32,
    )
    summed = lax.psum(partial_blocks, "col")
    factor = float(BLK * width_x * width_y * depth_z * lax.axis_size("col")) ** (-0.5)
    potential_blocks = (summed * factor).astype(jnp.bfloat16)
    block_total = hmask.shape[0]
    blocks_wide = block_total // lax.axis_size("col")
    row_start = lax.axis_index("row") * blocks_here
    col_start = lax.axis_index("col") * blocks_wide
    hpattern = lax.dynamic_slice(hmask, (row_start, col_start), (blocks_here, blocks_wide))
    ppattern = lax.dynamic_slice(pmask, (row_start, col_start), (blocks_here, blocks_wide))
    masked_h = (
        hamiltonian.reshape(blocks_here, BLK, blocks_wide, BLK)
        * hpattern[:, None, :, None].astype(jnp.bfloat16)
    ).reshape(blocks_here * BLK, blocks_wide * BLK)
    masked_p = (
        density.reshape(2, blocks_here, BLK, blocks_wide, BLK)
        * ppattern[None, :, None, :, None].astype(jnp.bfloat16)
    ).reshape(2, blocks_here * BLK, blocks_wide * BLK)

    def diagonal_term(operand):
        local = jnp.einsum(
            "kab,skbc->skac",
            potential_blocks,
            operand.reshape(2, blocks_here, BLK, operand.shape[2]),
            preferred_element_type=jnp.float32,
        )
        return local.reshape(2, blocks_here * BLK, operand.shape[2])

    def apply(operand):
        column_whole = lax.all_gather(operand, "row", axis=1, tiled=True)
        remote = jnp.einsum(
            "rk,skc->src",
            lax.all_gather(masked_h, "col", axis=1, tiled=True),
            column_whole,
            preferred_element_type=jnp.float32,
        )
        return remote + diagonal_term(operand)

    first = apply(masked_p)
    first_rounded = first.astype(jnp.bfloat16)
    second = apply(first_rounded)
    base = masked_p.astype(jnp.float32)
    half_square = 0.5 * TIME_STEP * TIME_STEP
    real_part = base[0] + TIME_STEP * first[1] - half_square * second[0]
    imag_part = base[1] - TIME_STEP * first[0] - half_square * second[1]
    stacked = jnp.stack([real_part, imag_part]).reshape(2, blocks_here, BLK, blocks_wide, BLK)
    stacked = stacked * ppattern[None, :, None, :, None].astype(jnp.float32)
    return stacked.reshape(2, blocks_here * BLK, blocks_wide * BLK).astype(jnp.bfloat16)


def solution(mesh):
    in_specs = (
        P("row", "col", None),
        P("row", "col", None, None),
        P("row", "col"),
        P(None, "row", "col"),
        P(),
        P(),
    )
    out_specs = P(None, "row", "col")
    return jax.shard_map(shards, mesh=mesh, in_specs=in_specs, out_specs=out_specs, check_vma=False)
```

profile of v0, /device:TPU:0, one launch (start us, length us, event | category | flops | bytes accessed | tf_op | source)
XLA Modules:
  0.0 394.5 jit_solution(11533776390948993959)
XLA Ops:
  6.5 0.7 fusion.29
  7.3 4.8 %collective-permute-start.1 = (f32[1,4,512]{2,1,0:T(4,128)S(1)}, f32[1,4,512]{2,1,0:T(4,128)S(1)}, u32[]{:S(2)}, u32[]{:S(2)}) collective-permute-start(f32[1,4,512]{2,1,0:T(4,128)S(1)} %get-tuple-element.12), channel_id=1, source_target_pairs={{0,4},{4,8},{8,12},{12,16},{16,20},{20,24},{24,28},{1,5},{5,9},{9,... | collective-permute-start | bytes 24584 | tf_op jit(solution)/shard_map/ppermute | solution.py:18
  12.1 1.3 collective-permute-start
  13.4 0.0 collective-permute-done.1
  13.4 0.7 constant_dynamic-update-slice_fusion.1
  14.2 3.5 collective-permute-done
  17.7 1.3 collective-permute-start.2
  19.0 3.0 collective-permute-start.3
  22.0 0.8 dynamic-slice_convert_fusion.1
  22.8 0.0 collective-permute-done.2
  22.8 0.0 collective-permute-done.3
  22.8 0.1 select_maximum_fusion
  23.0 0.9 fusion.21
  23.8 0.0 copy-start
  23.9 2.7 multiply_convert_fusion
  26.6 0.1 copy-done
  26.7 1.6 convolution_bitcast_fusion.2
  28.3 0.0 all-reduce.3.cloned.1.call-update
  28.3 0.0 all-gather.6.cloned.1.call-start
  28.4 0.2 mul.100
  28.6 0.0 copy-start.2
  28.6 0.9 bitcast_multiply_fusion
  29.5 0.0 all-gather.6.cloned.1.call-update
  29.5 0.0 all-gather.4.cloned.1.call-start
  29.6 0.2 mul.96
  29.7 0.1 copy.42
  29.8 0.2 copy-done.2
  30.1 1.2 fusion.27
  31.3 0.0 all-gather.4.cloned.1.call-update
  31.3 0.0 all-gather.8.cloned.1.call-start
  31.4 0.1 broadcast_bitcast_fusion
  31.5 31.7 %all-reduce.3.cloned.1.call-done = f32[3,128,128]{2,1,0:T(8,128)} async-done(((f32[3,128,128]{2,1,0:T(8,128)}), f32[3,128,128]{2,1,0:T(8,128)}) %all-reduce.3.cloned.1.call-update) | async-done | bytes 196624 | tf_op jit(solution)/shard_map/psum | solution.py:42
  63.1 1.4 convolution_bitcast_fusion.1
  64.5 1.5 copy.18
  66.1 22.8 %all-gather.6.cloned.1.call-done = bf16[384,3072]{1,0:T(8,128)(2,1)} async-done(((bf16[384,768]{1,0:T(8,128)(2,1)}), bf16[384,3072]{1,0:T(8,128)(2,1)}) %all-gather.6.cloned.1.call-update) | async-done | bytes 2359312 | tf_op jit(solution)/shard_map/all_gather | solution.py:73
  88.9 140.5 %all-gather.4.cloned.1.call-done = bf16[2,3072,768]{2,1,0:T(8,128)(2,1)} async-done(((bf16[2,384,768]{2,1,0:T(8,128)(2,1)}), bf16[2,3072,768]{2,1,0:T(8,128)(2,1)}) %all-gather.4.cloned.1.call-update) | async-done | bytes 9437200 | tf_op jit(solution)/shard_map/all_gather | solution.py:70
  229.4 10.6 %fusion.30 = (bf16[2,384,768]{2,1,0:T(8,128)(2,1)}, f32[2,384,768]{2,1,0:T(8,128)}) fusion(f32[2,3,128,768]{3,2,1,0:T(8,128)} %copy.18, bf16[2,3072,768]{2,1,0:T(8,128)(2,1)} %all-gather.4.cloned.1.call-done, bf16[384,3072]{1,0:T(8,128)(2,1)} %all-gather.6.cloned.1.call-done), kind=kOutput, calls=%fused_computation.59 | convolution fusion | flops 3625058304 | bytes 17694720 | tf_op jit(solution)/shard_map/rk,skc->src/dot_general | solution.py:71
  240.0 0.0 all-gather.8.cloned.1.call-update
  240.0 0.0 copy-start.1
  240.1 0.2 mul.119
  240.2 1.3 copy.41
  241.5 0.5 convolution_bitcast_fusion
  242.0 1.5 copy.22
  243.5 132.9 %all-gather.8.cloned.1.call-done = bf16[2,3072,768]{2,1,0:T(8,128)(2,1)} async-done(((bf16[2,384,768]{2,1,0:T(8,128)(2,1)}), bf16[2,3072,768]{2,1,0:T(8,128)(2,1)}) %all-gather.8.cloned.1.call-update) | async-done | bytes 9437200 | tf_op jit(solution)/shard_map/all_gather | solution.py:70
  376.5 9.0 %bitcast_add_fusion = f32[2,384,768]{2,1,0:T(8,128)S(1)} fusion(f32[2,3,128,768]{3,2,1,0:T(8,128)} %copy.22, bf16[2,3072,768]{2,1,0:T(8,128)(2,1)} %all-gather.8.cloned.1.call-done, bf16[384,3072]{1,0:T(8,128)(2,1)} %all-gather.6.cloned.1.call-done), kind=kOutput, calls=%fused_computation.3 | convolution fusion | flops 3624468480 | bytes 16515072 | tf_op jit(solution)/shard_map/rk,skc->src/dot_general | solution.py:71
  385.5 0.5 fusion.11
  386.0 0.7 copy-done.3
  386.7 1.3 fusion
  (13 shorter events, 0.1 us)
Async XLA Ops:
  6.5 56.6 %all-reduce.3.cloned.1.call-start = ((), (), s32[]{:S(2)}) async-start(), calls=%async_computation.2 | async-start | bytes 393216 | tf_op jit(solution)/shard_map/psum | solution.py:42
  7.3 6.2 %collective-permute-start.1 = (f32[1,4,512]{2,1,0:T(4,128)S(1)}, f32[1,4,512]{2,1,0:T(4,128)S(1)}, u32[]{:S(2)}, u32[]{:S(2)}) collective-permute-start(f32[1,4,512]{2,1,0:T(4,128)S(1)} %get-tuple-element.12), channel_id=1, source_target_pairs={{0,4},{4,8},{8,12},{12,16},{16,20},{20,24},{24,28},{1,5},{5,9},{9,... | collective-permute-start | bytes 24584 | tf_op jit(solution)/shard_map/ppermute | solution.py:18
  12.1 5.5 %collective-permute-start = (f32[1,4,512]{2,1,0:T(4,128)S(1)}, f32[1,4,512]{2,1,0:T(4,128)S(1)}, u32[]{:S(2)}, u32[]{:S(2)}) collective-permute-start(f32[1,4,512]{2,1,0:T(4,128)S(1)} %get-tuple-element.11), channel_id=1, source_target_pairs={{4,0},{8,4},{12,8},{16,12},{20,16},{24,20},{28,24},{5,1},{9,5},{13... | collective-permute-start | bytes 24584 | tf_op jit(solution)/shard_map/ppermute | solution.py:21
  17.7 5.1 %collective-permute-start.2 = (f32[4,1,512]{2,1,0:T(1,128)S(1)}, f32[4,1,512]{2,1,0:T(1,128)S(1)}, u32[]{:S(2)}, u32[]{:S(2)}) collective-permute-start(f32[4,1,512]{2,1,0:T(1,128)S(1)} %get-tuple-element.10), channel_id=1, source_target_pairs={{1,0},{2,1},{3,2},{5,4},{6,5},{7,6},{9,8},{10,9},{11,10},{13,12},{... | collective-permute-start | bytes 24584 | tf_op jit(solution)/shard_map/ppermute | solution.py:21
  19.0 3.8 collective-permute-start.3
  23.8 2.8 copy-start
  26.7 1.9 copy-start.6
  28.3 60.5 %all-gather.6.cloned.1.call-start = ((), (), s32[]{:S(2)}) async-start(), calls=%async_computation.1 | async-start | bytes 2949120 | tf_op jit(solution)/shard_map/all_gather | solution.py:73
  28.6 1.5 copy-start.2
  29.5 199.9 %all-gather.4.cloned.1.call-start = ((), (), s32[]{:S(2)}) async-start(), calls=%async_computation | async-start | bytes 10616832 | tf_op jit(solution)/shard_map/all_gather | solution.py:70
  31.3 345.1 %all-gather.8.cloned.1.call-start = ((), (), s32[]{:S(2)}) async-start(), calls=%async_computation.3 | async-start | bytes 10616832 | tf_op jit(solution)/shard_map/all_gather | solution.py:70
  240.0 1.5 copy-start.1
  240.1 1.5 copy-start.5
  376.4 9.0 %copy-start.4 = (f32[2,384,768]{2,1,0:T(8,128)S(1)}, f32[2,384,768]{2,1,0:T(8,128)}, u32[]{:S(2)}) copy-start(f32[2,384,768]{2,1,0:T(8,128)} %get-tuple-element.16) | copy-start | bytes 7077892
  385.4 1.3 copy-start.3
Sparse Core Ops, SparseCore 0:
  28.5 34.6 all-reduce.2
  64.8 24.0 all-gather.5
  91.3 138.0 all-gather.3
  240.2 136.2 all-gather.7
where the time goes:
time: 395 us
  waiting for transfers between devices  332 us (84%)
  matrix products  23.1 us (6%)
  between operations  13.3 us (3%)
  starting transfers between devices  10.6 us (3%)
  other arithmetic  8.46 us (2%)
  local copies, waits for them, and re-layouts  7.56 us (2%)
    all_gather x2, waiting for transfers between devices, apply(): column_whole = lax.all_gather(operand, 'row', axis=1, tiled=True)  273 us
    psum x1, waiting for transfers between devices, shards(): summed = lax.psum(partial_blocks, 'col')  31.7 us
    all_gather x1, waiting for transfers between devices, apply(): lax.all_gather(masked_h, 'col', axis=1, tiled=True)  22.8 us
    dot_general x2, matrix products, apply(): jnp.einsum('rk,skc->src', lax.all_gather(masked_h, 'col', axis=1, tiled=T...  19.6 us
  transfers between devices with their start and end apart: 8, of which 5 were waited for; matrix products, arithmetic and copies ran while one was open for 3% of the time, Pallas kernels for 0%

commit v1 on v0

v1 whole, which is shorter than its diff:
```python
import functools

import jax
import jax.numpy as jnp
from jax import lax
from jax.experimental import pallas as pl
from jax.experimental.pallas import tpu as pltpu
from jax.sharding import PartitionSpec as P

BLK = 128
KAPPA = 0.4
TIME_STEP = 0.5
BF16 = jnp.bfloat16
F32 = jnp.float32
VMEM_BYTES = 48 * 1024 * 1024

SMEM_SPEC = pl.BlockSpec(memory_space=pltpu.SMEM)
VMEM_SPEC = pl.BlockSpec(memory_space=pltpu.VMEM)


def call(body, scalars, arrays, outs, scratch=(), flops=0):
    moved = sum(a.size * a.dtype.itemsize for a in arrays)
    moved += sum(o.size * o.dtype.itemsize for o in outs)
    return pl.pallas_call(
        body,
        out_shape=tuple(outs),
        in_specs=[SMEM_SPEC] * len(scalars) + [VMEM_SPEC] * len(arrays),
        out_specs=tuple(VMEM_SPEC for _ in outs),
        scratch_shapes=list(scratch),
        compiler_params=pltpu.CompilerParams(vmem_limit_bytes=VMEM_BYTES),
        cost_estimate=pl.CostEstimate(flops=flops, bytes_accessed=moved, transcendentals=0),
    )(*scalars, *arrays)


def shape(*dims, dtype=BF16):
    return jax.ShapeDtypeStruct(dims, dtype)


def pack_kernel(cap, kb, jb, info, hmask, h, packed):
    row, col = info[0], info[1]
    place = jnp.int32(0)
    for k in range(kb):
        for j in range(jb):
            keep = (hmask[row * kb + k, col * jb + j] != 0) & (place < cap)

            @pl.when(keep)
            def _(k=k, j=j, place=place):
                packed[place] = h[k * BLK : (k + 1) * BLK, j * BLK : (j + 1) * BLK]

            place = place + keep.astype(jnp.int32)


def turn_kernel(zs, kb, jb, info, pmask, p, *rest):
    pieces, turned = rest[:-1], rest[-1]
    row, col = info[0], info[1]
    z = row // 2
    wide = BLK // zs
    for k in range(kb):
        for j in range(jb):
            keep = pmask[row * kb + k, col * jb + j] != 0
            for part in range(2):
                here = p[part, k * BLK : (k + 1) * BLK, j * BLK : (j + 1) * BLK]
                here = jnp.where(keep, here, jnp.zeros_like(here)).T
                top = (part * jb + j) * BLK
                turned[top : top + BLK, k * BLK : (k + 1) * BLK] = here
    for s in range(zs):
        start = pl.multiple_of((z ^ s) * wide, wide)
        for i in range(2 * jb):
            pieces[s][i * wide : (i + 1) * wide, :] = turned[pl.ds(i * BLK + start, wide), :]


def return_kernel(zs, kb, jb, info, pmask, *rest):
    pieces, out, turned = rest[:zs], rest[zs], rest[zs + 1]
    row, col = info[0], info[1]
    z = row // 2
    wide = BLK // zs
    for s in range(zs):
        start = pl.multiple_of((z ^ s) * wide, wide)
        for i in range(2 * jb):
            turned[pl.ds(i * BLK + start, wide), :] = pieces[s][i * wide : (i + 1) * wide, :]
    for k in range(kb):
        for j in range(jb):
            keep = pmask[row * kb + k, col * jb + j] != 0
            for part in range(2):
                top = (part * jb + j) * BLK
                here = turned[top : top + BLK, k * BLK : (k + 1) * BLK]
                here = jnp.where(keep, here, jnp.zeros_like(here)).T
                out[part, k * BLK : (k + 1) * BLK, j * BLK : (j + 1) * BLK] = here


def join_kernel(zs, side, info, *rest):
    out = rest[-1]
    z, x = info[0] // 2, info[0] % 2
    for s in range(zs):
        for other in range(2):
            start = pl.multiple_of((2 * (z ^ s) + (x ^ other)) * side, side)
            out[:, pl.ds(start, side)] = rest[2 * s + other][...]


def first_kernel(s, kb, jb, info, hmask, joined, diagonal, *rest):
    packed, (dense, first) = rest[:-2], rest[-2:]
    row = info[0] ^ (2 * s)
    for m in range(len(packed)):
        col = info[1] ^ m
        place = jnp.int32(0)
        for k in range(kb):
            for j in range(jb):
                block_col = col * jb + j
                keep = hmask[row * kb + k, block_col] != 0
                start = pl.multiple_of(block_col * BLK, BLK)

                @pl.when(keep)
                def _(k=k, m=m, place=place, start=start):
                    dense[k * BLK : (k + 1) * BLK, pl.ds(start, BLK)] = packed[m][place]

                @pl.when(jnp.logical_not(keep))
                def _(k=k, start=start):
                    dense[k * BLK : (k + 1) * BLK, pl.ds(start, BLK)] = jnp.zeros((BLK, BLK), BF16)

                place = place + keep.astype(jnp.int32)
    for k in range(kb):
        rows = pl.ds(k * BLK, BLK)
        columns = pl.ds(pl.multiple_of((row * kb + k) * BLK, BLK), BLK)
        both = dense[rows, columns].astype(F32) + diagonal[k * BLK : (k + 1) * BLK, :].astype(F32)
        dense[rows, columns] = both.astype(BF16)
    first[...] = lax.dot_general(
        joined[...], dense[...], (((1,), (1,)), ((), ())), preferred_element_type=F32
    ).astype(BF16)


def second_kernel(count, joined, *rest):
    half_square = 0.5 * TIME_STEP * TIME_STEP
    dense, density, first, outs = (rest[i * count : (i + 1) * count] for i in range(4))
    for i in range(count):
        second = lax.dot_general(
            joined[...], dense[i][...], (((1,), (1,)), ((), ())), preferred_element_type=F32
        )
        half = second.shape[0] // 2
        real, imag = slice(0, half), slice(half, 2 * half)
        outs[i][real, :] = (
            density[i][real, :].astype(F32)
            + TIME_STEP * first[i][imag, :].astype(F32)
            - half_square * second[real, :]
        ).astype(BF16)
        outs[i][imag, :] = (
            density[i][imag, :].astype(F32)
            - TIME_STEP * first[i][real, :].astype(F32)
            - half_square * second[imag, :]
        ).astype(BF16)


def swap_row(value, bits):
    count = lax.axis_size("row")
    return lax.ppermute(value, "row", [(i, i ^ bits) for i in range(count)])


def swap_col(value, bits):
    count = lax.axis_size("col")
    return lax.ppermute(value, "col", [(i, i ^ bits) for i in range(count)])


def from_line(own, z):
    zs = lax.axis_size("row") // 2
    if zs != 4:
        return [own] + [swap_row(own, 2 * s) for s in range(1, zs)]

    def along(value, pairs):
        return lax.ppermute(value, "row", [(2 * a + x, 2 * b + x) for a, b in pairs for x in range(2)])

    middle, outward = [(1, 2), (2, 1)], [(1, 0), (2, 3)]
    beside = swap_row(own, 2)
    across = along(own, middle)
    across_beside = along(beside, middle)
    out_near = along(across, outward)
    out_far = along(across_beside, outward)
    inner = (z == 1) | (z == 2)
    return [
        own,
        beside,
        jnp.where(inner, across_beside, out_near),
        jnp.where(inner, across, out_far),
    ]


def effective_potential(potential):
    def beyond(axis, dim):
        count = lax.axis_size(axis)
        forward = [(i, i + 1) for i in range(count - 1)]
        backward = [(target, source) for source, target in forward]
        last = potential.shape[dim] - 1
        low = lax.ppermute(lax.slice_in_dim(potential, last, None, axis=dim), axis, forward)
        high = lax.ppermute(lax.slice_in_dim(potential, 0, 1, axis=dim), axis, backward)
        return jnp.concatenate([low, potential, high], axis=dim)

    in_x, in_y = beyond("row", 0), beyond("col", 1)
    in_z = jnp.pad(potential, ((0, 0), (0, 0), (1, 1)))
    beside = in_x[2:] + in_x[:-2]
    beside = beside + in_y[:, 2:] + in_y[:, :-2]
    beside = beside + in_z[:, :, 2:] + in_z[:, :, :-2]
    return potential + KAPPA * (beside - 6.0 * potential)


def potential_blocks(potential, basis):
    width_x, width_y, depth_z = potential.shape
    kb = basis.shape[2] // BLK
    effective = effective_potential(potential)
    weighted = (basis * effective[:, :, None, :]).astype(BF16)
    partial = jnp.einsum(
        "xykaz,xykbz->kab",
        weighted.reshape(width_x, width_y, kb, BLK, depth_z),
        basis.reshape(width_x, width_y, kb, BLK, depth_z),
        preferred_element_type=F32,
    ).reshape(kb * BLK, BLK)
    half = kb * BLK // 2
    low, high = partial[:half], partial[half:]
    even = lax.axis_index("col") % 2 == 0
    mine = jnp.where(even, low, high) + swap_col(jnp.where(even, high, low), 1)
    total = mine
    for t in range(1, lax.axis_size("col") // 2):
        total = total + swap_col(mine, 2 * t)
    factor = float(BLK * width_x * width_y * depth_z * lax.axis_size("col")) ** (-0.5)
    return (total * factor).astype(BF16)


def shards(potential, basis, hamiltonian, density, hmask, pmask):
    row, col = lax.axis_index("row"), lax.axis_index("col")
    info = jnp.stack([row, col]).astype(jnp.int32)
    z, core = row // 2, col % 2
    zs = lax.axis_size("row") // 2
    cols = lax.axis_size("col")
    side, across = hamiltonian.shape
    order = side * lax.axis_size("row")
    kb, jb = side // BLK, across // BLK
    cap = kb * jb
    wide = 2 * across // zs

    (packed,) = call(
        functools.partial(pack_kernel, cap, kb, jb), [info, hmask], [hamiltonian], [shape(cap, BLK, BLK)]
    )
    lines = from_line(packed, z)

    pieces = call(
        functools.partial(turn_kernel, zs, kb, jb),
        [info, pmask],
        [density],
        [shape(wide, side)] * zs,
        scratch=[pltpu.VMEM((2 * across, side), BF16)],
    )

    def join(same, other):
        both = [piece for pair in zip(same, other) for piece in pair]
        return call(functools.partial(join_kernel, zs, side), [info], both, [shape(wide, order)])[0]

    mine = [pieces[s] if s == 0 else swap_row(pieces[s], 2 * s) for s in range(zs)]
    theirs = [swap_row(piece, 1) for piece in mine]
    joined = join(mine, theirs)

    own_half = potential_blocks(potential, basis)
    halves = [own_half] + [swap_row(own_half, 2 * s) for s in range(1, zs)]
    stacked = jnp.stack(halves)
    beside = swap_col(stacked, 1)
    diagonal = jnp.concatenate(
        [jnp.where(core == 0, stacked, beside), jnp.where(core == 0, beside, stacked)], axis=1
    )

    dense, first = [], []
    for s in range(zs):
        blocks = []
        for t in range(cols // 2):
            here = lines[s] if t == 0 else swap_col(lines[s], 2 * t)
            blocks += [here, swap_col(here, 1)]
        d, f = call(
            functools.partial(first_kernel, s, kb, jb),
            [info, hmask],
            [joined, diagonal[s], *blocks],
            [shape(side, order), shape(wide, side)],
            flops=2 * side * order * wide,
        )
        dense.append(d)
        first.append(f)
    first_joined = join(first, [swap_row(f, 1) for f in first])

    result = [None] * zs
    for slots in [[s] for s in range(zs - 1, -1, -1)]:
        outs = call(
            functools.partial(second_kernel, len(slots)),
            [],
            [first_joined]
            + [dense[s] for s in slots]
            + [mine[s] for s in slots]
            + [first[s] for s in slots],
            [shape(wide, side)] * len(slots),
            flops=2 * side * order * wide * len(slots),
        )
        for s, out in zip(slots, outs):
            result[s] = out if s == 0 else swap_row(out, 2 * s)

    return call(
        functools.partial(return_kernel, zs, kb, jb),
        [info, pmask],
        result,
        [shape(2, side, across)],
        scratch=[pltpu.VMEM((2 * across, side), BF16)],
    )[0]


def extended_2(block, sides, width):
    for axis, dim in sides:
        count = lax.axis_size(axis)
        forward = [(i, i + 1) for i in range(count - 1)]
        backward = [(target, source) for source, target in forward]
        low = lax.ppermute(
            lax.slice_in_dim(block, block.shape[dim] - width, None, axis=dim), axis, forward
        )
        high = lax.ppermute(lax.slice_in_dim(block, 0, width, axis=dim), axis, backward)
        block = jnp.concatenate([low, block, high], axis=dim)
    return block


def gathered(potential, basis, hamiltonian, density, hmask, pmask):
    width_x, width_y, depth_z = potential.shape
    extended = extended_2(potential, (("row", 0), ("col", 1)), 1)
    padded = jnp.pad(extended, ((0, 0), (0, 0), (1, 1)))
    beside = padded[2:, 1:-1, 1:-1] + padded[:-2, 1:-1, 1:-1]
    beside = beside + padded[1:-1, 2:, 1:-1] + padded[1:-1, :-2, 1:-1]
    beside = beside + padded[1:-1, 1:-1, 2:] + padded[1:-1, 1:-1, :-2]
    effective = potential + KAPPA * (beside - 6.0 * potential)
    blocks_here = basis.shape[2] // BLK
    weighted = (basis * effective[:, :, None, :]).astype(BF16)
    partial_blocks = jnp.einsum(
        "xykaz,xykbz->kab",
        weighted.reshape(width_x, width_y, blocks_here, BLK, depth_z),
        basis.reshape(width_x, width_y, blocks_here, BLK, depth_z),
        preferred_element_type=F32,
    )
    summed = lax.psum(partial_blocks, "col")
    factor = float(BLK * width_x * width_y * depth_z * lax.axis_size("col")) ** (-0.5)
    potential_blocks = (summed * factor).astype(BF16)
    block_total = hmask.shape[0]
    blocks_wide = block_total // lax.axis_size("col")
    row_start = lax.axis_index("row") * blocks_here
    col_start = lax.axis_index("col") * blocks_wide
    hpattern = lax.dynamic_slice(hmask, (row_start, col_start), (blocks_here, blocks_wide))
    ppattern = lax.dynamic_slice(pmask, (row_start, col_start), (blocks_here, blocks_wide))
    masked_h = (
        hamiltonian.reshape(blocks_here, BLK, blocks_wide, BLK)
        * hpattern[:, None, :, None].astype(BF16)
    ).reshape(blocks_here * BLK, blocks_wide * BLK)
    masked_p = (
        density.reshape(2, blocks_here, BLK, blocks_wide, BLK)
        * ppattern[None, :, None, :, None].astype(BF16)
    ).reshape(2, blocks_here * BLK, blocks_wide * BLK)

    def diagonal_term(operand):
        local = jnp.einsum(
            "kab,skbc->skac",
            potential_blocks,
            operand.reshape(2, blocks_here, BLK, operand.shape[2]),
            preferred_element_type=F32,
        )
        return local.reshape(2, blocks_here * BLK, operand.shape[2])

    def apply(operand):
        column_whole = lax.all_gather(operand, "row", axis=1, tiled=True)
        remote = jnp.einsum(
            "rk,skc->src",
            lax.all_gather(masked_h, "col", axis=1, tiled=True),
            column_whole,
            preferred_element_type=F32,
        )
        return remote + diagonal_term(operand)

    first = apply(masked_p)
    first_rounded = first.astype(BF16)
    second = apply(first_rounded)
    base = masked_p.astype(F32)
    half_square = 0.5 * TIME_STEP * TIME_STEP
    real_part = base[0] + TIME_STEP * first[1] - half_square * second[0]
    imag_part = base[1] - TIME_STEP * first[0] - half_square * second[1]
    stacked = jnp.stack([real_part, imag_part]).reshape(2, blocks_here, BLK, blocks_wide, BLK)
    stacked = stacked * ppattern[None, :, None, :, None].astype(F32)
    return stacked.reshape(2, blocks_here * BLK, blocks_wide * BLK).astype(BF16)


def solution(mesh):
    in_specs = (
        P("row", "col", None),
        P("row", "col", None, None),
        P("row", "col"),
        P(None, "row", "col"),
        P(),
        P(),
    )
    out_specs = P(None, "row", "col")
    body = shards if (mesh.shape["row"], mesh.shape["col"]) == (8, 4) else gathered
    return jax.shard_map(body, mesh=mesh, in_specs=in_specs, out_specs=out_specs, check_vma=False)
```

time: 395 us -> 212 us (0.54)
  waiting for transfers between devices: 332 us -> 87 us
  starting transfers between devices: 10.6 us -> 71.8 us
  Pallas kernels: 0 us -> 31.6 us
  matrix products: 23.1 us -> 0.96 us
  between operations: 13.3 us -> 0.47 us
    all_gather x3 -> x0, waiting for transfers between devices: 296 us -> none  [the longest x2 273 us: apply(): column_whole = lax.all_gather(operand, 'row', axis=1, tiled=True)]
    ppermute x4 -> x41, waiting for transfers between devices: 3.52 us -> 87 us  [the longest x18 44.1 us: swap_row(): return lax.ppermute(value, 'row', [(i, i ^ bits) for i in range(count)])]
    ppermute x4 -> x41, starting transfers between devices: 10.4 us -> 71.8 us  [the longest x18 47.9 us: swap_row(): return lax.ppermute(value, 'row', [(i, i ^ bits) for i in range(count)])]
    psum x1 -> x0, waiting for transfers between devices: 31.7 us -> none  [shards(): summed = lax.psum(partial_blocks, 'col')]
    pallas_call x0 -> x13, Pallas kernels: none -> 31.6 us  [call(): pl.pallas_call(body, out_shape=tuple(outs), in_specs=[SMEM_SPEC] * len(sc...]
    dot_general x5 -> x1, matrix products: 23.1 us -> 0.96 us  [potential_blocks(): jnp.einsum('xykaz,xykbz->kab', weighted.reshape(width_x, width_y, kb, BLK...]
    unnamed x20 -> x50, local copies, waits for them, and re-layouts: 3.25 us -> 9.25 us
  transfers between devices with their start and end apart: 8 -> 41, of which waited for: 5 -> 17; matrix products, arithmetic and copies ran while one was open for 3% -> 4% of each run, Pallas kernels for 0% -> 13%
where the time goes in v1:
time: 212 us; the launch traced here: 209 us
  waiting for transfers between devices  87 us (41%)
  starting transfers between devices  71.8 us (34%)
  Pallas kernels  31.6 us (15%)
  local copies, waits for them, and re-layouts  10.8 us (5%)
  other arithmetic  6.23 us (3%)
    ppermute x18, starting transfers between devices, swap_row(): return lax.ppermute(value, 'row', [(i, i ^ bits) for i in range(count)])  47.9 us
    ppermute x18, waiting for transfers between devices, swap_row(): return lax.ppermute(value, 'row', [(i, i ^ bits) for i in range(count)])  44.1 us
    pallas_call x13, Pallas kernels, call(): pl.pallas_call(body, out_shape=tuple(outs), in_specs=[SMEM_SPEC] * len(sc...  31.6 us
    ppermute x15, waiting for transfers between devices, swap_col(): return lax.ppermute(value, 'col', [(i, i ^ bits) for i in range(count)])  27.2 us
    ppermute x4, waiting for transfers between devices, along(): lax.ppermute(value, 'row', [(2 * a + x, 2 * b + x) for a, b in pairs for...  15.7 us
    unnamed x50, local copies, waits for them, and re-layouts  9.25 us
    ppermute x2, starting transfers between devices, beyond(): lax.ppermute(lax.slice_in_dim(potential, last, None, axis=dim), axis, for...  8.5 us
    ppermute x15, starting transfers between devices, swap_col(): return lax.ppermute(value, 'col', [(i, i ^ bits) for i in range(count)])  7.24 us
  transfers between devices with their start and end apart: 41, of which 17 were waited for; matrix products, arithmetic and copies ran while one was open for 4% of the time, Pallas kernels for 13%

profile of v1, /device:TPU:0, one launch (start us, length us, event | category | flops | bytes accessed | tf_op | source)
XLA Modules:
  0.0 208.9 jit_solution(14269065338936324368)
XLA Ops:
  0.8 1.3 collective-permute-start.9
  2.1 3.0 %collective-permute-start.10 = (f32[2,1,512]{2,1,0:T(1,128)S(1)}, f32[2,1,512]{2,1,0:T(1,128)S(1)}, u32[]{:S(2)}, u32[]{:S(2)}) collective-permute-start(f32[2,1,512]{2,1,0:T(1,128)S(1)} %get-tuple-element.38), channel_id=1, source_target_pairs={{0,1},{1,2},{2,3},{4,5},{5,6},{6,7},{8,9},{9,10},{10,11},{12,13},{... | collective-permute-start | bytes 12296 | tf_op jit(solution)/shard_map/ppermute | solution.py:191
  5.9 1.3 collective-permute-start.7
  7.2 5.5 %collective-permute-start.8 = (f32[1,4,512]{2,1,0:T(4,128)S(1)}, f32[1,4,512]{2,1,0:T(4,128)S(1)}, u32[]{:S(2)}, u32[]{:S(2)}) collective-permute-start(f32[1,4,512]{2,1,0:T(4,128)S(1)} %get-tuple-element.36), channel_id=1, source_target_pairs={{0,4},{4,8},{8,12},{12,16},{16,20},{20,24},{24,28},{1,5},{5,9},{9,... | collective-permute-start | bytes 24584 | tf_op jit(solution)/shard_map/ppermute | solution.py:191
  15.4 2.2 %collective-permute-start.21 = (bf16[18,128,128]{2,1,0:T(8,128)(2,1)S(1)}, bf16[18,128,128]{2,1,0:T(8,128)(2,1)}, u32[]{:S(2)}, u32[]{:S(2)}) collective-permute-start(bf16[18,128,128]{2,1,0:T(8,128)(2,1)S(1)} %shard_map.66.rest_0_), channel_id=1, source_target_pairs={{0,8},{4,12},{8,0},{12,4},{16,24},{20,28},{24,16},{28,20},{1,9},{5... | collective-permute-start | bytes 1769480 | tf_op jit(solution)/shard_map/ppermute | solution.py:154
  18.7 2.7 %multiply_convert_fusion = bf16[2,4,384,512]{3,2,1,0:T(8,128)(2,1)S(1)} fusion(bf16[2,4,384,512]{3,2,1,0:T(8,128)(2,1)} %param.7, f32[2,4,512]{2,1,0:T(4,128)S(1)} %fusion.11), kind=kLoop, calls=%fused_computation | loop fusion | flops 4718592 | bytes 6307840 | tf_op jit(solution)/shard_map/convert_element_type | solution.py:207
  22.9 1.5 collective-permute-start.27
  24.4 1.3 collective-permute-start.12
  25.7 1.2 shard_map.64
  27.0 3.6 %collective-permute-start.1 = (bf16[384,384]{1,0:T(8,128)(2,1)S(1)}, bf16[384,384]{1,0:T(8,128)(2,1)S(1)}, u32[]{:S(2)}, u32[]{:S(2)}) collective-permute-start(bf16[384,384]{1,0:T(8,128)(2,1)S(1)} %get-tuple-element.18), channel_id=1, source_target_pairs={{0,8},{4,12},{8,0},{12,4},{16,24},{20,28},{24,16},{28,20},{1,9},{5... | collective-permute-start | bytes 884744 | tf_op jit(solution)/shard_map/ppermute | solution.py:154
  31.9 1.5 collective-permute-start.26
  33.4 4.1 %collective-permute-start.15 = (bf16[192,128]{1,0:T(8,128)(2,1)S(1)}, bf16[192,128]{1,0:T(8,128)(2,1)S(1)}, u32[]{:S(2)}, u32[]{:S(2)}) collective-permute-start(bf16[192,128]{1,0:T(8,128)(2,1)S(1)} %multiply_convert_fusion.1), channel_id=1, source_target_pairs={{0,24},{4,28},{8,16},{12,20},{16,8},{20,12},{24,0},{28,4},{1,25},{... | collective-permute-start | bytes 147464 | tf_op jit(solution)/shard_map/ppermute | solution.py:154
  37.4 10.2 %collective-permute-done.15 = bf16[192,128]{1,0:T(8,128)(2,1)S(1)} collective-permute-done((bf16[192,128]{1,0:T(8,128)(2,1)S(1)}, bf16[192,128]{1,0:T(8,128)(2,1)S(1)}, u32[]{:S(2)}, u32[]{:S(2)}) %collective-permute-start.15) | collective-permute-done | bytes 49184 | tf_op jit(solution)/shard_map/ppermute | solution.py:154
  47.7 22.5 %collective-permute-start.14 = (bf16[192,128]{1,0:T(8,128)(2,1)S(1)}, bf16[192,128]{1,0:T(8,128)(2,1)S(1)}, u32[]{:S(2)}, u32[]{:S(2)}) collective-permute-start(bf16[192,128]{1,0:T(8,128)(2,1)S(1)} %multiply_convert_fusion.1), channel_id=1, source_target_pairs={{0,16},{4,20},{8,24},{12,28},{16,0},{20,4},{24,8},{28,12},{1,17},{... | collective-permute-start | bytes 147464 | tf_op jit(solution)/shard_map/ppermute | solution.py:154
  70.2 2.5 %collective-permute-done.14 = bf16[192,128]{1,0:T(8,128)(2,1)S(1)} collective-permute-done((bf16[192,128]{1,0:T(8,128)(2,1)S(1)}, bf16[192,128]{1,0:T(8,128)(2,1)S(1)}, u32[]{:S(2)}, u32[]{:S(2)}) %collective-permute-start.14) | collective-permute-done | bytes 49184 | tf_op jit(solution)/shard_map/ppermute | solution.py:154
  72.7 1.3 collective-permute-start.13
  74.0 2.8 %collective-permute-done.13 = bf16[192,128]{1,0:T(8,128)(2,1)S(1)} collective-permute-done((bf16[192,128]{1,0:T(8,128)(2,1)S(1)}, bf16[192,128]{1,0:T(8,128)(2,1)S(1)}, u32[]{:S(2)}, u32[]{:S(2)}) %collective-permute-start.13) | collective-permute-done | bytes 49184 | tf_op jit(solution)/shard_map/ppermute | solution.py:154
  76.8 1.9 collective-permute-start.5
  78.7 1.5 collective-permute-start.18
  80.2 1.3 collective-permute-start.28
  82.5 3.0 %collective-permute-done.5.rest_6_.rest_1_ = bf16[384,384]{1,0:T(8,128)(2,1)S(1)} collective-permute-done((bf16[384,384]{1,0:T(8,128)(2,1)S(1)}, bf16[384,384]{1,0:T(8,128)(2,1)S(1)}, u32[]{:S(2)}, u32[]{:S(2)}) %collective-permute-start.5) | collective-permute-done | bytes 294944 | tf_op jit(solution)/shard_map/ppermute | solution.py:154
  85.4 1.3 collective-permute-start.33
  86.8 1.5 collective-permute-done.rest_1_
  88.3 1.4 collective-permute-done.16
  92.0 6.7 %collective-permute-done.28 = bf16[18,128,128]{2,1,0:T(8,128)(2,1)} collective-permute-done((bf16[18,128,128]{2,1,0:T(8,128)(2,1)}, bf16[18,128,128]{2,1,0:T(8,128)(2,1)}, u32[]{:S(2)}, u32[]{:S(2)}) %collective-permute-start.28) | collective-permute-done | bytes 589856 | tf_op jit(solution)/shard_map/ppermute | solution.py:168
  101.6 9.0 %collective-permute-done.33 = bf16[18,128,128]{2,1,0:T(8,128)(2,1)} collective-permute-done((bf16[18,128,128]{2,1,0:T(8,128)(2,1)}, bf16[18,128,128]{2,1,0:T(8,128)(2,1)}, u32[]{:S(2)}, u32[]{:S(2)}) %collective-permute-start.33) | collective-permute-done | bytes 589856 | tf_op jit(solution)/shard_map/ppermute | solution.py:168
  110.6 1.4 collective-permute-start.30
  113.9 3.3 %collective-permute-done.23.rest_2_ = bf16[18,128,128]{2,1,0:T(8,128)(2,1)S(1)} collective-permute-done((bf16[18,128,128]{2,1,0:T(8,128)(2,1)}, bf16[18,128,128]{2,1,0:T(8,128)(2,1)S(1)}, u32[]{:S(2)}, u32[]{:S(2)}) %collective-permute-start.23) | collective-permute-done | bytes 589856 | tf_op jit(solution)/shard_map/ppermute | solution.py:159
  117.8 12.1 %collective-permute-done.30.rest_2_ = bf16[18,128,128]{2,1,0:T(8,128)(2,1)S(1)} collective-permute-done((bf16[18,128,128]{2,1,0:T(8,128)(2,1)S(1)}, bf16[18,128,128]{2,1,0:T(8,128)(2,1)S(1)}, u32[]{:S(2)}, u32[]{:S(2)}) %collective-permute-start.30) | collective-permute-done | bytes 589856 | tf_op jit(solution)/shard_map/ppermute | solution.py:159
  130.4 9.8 %collective-permute-done.35.rest_2_ = bf16[18,128,128]{2,1,0:T(8,128)(2,1)S(1)} collective-permute-done((bf16[18,128,128]{2,1,0:T(8,128)(2,1)S(1)}, bf16[18,128,128]{2,1,0:T(8,128)(2,1)S(1)}, u32[]{:S(2)}, u32[]{:S(2)}) %collective-permute-start.35) | collective-permute-done | bytes 589856 | tf_op jit(solution)/shard_map/ppermute | solution.py:159
  141.6 1.4 copy-done
  143.0 4.6 %shard_map.67 = (bf16[384,3072]{1,0:T(8,128)(2,1)S(1)}, bf16[384,384]{1,0:T(8,128)(2,1)S(1)}) custom-call(s32[2]{0:T(128)S(1)} %pad_add_fusion.info, s32[24,24]{1,0:T(8,128)S(1)} %copy-done.16, bf16[384,3072]{1,0:T(8,128)(2,1)} %copy-done, bf16[384,128]{1,0:T(8,128)(2,1)S(1)} %get-tuple-element.30.diagonal, bf16[18,128,128]{2,1,0:T(8,128)(2,1)S(1)} %shard_map.66.rest_0_, ...), custom_call_target="tpu_custom_call" | custom-call | flops 905969664 | bytes 7471104 | tf_op jit(solution)/shard_map/pallas_call | solution.py:24
  150.3 4.7 %shard_map.68 = (bf16[384,3072]{1,0:T(8,128)(2,1)S(1)}, bf16[384,384]{1,0:T(8,128)(2,1)S(1)}) custom-call(s32[2]{0:T(128)S(1)} %pad_add_fusion.info, s32[24,24]{1,0:T(8,128)S(1)} %copy-done.16, bf16[384,3072]{1,0:T(8,128)(2,1)} %copy-done, bf16[384,128]{1,0:T(8,128)(2,1)S(1)} %get-tuple-element.31.diagonal, ...), custom_call_target="tpu_custom_call" | custom-call | flops 905969664 | bytes 7471104 | tf_op jit(solution)/shard_map/pallas_call | solution.py:24
  155.0 1.3 collective-permute-start.25
  156.3 5.0 %shard_map.69 = (bf16[384,3072]{1,0:T(8,128)(2,1)S(1)}, bf16[384,384]{1,0:T(8,128)(2,1)S(1)}) custom-call(s32[2]{0:T(128)S(1)} %pad_add_fusion.info, s32[24,24]{1,0:T(8,128)S(1)} %copy-done.16, bf16[384,3072]{1,0:T(8,128)(2,1)} %copy-done, bf16[384,128]{1,0:T(8,128)(2,1)S(1)} %get-tuple-element.32.diagonal, ...), custom_call_target="tpu_custom_call" | custom-call | flops 905969664 | bytes 7471104 | tf_op jit(solution)/shard_map/pallas_call | solution.py:24
  162.2 4.8 %shard_map.70 = (bf16[384,3072]{1,0:T(8,128)(2,1)S(1)}, bf16[384,384]{1,0:T(8,128)(2,1)S(1)}) custom-call(s32[2]{0:T(128)S(1)} %pad_add_fusion.info, s32[24,24]{1,0:T(8,128)S(1)} %copy-done.16, bf16[384,3072]{1,0:T(8,128)(2,1)} %copy-done, bf16[384,128]{1,0:T(8,128)(2,1)S(1)} %get-tuple-element.29.diagonal, ...), custom_call_target="tpu_custom_call" | custom-call | flops 905969664 | bytes 7471104 | tf_op jit(solution)/shard_map/pallas_call | solution.py:24
  167.0 1.4 copy-done.1
  168.4 1.2 collective-permute-start.37
  170.5 6.5 %collective-permute-done.37.rest_7_ = bf16[384,384]{1,0:T(8,128)(2,1)S(1)} collective-permute-done((bf16[384,384]{1,0:T(8,128)(2,1)S(1)}, bf16[384,384]{1,0:T(8,128)(2,1)S(1)}, u32[]{:S(2)}, u32[]{:S(2)}) %collective-permute-start.37) | collective-permute-done | bytes 294944 | tf_op jit(solution)/shard_map/ppermute | solution.py:154
  180.2 1.4 shard_map.73
  181.7 1.4 shard_map.74
  183.1 3.0 %collective-permute-start.39 = (bf16[384,384]{1,0:T(8,128)(2,1)S(1)}, bf16[384,384]{1,0:T(8,128)(2,1)S(1)}, u32[]{:S(2)}, u32[]{:S(2)}) collective-permute-start(bf16[384,384]{1,0:T(8,128)(2,1)S(1)} %shard_map.74), channel_id=1, source_target_pairs={{0,16},{4,20},{8,24},{12,28},{16,0},{20,4},{24,8},{28,12},{1,17},{... | collective-permute-start | bytes 884744 | tf_op jit(solution)/shard_map/ppermute | solution.py:154
  186.1 1.4 shard_map.75
  187.5 1.5 collective-permute-start.40
  189.0 1.4 shard_map.72.rest_0_
  190.4 3.3 %collective-permute-done.38.rest_1_ = bf16[384,384]{1,0:T(8,128)(2,1)S(1)} collective-permute-done((bf16[384,384]{1,0:T(8,128)(2,1)S(1)}, bf16[384,384]{1,0:T(8,128)(2,1)S(1)}, u32[]{:S(2)}, u32[]{:S(2)}) %collective-permute-start.38) | collective-permute-done | bytes 294944 | tf_op jit(solution)/shard_map/ppermute | solution.py:154
  193.7 12.9 %collective-permute-done.39.rest_2_ = bf16[384,384]{1,0:T(8,128)(2,1)S(1)} collective-permute-done((bf16[384,384]{1,0:T(8,128)(2,1)S(1)}, bf16[384,384]{1,0:T(8,128)(2,1)S(1)}, u32[]{:S(2)}, u32[]{:S(2)}) %collective-permute-start.39) | collective-permute-done | bytes 294944 | tf_op jit(solution)/shard_map/ppermute | solution.py:154
  206.6 2.2 %shard_map.76 = bf16[2,384,768]{2,1,0:T(8,128)(2,1)} custom-call(s32[2]{0:T(128)S(1)} %pad_add_fusion.info, s32[24,24]{1,0:T(8,128)S(1)} %copy-done.19, bf16[384,384]{1,0:T(8,128)(2,1)S(1)} %shard_map.72.rest_0_, bf16[384,384]{1,0:T(8,128)(2,1)S(1)} %collective-permute-done.38.rest_1_, bf16[384,384]{1,0:T(8,128)(2,1)S(1)} %collective-permute-done.39.rest_2_, ...), custom_call_target="tpu_custom_call" | custom-call | bytes 2359296 | tf_op jit(solution)/shard_map/pallas_call | solution.py:24
  (111 shorter events, 26.0 us)
Async XLA Ops:
  0.8 16.8 %collective-permute-start.9 = (f32[2,1,512]{2,1,0:T(1,128)S(1)}, f32[2,1,512]{2,1,0:T(1,128)S(1)}, u32[]{:S(2)}, u32[]{:S(2)}) collective-permute-start(f32[2,1,512]{2,1,0:T(1,128)S(1)} %get-tuple-element.37), channel_id=1, source_target_pairs={{1,0},{2,1},{3,2},{5,4},{6,5},{7,6},{9,8},{10,9},{11,10},{13,12},{... | collective-permute-start | bytes 12296 | tf_op jit(solution)/shard_map/ppermute | solution.py:192
  2.1 15.5 %collective-permute-start.10 = (f32[2,1,512]{2,1,0:T(1,128)S(1)}, f32[2,1,512]{2,1,0:T(1,128)S(1)}, u32[]{:S(2)}, u32[]{:S(2)}) collective-permute-start(f32[2,1,512]{2,1,0:T(1,128)S(1)} %get-tuple-element.38), channel_id=1, source_target_pairs={{0,1},{1,2},{2,3},{4,5},{5,6},{6,7},{8,9},{9,10},{10,11},{12,13},{... | collective-permute-start | bytes 12296 | tf_op jit(solution)/shard_map/ppermute | solution.py:191
  5.9 11.8 %collective-permute-start.7 = (f32[1,4,512]{2,1,0:T(4,128)S(1)}, f32[1,4,512]{2,1,0:T(4,128)S(1)}, u32[]{:S(2)}, u32[]{:S(2)}) collective-permute-start(f32[1,4,512]{2,1,0:T(4,128)S(1)} %get-tuple-element.35), channel_id=1, source_target_pairs={{4,0},{8,4},{12,8},{16,12},{20,16},{24,20},{28,24},{5,1},{9,5},{13... | collective-permute-start | bytes 24584 | tf_op jit(solution)/shard_map/ppermute | solution.py:192
  7.2 10.5 %collective-permute-start.8 = (f32[1,4,512]{2,1,0:T(4,128)S(1)}, f32[1,4,512]{2,1,0:T(4,128)S(1)}, u32[]{:S(2)}, u32[]{:S(2)}) collective-permute-start(f32[1,4,512]{2,1,0:T(4,128)S(1)} %get-tuple-element.36), channel_id=1, source_target_pairs={{0,4},{4,8},{8,12},{12,16},{16,20},{20,24},{24,28},{1,5},{5,9},{9,... | collective-permute-start | bytes 24584 | tf_op jit(solution)/shard_map/ppermute | solution.py:191
  15.4 16.4 %collective-permute-start.21 = (bf16[18,128,128]{2,1,0:T(8,128)(2,1)S(1)}, bf16[18,128,128]{2,1,0:T(8,128)(2,1)}, u32[]{:S(2)}, u32[]{:S(2)}) collective-permute-start(bf16[18,128,128]{2,1,0:T(8,128)(2,1)S(1)} %shard_map.66.rest_0_), channel_id=1, source_target_pairs={{0,8},{4,12},{8,0},{12,4},{16,24},{20,28},{24,16},{28,20},{1,9},{5... | collective-permute-start | bytes 1769480 | tf_op jit(solution)/shard_map/ppermute | solution.py:154
  22.5 1.9 collective-permute-start.11
  22.9 57.3 %collective-permute-start.27 = (bf16[18,128,128]{2,1,0:T(8,128)(2,1)S(1)}, bf16[18,128,128]{2,1,0:T(8,128)(2,1)}, u32[]{:S(2)}, u32[]{:S(2)}) collective-permute-start(bf16[18,128,128]{2,1,0:T(8,128)(2,1)S(1)} %shard_map.66.rest_0_), channel_id=1, source_target_pairs={{8,16},{12,20},{16,8},{20,12},{9,17},{13,21},{17,9},{21,13},{10,18... | collective-permute-start | bytes 1769480 | tf_op jit(solution)/shard_map/ppermute | solution.py:168
  24.4 8.9 %collective-permute-start.12 = (f32[192,128]{1,0:T(8,128)S(1)}, f32[192,128]{1,0:T(8,128)S(1)}, u32[]{:S(2)}, u32[]{:S(2)}) collective-permute-start(f32[192,128]{1,0:T(8,128)S(1)} %select_add_fusion), channel_id=1, source_target_pairs={{0,2},{1,3},{2,0},{3,1},{4,6},{5,7},{6,4},{7,5},{8,10},{9,11},{10,... | collective-permute-start | bytes 294920 | tf_op jit(solution)/shard_map/ppermute | solution.py:159
  27.0 51.7 %collective-permute-start.1 = (bf16[384,384]{1,0:T(8,128)(2,1)S(1)}, bf16[384,384]{1,0:T(8,128)(2,1)S(1)}, u32[]{:S(2)}, u32[]{:S(2)}) collective-permute-start(bf16[384,384]{1,0:T(8,128)(2,1)S(1)} %get-tuple-element.18), channel_id=1, source_target_pairs={{0,8},{4,12},{8,0},{12,4},{16,24},{20,28},{24,16},{28,20},{1,9},{5... | collective-permute-start | bytes 884744 | tf_op jit(solution)/shard_map/ppermute | solution.py:154
  30.6 50.9 %collective-permute-start.3 = (bf16[384,384]{1,0:T(8,128)(2,1)S(1)}, bf16[384,384]{1,0:T(8,128)(2,1)S(1)}, u32[]{:S(2)}, u32[]{:S(2)}) collective-permute-start(bf16[384,384]{1,0:T(8,128)(2,1)S(1)} %get-tuple-element.19), channel_id=1, source_target_pairs={{0,16},{4,20},{8,24},{12,28},{16,0},{20,4},{24,8},{28,12},{1,17},{... | collective-permute-start | bytes 884744 | tf_op jit(solution)/shard_map/ppermute | solution.py:154
  31.9 53.6 %collective-permute-start.26 = (bf16[18,128,128]{2,1,0:T(8,128)(2,1)}, bf16[18,128,128]{2,1,0:T(8,128)(2,1)}, u32[]{:S(2)}, u32[]{:S(2)}) collective-permute-start(bf16[18,128,128]{2,1,0:T(8,128)(2,1)} %collective-permute-done.21.rest_0_), channel_id=1, source_target_pairs={{8,16},{12,20},{16,8},{20,12},{9,17},{13,21},{17,9},{21,13},{10,18... | collective-permute-start | bytes 1769480 | tf_op jit(solution)/shard_map/ppermute | solution.py:168
  33.4 14.3 %collective-permute-start.15 = (bf16[192,128]{1,0:T(8,128)(2,1)S(1)}, bf16[192,128]{1,0:T(8,128)(2,1)S(1)}, u32[]{:S(2)}, u32[]{:S(2)}) collective-permute-start(bf16[192,128]{1,0:T(8,128)(2,1)S(1)} %multiply_convert_fusion.1), channel_id=1, source_target_pairs={{0,24},{4,28},{8,16},{12,20},{16,8},{20,12},{24,0},{28,4},{1,25},{... | collective-permute-start | bytes 147464 | tf_op jit(solution)/shard_map/ppermute | solution.py:154
  47.7 25.0 %collective-permute-start.14 = (bf16[192,128]{1,0:T(8,128)(2,1)S(1)}, bf16[192,128]{1,0:T(8,128)(2,1)S(1)}, u32[]{:S(2)}, u32[]{:S(2)}) collective-permute-start(bf16[192,128]{1,0:T(8,128)(2,1)S(1)} %multiply_convert_fusion.1), channel_id=1, source_target_pairs={{0,16},{4,20},{8,24},{12,28},{16,0},{20,4},{24,8},{28,12},{1,17},{... | collective-permute-start | bytes 147464 | tf_op jit(solution)/shard_map/ppermute | solution.py:154
  72.7 14.1 %copy-start.21 = (bf16[192,128]{1,0:T(8,128)(2,1)}, bf16[192,128]{1,0:T(8,128)(2,1)S(1)}, u32[]{:S(2)}) copy-start(bf16[192,128]{1,0:T(8,128)(2,1)S(1)} %collective-permute-done.14) | copy-start | bytes 147460
  72.7 4.1 %collective-permute-start.13 = (bf16[192,128]{1,0:T(8,128)(2,1)S(1)}, bf16[192,128]{1,0:T(8,128)(2,1)S(1)}, u32[]{:S(2)}, u32[]{:S(2)}) collective-permute-start(bf16[192,128]{1,0:T(8,128)(2,1)S(1)} %multiply_convert_fusion.1), channel_id=1, source_target_pairs={{0,8},{4,12},{8,0},{12,4},{16,24},{20,28},{24,16},{28,20},{1,9},{5... | collective-permute-start | bytes 147464 | tf_op jit(solution)/shard_map/ppermute | solution.py:154
  76.8 8.6 %collective-permute-start.5 = (bf16[384,384]{1,0:T(8,128)(2,1)S(1)}, bf16[384,384]{1,0:T(8,128)(2,1)S(1)}, u32[]{:S(2)}, u32[]{:S(2)}) collective-permute-start(bf16[384,384]{1,0:T(8,128)(2,1)S(1)} %get-tuple-element.20), channel_id=1, source_target_pairs={{0,24},{4,28},{8,16},{12,20},{16,8},{20,12},{24,0},{28,4},{1,25},{... | collective-permute-start | bytes 884744 | tf_op jit(solution)/shard_map/ppermute | solution.py:154
  78.7 12.4 %collective-permute-start.18 = (bf16[18,128,128]{2,1,0:T(8,128)(2,1)S(1)}, bf16[18,128,128]{2,1,0:T(8,128)(2,1)S(1)}, u32[]{:S(2)}, u32[]{:S(2)}) collective-permute-start(bf16[18,128,128]{2,1,0:T(8,128)(2,1)S(1)} %shard_map.66.rest_0_), channel_id=1, source_target_pairs={{0,2},{1,3},{2,0},{3,1},{4,6},{5,7},{6,4},{7,5},{8,10},{9,11},{10,... | collective-permute-start | bytes 1769480 | tf_op jit(solution)/shard_map/ppermute | solution.py:159
  80.2 18.5 %collective-permute-start.28 = (bf16[18,128,128]{2,1,0:T(8,128)(2,1)}, bf16[18,128,128]{2,1,0:T(8,128)(2,1)}, u32[]{:S(2)}, u32[]{:S(2)}) collective-permute-start(bf16[18,128,128]{2,1,0:T(8,128)(2,1)} %collective-permute-done.27), channel_id=1, source_target_pairs={{8,0},{12,4},{16,24},{20,28},{9,1},{13,5},{17,25},{21,29},{10,2},{... | collective-permute-start | bytes 1769480 | tf_op jit(solution)/shard_map/ppermute | solution.py:168
  81.5 6.8 %collective-permute-start = (bf16[384,384]{1,0:T(8,128)(2,1)S(1)}, bf16[384,384]{1,0:T(8,128)(2,1)S(1)}, u32[]{:S(2)}, u32[]{:S(2)}) collective-permute-start(bf16[384,384]{1,0:T(8,128)(2,1)S(1)} %get-tuple-element.17.rest_0_.rest_1_), channel_id=1, source_target_pairs={{0,4},{4,0},{8,12},{12,8},{16,20},{20,16},{24,28},{28,24},{1,5},{5... | collective-permute-start | bytes 884744 | tf_op jit(solution)/shard_map/ppermute | solution.py:154
  85.4 15.3 %collective-permute-start.17 = (bf16[18,128,128]{2,1,0:T(8,128)(2,1)S(1)}, bf16[18,128,128]{2,1,0:T(8,128)(2,1)S(1)}, u32[]{:S(2)}, u32[]{:S(2)}) collective-permute-start(bf16[18,128,128]{2,1,0:T(8,128)(2,1)S(1)} %shard_map.66.rest_0_), channel_id=1, source_target_pairs={{0,1},{1,0},{2,3},{3,2},{4,5},{5,4},{6,7},{7,6},{8,9},{9,8},{10,11... | collective-permute-start | bytes 1769480 | tf_op jit(solution)/shard_map/ppermute | solution.py:159
  85.4 25.2 %collective-permute-start.33 = (bf16[18,128,128]{2,1,0:T(8,128)(2,1)}, bf16[18,128,128]{2,1,0:T(8,128)(2,1)}, u32[]{:S(2)}, u32[]{:S(2)}) collective-permute-start(bf16[18,128,128]{2,1,0:T(8,128)(2,1)} %collective-permute-done.26), channel_id=1, source_target_pairs={{8,0},{12,4},{16,24},{20,28},{9,1},{13,5},{17,25},{21,29},{10,2},{... | collective-permute-start | bytes 1769480 | tf_op jit(solution)/shard_map/ppermute | solution.py:168
  88.3 1.4 collective-permute-start.16
  89.8 11.9 %collective-permute-start.2 = (bf16[384,384]{1,0:T(8,128)(2,1)S(1)}, bf16[384,384]{1,0:T(8,128)(2,1)}, u32[]{:S(2)}, u32[]{:S(2)}) collective-permute-start(bf16[384,384]{1,0:T(8,128)(2,1)S(1)} %collective-permute-done.1.rest_2_.rest_1_), channel_id=1, source_target_pairs={{0,4},{4,0},{8,12},{12,8},{16,20},{20,16},{24,28},{28,24},{1,5},{5... | collective-permute-start | bytes 884744 | tf_op jit(solution)/shard_map/ppermute | solution.py:154
  90.6 49.6 %copy-start.22 = (bf16[192,128]{1,0:T(8,128)(2,1)S(1)}, bf16[192,128]{1,0:T(8,128)(2,1)}, u32[]{:S(2)}) copy-start(bf16[192,128]{1,0:T(8,128)(2,1)} %copy-done.21) | copy-start | bytes 147460
  90.6 49.6 %copy-start.24 = (bf16[192,128]{1,0:T(8,128)(2,1)S(1)}, bf16[192,128]{1,0:T(8,128)(2,1)}, u32[]{:S(2)}) copy-start(bf16[192,128]{1,0:T(8,128)(2,1)} %copy-done.23) | copy-start | bytes 147460
  91.1 22.0 %collective-permute-start.4 = (bf16[384,384]{1,0:T(8,128)(2,1)S(1)}, bf16[384,384]{1,0:T(8,128)(2,1)S(1)}, u32[]{:S(2)}, u32[]{:S(2)}) collective-permute-start(bf16[384,384]{1,0:T(8,128)(2,1)S(1)} %collective-permute-done.3.rest_4_.rest_1_), channel_id=1, source_target_pairs={{0,4},{4,0},{8,12},{12,8},{16,20},{20,16},{24,28},{28,24},{1,5},{5... | collective-permute-start | bytes 884744 | tf_op jit(solution)/shard_map/ppermute | solution.py:154
  98.7 14.6 %collective-permute-start.6 = (bf16[384,384]{1,0:T(8,128)(2,1)S(1)}, bf16[384,384]{1,0:T(8,128)(2,1)S(1)}, u32[]{:S(2)}, u32[]{:S(2)}) collective-permute-start(bf16[384,384]{1,0:T(8,128)(2,1)S(1)} %collective-permute-done.5.rest_6_.rest_1_), channel_id=1, source_target_pairs={{0,4},{4,0},{8,12},{12,8},{16,20},{20,16},{24,28},{28,24},{1,5},{5... | collective-permute-start | bytes 884744 | tf_op jit(solution)/shard_map/ppermute | solution.py:154
  100.7 16.5 %collective-permute-start.23 = (bf16[18,128,128]{2,1,0:T(8,128)(2,1)}, bf16[18,128,128]{2,1,0:T(8,128)(2,1)S(1)}, u32[]{:S(2)}, u32[]{:S(2)}) collective-permute-start(bf16[18,128,128]{2,1,0:T(8,128)(2,1)} %collective-permute-done.21.rest_0_), channel_id=1, source_target_pairs={{0,2},{1,3},{2,0},{3,1},{4,6},{5,7},{6,4},{7,5},{8,10},{9,11},{10,... | collective-permute-start | bytes 1769480 | tf_op jit(solution)/shard_map/ppermute | solution.py:159
  101.6 15.6 %collective-permute-start.22 = (bf16[18,128,128]{2,1,0:T(8,128)(2,1)}, bf16[18,128,128]{2,1,0:T(8,128)(2,1)S(1)}, u32[]{:S(2)}, u32[]{:S(2)}) collective-permute-start(bf16[18,128,128]{2,1,0:T(8,128)(2,1)} %collective-permute-done.21.rest_0_), channel_id=1, source_target_pairs={{0,1},{1,0},{2,3},{3,2},{4,5},{5,4},{6,7},{7,6},{8,9},{9,8},{10,11... | collective-permute-start | bytes 1769480 | tf_op jit(solution)/shard_map/ppermute | solution.py:159
  110.6 19.3 %collective-permute-start.30 = (bf16[18,128,128]{2,1,0:T(8,128)(2,1)S(1)}, bf16[18,128,128]{2,1,0:T(8,128)(2,1)S(1)}, u32[]{:S(2)}, u32[]{:S(2)}) collective-permute-start(bf16[18,128,128]{2,1,0:T(8,128)(2,1)S(1)} %broadcast_select_fusion.1.rest_0_), channel_id=1, source_target_pairs={{0,2},{1,3},{2,0},{3,1},{4,6},{5,7},{6,4},{7,5},{8,10},{9,11},{10,... | collective-permute-start | bytes 1769480 | tf_op jit(solution)/shard_map/ppermute | solution.py:159
  113.1 29.8 %copy-start.16 = (s32[24,24]{1,0:T(8,128)S(1)}, s32[24,24]{1,0:T(8,128)}, u32[]{:S(2)}) copy-start(s32[24,24]{1,0:T(8,128)} %hmask.9) | copy-start | bytes 6916
  113.2 16.7 %collective-permute-start.19 = (bf16[18,128,128]{2,1,0:T(8,128)(2,1)S(1)}, bf16[18,128,128]{2,1,0:T(8,128)(2,1)S(1)}, u32[]{:S(2)}, u32[]{:S(2)}) collective-permute-start(bf16[18,128,128]{2,1,0:T(8,128)(2,1)S(1)} %collective-permute-done.18.rest_2_), channel_id=1, source_target_pairs={{0,1},{1,0},{2,3},{3,2},{4,5},{5,4},{6,7},{7,6},{8,9},{9,8},{10,11... | collective-permute-start | bytes 1769480 | tf_op jit(solution)/shard_map/ppermute | solution.py:159
  113.3 27.0 %collective-permute-start.35 = (bf16[18,128,128]{2,1,0:T(8,128)(2,1)S(1)}, bf16[18,128,128]{2,1,0:T(8,128)(2,1)S(1)}, u32[]{:S(2)}, u32[]{:S(2)}) collective-permute-start(bf16[18,128,128]{2,1,0:T(8,128)(2,1)S(1)} %broadcast_select_fusion.rest_0_), channel_id=1, source_target_pairs={{0,2},{1,3},{2,0},{3,1},{4,6},{5,7},{6,4},{7,5},{8,10},{9,11},{10,... | collective-permute-start | bytes 1769480 | tf_op jit(solution)/shard_map/ppermute | solution.py:159
  117.2 24.3 %copy-start.9 = (bf16[18,128,128]{2,1,0:T(8,128)(2,1)}, bf16[18,128,128]{2,1,0:T(8,128)(2,1)S(1)}, u32[]{:S(2)}) copy-start(bf16[18,128,128]{2,1,0:T(8,128)(2,1)S(1)} %collective-permute-done.23.rest_2_) | copy-start | bytes 1769476
  117.2 30.4 %collective-permute-start.24 = (bf16[18,128,128]{2,1,0:T(8,128)(2,1)S(1)}, bf16[18,128,128]{2,1,0:T(8,128)(2,1)S(1)}, u32[]{:S(2)}, u32[]{:S(2)}) collective-permute-start(bf16[18,128,128]{2,1,0:T(8,128)(2,1)S(1)} %collective-permute-done.23.rest_2_), channel_id=1, source_target_pairs={{0,1},{1,0},{2,3},{3,2},{4,5},{5,4},{6,7},{7,6},{8,9},{9,8},{10,11... | collective-permute-start | bytes 1769480 | tf_op jit(solution)/shard_map/ppermute | solution.py:159
  117.3 24.3 %copy-start.11 = (bf16[18,128,128]{2,1,0:T(8,128)(2,1)}, bf16[18,128,128]{2,1,0:T(8,128)(2,1)S(1)}, u32[]{:S(2)}) copy-start(bf16[18,128,128]{2,1,0:T(8,128)(2,1)S(1)} %collective-permute-done.22.rest_1_) | copy-start | bytes 1769476
  117.3 37.7 %collective-permute-start.29 = (bf16[18,128,128]{2,1,0:T(8,128)(2,1)S(1)}, bf16[18,128,128]{2,1,0:T(8,128)(2,1)}, u32[]{:S(2)}, u32[]{:S(2)}) collective-permute-start(bf16[18,128,128]{2,1,0:T(8,128)(2,1)S(1)} %broadcast_select_fusion.1.rest_0_), channel_id=1, source_target_pairs={{0,1},{1,0},{2,3},{3,2},{4,5},{5,4},{6,7},{7,6},{8,9},{9,8},{10,11... | collective-permute-start | bytes 1769480 | tf_op jit(solution)/shard_map/ppermute | solution.py:159
  129.9 26.4 %collective-permute-start.31 = (bf16[18,128,128]{2,1,0:T(8,128)(2,1)S(1)}, bf16[18,128,128]{2,1,0:T(8,128)(2,1)}, u32[]{:S(2)}, u32[]{:S(2)}) collective-permute-start(bf16[18,128,128]{2,1,0:T(8,128)(2,1)S(1)} %collective-permute-done.30.rest_2_), channel_id=1, source_target_pairs={{0,1},{1,0},{2,3},{3,2},{4,5},{5,4},{6,7},{7,6},{8,9},{9,8},{10,11... | collective-permute-start | bytes 1769480 | tf_op jit(solution)/shard_map/ppermute | solution.py:159
  129.9 32.3 %collective-permute-start.34 = (bf16[18,128,128]{2,1,0:T(8,128)(2,1)S(1)}, bf16[18,128,128]{2,1,0:T(8,128)(2,1)}, u32[]{:S(2)}, u32[]{:S(2)}) collective-permute-start(bf16[18,128,128]{2,1,0:T(8,128)(2,1)S(1)} %broadcast_select_fusion.rest_0_), channel_id=1, source_target_pairs={{0,1},{1,0},{2,3},{3,2},{4,5},{5,4},{6,7},{7,6},{8,9},{9,8},{10,11... | collective-permute-start | bytes 1769480 | tf_op jit(solution)/shard_map/ppermute | solution.py:159
  140.2 22.0 %collective-permute-start.36 = (bf16[18,128,128]{2,1,0:T(8,128)(2,1)S(1)}, bf16[18,128,128]{2,1,0:T(8,128)(2,1)}, u32[]{:S(2)}, u32[]{:S(2)}) collective-permute-start(bf16[18,128,128]{2,1,0:T(8,128)(2,1)S(1)} %collective-permute-done.35.rest_2_), channel_id=1, source_target_pairs={{0,1},{1,0},{2,3},{3,2},{4,5},{5,4},{6,7},{7,6},{8,9},{9,8},{10,11... | collective-permute-start | bytes 1769480 | tf_op jit(solution)/shard_map/ppermute | solution.py:159
  148.4 21.2 %collective-permute-start.20 = (bf16[384,384]{1,0:T(8,128)(2,1)S(1)}, bf16[384,384]{1,0:T(8,128)(2,1)}, u32[]{:S(2)}, u32[]{:S(2)}) collective-permute-start(bf16[384,384]{1,0:T(8,128)(2,1)S(1)} %get-tuple-element.21.rest_0_.rest_2_), channel_id=1, source_target_pairs={{0,4},{4,0},{8,12},{12,8},{16,20},{20,16},{24,28},{28,24},{1,5},{5... | collective-permute-start | bytes 884744 | tf_op jit(solution)/shard_map/ppermute | solution.py:154
  155.0 14.7 %collective-permute-start.25 = (bf16[384,384]{1,0:T(8,128)(2,1)S(1)}, bf16[384,384]{1,0:T(8,128)(2,1)S(1)}, u32[]{:S(2)}, u32[]{:S(2)}) collective-permute-start(bf16[384,384]{1,0:T(8,128)(2,1)S(1)} %get-tuple-element.22.rest_2_), channel_id=1, source_target_pairs={{0,4},{4,0},{8,12},{12,8},{16,20},{20,16},{24,28},{28,24},{1,5},{5... | collective-permute-start | bytes 884744 | tf_op jit(solution)/shard_map/ppermute | solution.py:154
  161.3 18.8 %copy-start.5 = (bf16[384,384]{1,0:T(8,128)(2,1)}, bf16[384,384]{1,0:T(8,128)(2,1)S(1)}, u32[]{:S(2)}) copy-start(bf16[384,384]{1,0:T(8,128)(2,1)S(1)} %get-tuple-element.23.rest_4_.rest_2_) | copy-start | bytes 884740
  161.3 9.2 %collective-permute-start.32 = (bf16[384,384]{1,0:T(8,128)(2,1)S(1)}, bf16[384,384]{1,0:T(8,128)(2,1)S(1)}, u32[]{:S(2)}, u32[]{:S(2)}) collective-permute-start(bf16[384,384]{1,0:T(8,128)(2,1)S(1)} %get-tuple-element.23.rest_4_.rest_2_), channel_id=1, source_target_pairs={{0,4},{4,0},{8,12},{12,8},{16,20},{20,16},{24,28},{28,24},{1,5},{5... | collective-permute-start | bytes 884744 | tf_op jit(solution)/shard_map/ppermute | solution.py:154
  168.4 8.6 %collective-permute-start.37 = (bf16[384,384]{1,0:T(8,128)(2,1)S(1)}, bf16[384,384]{1,0:T(8,128)(2,1)S(1)}, u32[]{:S(2)}, u32[]{:S(2)}) collective-permute-start(bf16[384,384]{1,0:T(8,128)(2,1)S(1)} %get-tuple-element.24.rest_6_.rest_2_), channel_id=1, source_target_pairs={{0,4},{4,0},{8,12},{12,8},{16,20},{20,16},{24,28},{28,24},{1,5},{5... | collective-permute-start | bytes 884744 | tf_op jit(solution)/shard_map/ppermute | solution.py:154
  181.6 12.1 %collective-permute-start.38 = (bf16[384,384]{1,0:T(8,128)(2,1)S(1)}, bf16[384,384]{1,0:T(8,128)(2,1)S(1)}, u32[]{:S(2)}, u32[]{:S(2)}) collective-permute-start(bf16[384,384]{1,0:T(8,128)(2,1)S(1)} %shard_map.73), channel_id=1, source_target_pairs={{0,8},{4,12},{8,0},{12,4},{16,24},{20,28},{24,16},{28,20},{1,9},{5... | collective-permute-start | bytes 884744 | tf_op jit(solution)/shard_map/ppermute | solution.py:154
  183.1 23.6 %collective-permute-start.39 = (bf16[384,384]{1,0:T(8,128)(2,1)S(1)}, bf16[384,384]{1,0:T(8,128)(2,1)S(1)}, u32[]{:S(2)}, u32[]{:S(2)}) collective-permute-start(bf16[384,384]{1,0:T(8,128)(2,1)S(1)} %shard_map.74), channel_id=1, source_target_pairs={{0,16},{4,20},{8,24},{12,28},{16,0},{20,4},{24,8},{28,12},{1,17},{... | collective-permute-start | bytes 884744 | tf_op jit(solution)/shard_map/ppermute | solution.py:154
  187.5 19.2 %collective-permute-start.40 = (bf16[384,384]{1,0:T(8,128)(2,1)S(1)}, bf16[384,384]{1,0:T(8,128)(2,1)S(1)}, u32[]{:S(2)}, u32[]{:S(2)}) collective-permute-start(bf16[384,384]{1,0:T(8,128)(2,1)S(1)} %shard_map.75), channel_id=1, source_target_pairs={{0,24},{4,28},{8,16},{12,20},{16,8},{20,12},{24,0},{28,4},{1,25},{... | collective-permute-start | bytes 884744 | tf_op jit(solution)/shard_map/ppermute | solution.py:154
  (18 other events, 60.9 us)

commit v2 on v0

v2 whole, which is shorter than its diff:
```python
import functools

import jax
import jax.numpy as jnp
from jax import lax
from jax.experimental import pallas as pl
from jax.experimental.pallas import tpu as pltpu
from jax.sharding import PartitionSpec as P

BLK = 128
KAPPA = 0.4
TIME_STEP = 0.5
BF16 = jnp.bfloat16
F32 = jnp.float32
VMEM_BYTES = 48 * 1024 * 1024

SMEM_SPEC = pl.BlockSpec(memory_space=pltpu.SMEM)
VMEM_SPEC = pl.BlockSpec(memory_space=pltpu.VMEM)


def call(body, scalars, arrays, outs, scratch=(), flops=0, weight=1):
    moved = sum(a.size * a.dtype.itemsize for a in arrays)
    moved += sum(o.size * o.dtype.itemsize for o in outs)
    return pl.pallas_call(
        body,
        out_shape=tuple(outs),
        in_specs=[SMEM_SPEC] * len(scalars) + [VMEM_SPEC] * len(arrays),
        out_specs=tuple(VMEM_SPEC for _ in outs),
        scratch_shapes=list(scratch),
        compiler_params=pltpu.CompilerParams(vmem_limit_bytes=VMEM_BYTES),
        cost_estimate=pl.CostEstimate(flops=flops, bytes_accessed=weight * moved, transcendentals=0),
    )(*scalars, *arrays)


def shape(*dims, dtype=BF16):
    return jax.ShapeDtypeStruct(dims, dtype)


def kept(mask, row, start, kb, width):
    place = jnp.int32(0)
    for k in range(kb):
        for j in range(width):
            keep = mask[row * kb + k, start + j] != 0
            yield k, j, keep, place
            place = place + keep.astype(jnp.int32)


def pack_kernel(cap, kb, jb, info, hmask, h, h_core, quarter, packed, slots):
    core = info[1] % 2
    for k, j, _, place in kept(hmask, info[0], (info[1] - core) * jb, kb, 2 * jb):
        columns = slice(j % jb * BLK, (j % jb + 1) * BLK)
        block = jnp.where(core == j // jb, h[k * BLK : (k + 1) * BLK, columns], h_core[k * BLK : (k + 1) * BLK, columns])
        here = jnp.clip(place - core * cap, -1, cap) + 1
        slots[pl.ds(pl.multiple_of(here * BLK, BLK), BLK), :] = block
    packed[: cap * BLK, :] = slots[BLK : (cap + 1) * BLK, :]
    packed[cap * BLK :, :] = quarter[...]


def turn_kernel(cap, zs, kb, jb, info, pmask, p, *rest):
    pieces, turned = rest[:-1], rest[-1]
    wide = BLK // zs
    for k, j, _, place in kept(pmask, info[0], info[1] * jb, kb, jb):
        for part in range(2):
            here = p[part, k * BLK : (k + 1) * BLK, j * BLK : (j + 1) * BLK]
            top = pl.multiple_of((2 * place + part) * BLK, BLK)
            turned[pl.ds(top, BLK), :] = here.T
    for s in range(zs):
        start = pl.multiple_of(((info[0] // 2) ^ s) * wide, wide)
        for i in range(2 * cap):
            pieces[s][i * wide : (i + 1) * wide, :] = turned[pl.ds(i * BLK + start, wide), :]


def return_kernel(cap, zs, kb, jb, info, pmask, p, *rest):
    pieces, out, turned = rest[:zs], rest[zs], rest[zs + 1]
    wide = BLK // zs
    for s in range(zs):
        start = pl.multiple_of(((info[0] // 2) ^ s) * wide, wide)
        for i in range(2 * cap):
            turned[pl.ds(i * BLK + start, wide), :] = pieces[s][i * wide : (i + 1) * wide, :]
    for k, j, keep, place in kept(pmask, info[0], info[1] * jb, kb, jb):
        for part in range(2):
            block = (part, slice(k * BLK, (k + 1) * BLK), slice(j * BLK, (j + 1) * BLK))
            top = pl.multiple_of((2 * jnp.minimum(place, cap - 1) + part) * BLK, BLK)
            both = p[block].astype(F32) + turned[pl.ds(top, BLK), :].T.astype(F32)
            out[block] = jnp.where(keep, both, jnp.zeros_like(both)).astype(BF16)


def unpack_kernel(cap, zs, kb, jb, info, pmask, *rest):
    out = rest[-1]
    wide = BLK // zs
    for s in range(zs):
        for other in range(2):
            piece = rest[2 * s + other]
            row = info[0] ^ (2 * s + other)
            for k, j, keep, place in kept(pmask, row, info[1] * jb, kb, jb):
                columns = pl.ds(pl.multiple_of((row * kb + k) * BLK, BLK), BLK)
                for part in range(2):
                    top = pl.multiple_of((2 * jnp.minimum(place, cap - 1) + part) * wide, wide)
                    here = piece[pl.ds(top, wide), :]
                    rows = slice((part * jb + j) * wide, (part * jb + j + 1) * wide)
                    out[rows, columns] = jnp.where(keep, here, jnp.zeros_like(here))


def join_kernel(zs, side, info, *rest):
    out = rest[-1]
    for i in range(2 * zs):
        out[:, pl.ds(pl.multiple_of((info[0] ^ i) * side, side), side)] = rest[i][...]


def spread_kernel(s, cap, kb, jb, info, hmask, *rest):
    packed, (dense, diagonal, slots) = rest[:-3], rest[-3:]
    row = info[0] ^ (2 * s)
    part = kb * BLK // 4
    for m in range(4):
        col = info[1] ^ m
        start = pl.multiple_of(col % 2 * (cap * BLK), BLK)
        slots[pl.ds(start, cap * BLK), :] = packed[m][: cap * BLK, :]
        start = pl.multiple_of((2 * (col % 2) + col // 2) * part, part)
        diagonal[pl.ds(start, part), :] = packed[m][cap * BLK :, :]
        if m % 2 == 0:
            continue
        left = col // 2 * (2 * jb)
        for k, j, keep, place in kept(hmask, row, left, kb, 2 * jb):
            source = pl.multiple_of(jnp.minimum(place, 2 * cap - 1) * BLK, BLK)
            start = pl.multiple_of((left + j) * BLK, BLK)
            here = slots[pl.ds(source, BLK), :]
            dense[k * BLK : (k + 1) * BLK, pl.ds(start, BLK)] = jnp.where(keep, here, jnp.zeros_like(here))
    for k in range(kb):
        rows = pl.ds(k * BLK, BLK)
        columns = pl.ds(pl.multiple_of((row * kb + k) * BLK, BLK), BLK)
        both = dense[rows, columns].astype(F32) + diagonal[k * BLK : (k + 1) * BLK, :].astype(F32)
        dense[rows, columns] = both.astype(BF16)


def integral_kernel(effective, basis, total):
    width_x, width_y = effective.shape[:2]
    for k in range(total.shape[0] // BLK):
        rows = slice(k * BLK, (k + 1) * BLK)
        for x in range(width_x):
            for y in range(width_y):
                values = basis[x, y, rows, :]
                weighted = (values.astype(F32) * effective[x, y : y + 1, :]).astype(BF16)
                here = lax.dot_general(weighted, values, (((1,), (1,)), ((), ())), preferred_element_type=F32)
                total[rows, :] = here if x + y == 0 else total[rows, :] + here


def first_kernel(joined, dense, first):
    first[...] = lax.dot_general(
        joined[...], dense[...], (((1,), (1,)), ((), ())), preferred_element_type=F32
    ).astype(BF16)


def second_kernel(slots, cap, zs, kb, jb, info, pmask, joined, *rest):
    half_square = 0.5 * TIME_STEP * TIME_STEP
    count = len(slots)
    dense, first, packed, (change, room) = rest[:count], rest[count : 2 * count], rest[2 * count : -2], rest[-2:]
    wide = BLK // zs
    for i, s in enumerate(slots):
        second = lax.dot_general(
            joined[...], dense[i][...], (((1,), (1,)), ((), ())), preferred_element_type=F32
        )
        half = second.shape[0] // 2
        real, imag = slice(0, half), slice(half, 2 * half)
        other = first[i]
        change[i, real, :] = (TIME_STEP * other[imag, :].astype(F32) - half_square * second[real, :]).astype(BF16)
        change[i, imag, :] = (-TIME_STEP * other[real, :].astype(F32) - half_square * second[imag, :]).astype(BF16)
        for k, j, _, place in kept(pmask, info[0] ^ (2 * s), info[1] * jb, kb, jb):
            for part in range(2):
                top = pl.multiple_of((2 * place + part) * wide, wide)
                rows = slice((part * jb + j) * wide, (part * jb + j + 1) * wide)
                room[i, pl.ds(top, wide), :] = change[i, rows, k * BLK : (k + 1) * BLK]
        packed[i][...] = room[i, : 2 * cap * wide, :]


def swap_row(value, bits):
    count = lax.axis_size("row")
    return lax.ppermute(value, "row", [(i, i ^ bits) for i in range(count)])


def swap_col(value, bits):
    count = lax.axis_size("col")
    return lax.ppermute(value, "col", [(i, i ^ bits) for i in range(count)])


def along(value, pairs):
    return lax.ppermute(value, "row", [(2 * a + x, 2 * b + x) for a, b in pairs for x in range(2)])


def after(done, *values):
    return lax.optimization_barrier((values, done))[0]


def effective_potential(potential):
    def beyond(axis, dim):
        count = lax.axis_size(axis)
        forward = [(i, i + 1) for i in range(count - 1)]
        backward = [(target, source) for source, target in forward]
        last = potential.shape[dim] - 1
        low = lax.ppermute(lax.slice_in_dim(potential, last, None, axis=dim), axis, forward)
        high = lax.ppermute(lax.slice_in_dim(potential, 0, 1, axis=dim), axis, backward)
        return jnp.concatenate([low, potential, high], axis=dim)

    in_x, in_y = beyond("row", 0), beyond("col", 1)
    in_z = jnp.pad(potential, ((0, 0), (0, 0), (1, 1)))
    beside = in_x[2:] + in_x[:-2]
    beside = beside + in_y[:, 2:] + in_y[:, :-2]
    beside = beside + in_z[:, :, 2:] + in_z[:, :, :-2]
    return potential + KAPPA * (beside - 6.0 * potential)


def potential_blocks(potential, basis):
    width_x, width_y, depth_z = potential.shape
    kb = basis.shape[2] // BLK
    effective = effective_potential(potential)
    (total,) = call(
        integral_kernel,
        [],
        [effective, basis],
        [shape(kb * BLK, BLK, dtype=F32)],
        flops=2 * basis.size * BLK,
        weight=32,
    )
    for bits, side in ((1, lax.axis_index("col") % 2), (2, lax.axis_index("col") // 2)):
        half = total.shape[0] // 2
        low, high = total[:half], total[half:]
        total = jnp.where(side == 0, low, high) + swap_col(jnp.where(side == 0, high, low), bits)
    factor = float(BLK * width_x * width_y * depth_z * lax.axis_size("col")) ** (-0.5)
    return (total * factor).astype(BF16)


def step(cap, cap_h, potential, basis, hamiltonian, density, hmask, pmask):
    row, col = lax.axis_index("row"), lax.axis_index("col")
    info = jnp.stack([row, col]).astype(jnp.int32)
    z = row // 2
    zs = lax.axis_size("row") // 2
    side, across = hamiltonian.shape
    order = side * lax.axis_size("row")
    kb, jb = side // BLK, across // BLK
    wide = 2 * across // zs
    piece = shape(2 * cap * BLK // zs, BLK)

    pieces = call(
        functools.partial(turn_kernel, cap, zs, kb, jb),
        [info, pmask],
        [density],
        [piece] * zs,
        scratch=[pltpu.VMEM((2 * (kb * jb + 1) * BLK, BLK), BF16)],
    )

    mine = [pieces[s] if s == 0 else swap_row(pieces[s], 2 * s) for s in range(zs)]
    theirs = [swap_row(piece, 1) for piece in mine]
    hamiltonian_core = swap_col(hamiltonian, 1)
    (potential,) = after((hamiltonian_core, *pieces), potential)
    quarter = potential_blocks(potential, basis)
    hamiltonian, quarter = after(tuple(mine[1:]), hamiltonian, quarter)
    (own,) = call(
        functools.partial(pack_kernel, cap_h, kb, jb),
        [info, hmask],
        [hamiltonian, hamiltonian_core, quarter],
        [shape(cap_h * BLK + side // 4, BLK)],
        scratch=[pltpu.VMEM(((cap_h + 2) * BLK, BLK), BF16)],
    )

    def spread(s, near, far, near_core, far_core):
        return call(
            functools.partial(spread_kernel, s, cap_h, kb, jb),
            [info, hmask],
            [near, near_core, far, far_core],
            [shape(side, order)],
            scratch=[pltpu.VMEM((side, BLK), BF16), pltpu.VMEM((2 * cap_h * BLK, BLK), BF16)],
        )[0]

    def multiply(rows_of_g):
        return call(
            first_kernel, [], [joined, rows_of_g], [shape(wide, side)], flops=2 * side * order * wide
        )[0]

    middle, outward = [(1, 2), (2, 1)], [(1, 0), (2, 3)]
    inner = (z == 1) | (z == 2)
    beside, over, own_y = swap_row(own, 2), along(own, middle), swap_col(own, 2)

    own, beside, over, own_y = after((over, own_y), own, beside, over, own_y)
    over_beside, out_near = along(beside, middle), along(over, outward)
    beside_y, own_core, own_y_core = swap_col(beside, 2), swap_col(own, 1), swap_col(own_y, 1)
    (joined,) = call(
        functools.partial(unpack_kernel, cap, zs, kb, jb),
        [info, pmask],
        [piece for pair in zip(mine, theirs) for piece in pair],
        [shape(wide, order)],
    )

    done = (out_near, beside_y, own_core, own_y_core, joined)
    beside, over, over_beside, out_near, beside_y = after(
        done, beside, over, over_beside, out_near, beside_y
    )
    slot_2 = jnp.where(inner, over_beside, out_near)
    out_far, slot_2_y = along(over_beside, outward), swap_col(slot_2, 2)
    beside_core, beside_y_core = swap_col(beside, 1), swap_col(beside_y, 1)
    dense, first, first_x = [None] * zs, [None] * zs, [None] * zs
    dense[0] = spread(0, own, own_y, own_core, own_y_core)
    first[0] = multiply(dense[0])
    first_x[0] = swap_row(first[0], 1)
    dense[1] = spread(1, beside, beside_y, beside_core, beside_y_core)
    first[1] = multiply(dense[1])

    done = (out_far, slot_2_y, first[1], first_x[0])
    over, out_far, slot_2, slot_2_y = after(done, over, out_far, slot_2, slot_2_y)
    slot_3 = jnp.where(inner, over, out_far)
    slot_3_y = swap_col(slot_3, 2)
    slot_2_core, slot_2_y_core, slot_3_core = swap_col(slot_2, 1), swap_col(slot_2_y, 1), swap_col(slot_3, 1)
    first_x[1] = swap_row(first[1], 1)
    dense[2] = spread(2, slot_2, slot_2_y, slot_2_core, slot_2_y_core)
    first[2] = multiply(dense[2])
    first_x[2] = swap_row(first[2], 1)

    (slot_3_y,) = after((slot_3_core, first_x[1], first_x[2]), slot_3_y)
    slot_3_y_core = swap_col(slot_3_y, 1)
    dense[3] = spread(3, slot_3, slot_3_y, slot_3_core, slot_3_y_core)
    first[3] = multiply(dense[3])
    first_x[3] = swap_row(first[3], 1)
    (first_joined,) = call(
        functools.partial(join_kernel, zs, side),
        [info],
        [f for pair in zip(first, first_x) for f in pair],
        [shape(wide, order)],
    )

    result = [None] * zs
    for slots in ((3,), (2,), (1,), (0,)):
        outs = call(
            functools.partial(second_kernel, slots, cap, zs, kb, jb),
            [info, pmask],
            [first_joined, *(dense[s] for s in slots), *(first[s] for s in slots)],
            [piece] * len(slots),
            scratch=[
                pltpu.VMEM((len(slots), wide, side), BF16),
                pltpu.VMEM((len(slots), 2 * (kb * jb + 1) * BLK // zs, BLK), BF16),
            ],
            flops=2 * side * order * wide * len(slots),
            weight=1 if slots[0] else 32,
        )
        for s, out in zip(slots, outs):
            result[s] = out if s == 0 else swap_row(out, 2 * s)

    return call(
        functools.partial(return_kernel, cap, zs, kb, jb),
        [info, pmask],
        [density, *result],
        [shape(2, side, across)],
        scratch=[pltpu.VMEM((2 * cap * BLK, BLK), BF16)],
    )[0]


def shards(potential, basis, hamiltonian, density, hmask, pmask):
    side, across = hamiltonian.shape
    kb, jb = side // BLK, across // BLK

    def most(mask, width):
        return mask.reshape(mask.shape[0] // kb, kb, mask.shape[1] // width, width).sum((1, 3)).max()

    cap, cap_h = kb * jb - 2, kb * jb - 4
    arguments = (potential, basis, hamiltonian, density, hmask, pmask)
    result = step(cap, cap_h, *arguments)
    more = (most(pmask, jb) > cap) | (most(hmask, 2 * jb) > 2 * cap_h)
    return lax.while_loop(
        lambda state: state[0],
        lambda state: (jnp.array(False), step(kb * jb, kb * jb, *arguments)),
        (more, result),
    )[1]


def extended_2(block, sides, width):
    for axis, dim in sides:
        count = lax.axis_size(axis)
        forward = [(i, i + 1) for i in range(count - 1)]
        backward = [(target, source) for source, target in forward]
        low = lax.ppermute(
            lax.slice_in_dim(block, block.shape[dim] - width, None, axis=dim), axis, forward
        )
        high = lax.ppermute(lax.slice_in_dim(block, 0, width, axis=dim), axis, backward)
        block = jnp.concatenate([low, block, high], axis=dim)
    return block


def gathered(potential, basis, hamiltonian, density, hmask, pmask):
    width_x, width_y, depth_z = potential.shape
    extended = extended_2(potential, (("row", 0), ("col", 1)), 1)
    padded = jnp.pad(extended, ((0, 0), (0, 0), (1, 1)))
    beside = padded[2:, 1:-1, 1:-1] + padded[:-2, 1:-1, 1:-1]
    beside = beside + padded[1:-1, 2:, 1:-1] + padded[1:-1, :-2, 1:-1]
    beside = beside + padded[1:-1, 1:-1, 2:] + padded[1:-1, 1:-1, :-2]
    effective = potential + KAPPA * (beside - 6.0 * potential)
    blocks_here = basis.shape[2] // BLK
    weighted = (basis * effective[:, :, None, :]).astype(BF16)
    partial_blocks = jnp.einsum(
        "xykaz,xykbz->kab",
        weighted.reshape(width_x, width_y, blocks_here, BLK, depth_z),
        basis.reshape(width_x, width_y, blocks_here, BLK, depth_z),
        preferred_element_type=F32,
    )
    summed = lax.psum(partial_blocks, "col")
    factor = float(BLK * width_x * width_y * depth_z * lax.axis_size("col")) ** (-0.5)
    potential_blocks = (summed * factor).astype(BF16)
    block_total = hmask.shape[0]
    blocks_wide = block_total // lax.axis_size("col")
    row_start = lax.axis_index("row") * blocks_here
    col_start = lax.axis_index("col") * blocks_wide
    hpattern = lax.dynamic_slice(hmask, (row_start, col_start), (blocks_here, blocks_wide))
    ppattern = lax.dynamic_slice(pmask, (row_start, col_start), (blocks_here, blocks_wide))
    masked_h = (
        hamiltonian.reshape(blocks_here, BLK, blocks_wide, BLK)
        * hpattern[:, None, :, None].astype(BF16)
    ).reshape(blocks_here * BLK, blocks_wide * BLK)
    masked_p = (
        density.reshape(2, blocks_here, BLK, blocks_wide, BLK)
        * ppattern[None, :, None, :, None].astype(BF16)
    ).reshape(2, blocks_here * BLK, blocks_wide * BLK)

    def diagonal_term(operand):
        local = jnp.einsum(
            "kab,skbc->skac",
            potential_blocks,
            operand.reshape(2, blocks_here, BLK, operand.shape[2]),
            preferred_element_type=F32,
        )
        return local.reshape(2, blocks_here * BLK, operand.shape[2])

    def apply(operand):
        column_whole = lax.all_gather(operand, "row", axis=1, tiled=True)
        remote = jnp.einsum(
            "rk,skc->src",
            lax.all_gather(masked_h, "col", axis=1, tiled=True),
            column_whole,
            preferred_element_type=F32,
        )
        return remote + diagonal_term(operand)

    first = apply(masked_p)
    first_rounded = first.astype(BF16)
    second = apply(first_rounded)
    base = masked_p.astype(F32)
    half_square = 0.5 * TIME_STEP * TIME_STEP
    real_part = base[0] + TIME_STEP * first[1] - half_square * second[0]
    imag_part = base[1] - TIME_STEP * first[0] - half_square * second[1]
    stacked = jnp.stack([real_part, imag_part]).reshape(2, blocks_here, BLK, blocks_wide, BLK)
    stacked = stacked * ppattern[None, :, None, :, None].astype(F32)
    return stacked.reshape(2, blocks_here * BLK, blocks_wide * BLK).astype(BF16)


def solution(mesh):
    in_specs = (
        P("row", "col", None),
        P("row", "col", None, None),
        P("row", "col"),
        P(None, "row", "col"),
        P(),
        P(),
    )
    out_specs = P(None, "row", "col")
    body = shards if (mesh.shape["row"], mesh.shape["col"]) == (8, 4) else gathered
    return jax.shard_map(body, mesh=mesh, in_specs=in_specs, out_specs=out_specs, check_vma=False)
```

time: 395 us -> 179 us (0.45)
  waiting for transfers between devices: 332 us -> 73.6 us
  starting transfers between devices: 10.6 us -> 50.7 us
  Pallas kernels: 0 us -> 34.1 us
  matrix products: 23.1 us -> 0 us
  between operations: 13.3 us -> 1.88 us
  local copies, waits for them, and re-layouts: 7.56 us -> 13.7 us
  other arithmetic: 8.46 us -> 4.04 us
    all_gather x3 -> x0, waiting for transfers between devices: 296 us -> none  [the longest x2 273 us: apply(): column_whole = lax.all_gather(operand, 'row', axis=1, tiled=True)]
    ppermute x4 -> x38, waiting for transfers between devices: 3.52 us -> 73.6 us  [the longest x15 64.9 us: swap_row(): return lax.ppermute(value, 'row', [(i, i ^ bits) for i in range(count)])]
    ppermute x4 -> x38, starting transfers between devices: 10.4 us -> 50.7 us  [the longest x15 23.9 us: swap_row(): return lax.ppermute(value, 'row', [(i, i ^ bits) for i in range(count)])]
    pallas_call x0 -> x18, Pallas kernels: none -> 34.1 us  [call(): pl.pallas_call(body, out_shape=tuple(outs), in_specs=[SMEM_SPEC] * len(sc...]
    psum x1 -> x0, waiting for transfers between devices: 31.7 us -> none  [shards(): summed = lax.psum(partial_blocks, 'col')]
    dot_general x5 -> x0, matrix products: 23.1 us -> none  [the longest x2 19.6 us: apply(): jnp.einsum('rk,skc->src', lax.all_gather(masked_h, 'col', axis=1, tiled=T...]
    unnamed x20 -> x44, local copies, waits for them, and re-layouts: 3.25 us -> 11.2 us
    convert_element_type x4 -> x1, other arithmetic: 6.02 us -> 0.01 us  [potential_blocks(): return (total * factor).astype(BF16)]
  transfers between devices with their start and end apart: 8 -> 38, of which waited for: 5 -> 18; matrix products, arithmetic and copies ran while one was open for 3% -> 3% of each run, Pallas kernels for 0% -> 9%
where the time goes in v2:
time: 179 us; the launch traced here: 178 us
  waiting for transfers between devices  73.6 us (41%)
  starting transfers between devices  50.7 us (28%)
  Pallas kernels  34.1 us (19%)
  local copies, waits for them, and re-layouts  13.7 us (8%)
  other arithmetic  4.04 us (2%)
  between operations  1.88 us (1%)
    ppermute x15, waiting for transfers between devices, swap_row(): return lax.ppermute(value, 'row', [(i, i ^ bits) for i in range(count)])  64.9 us
    pallas_call x18, Pallas kernels, call(): pl.pallas_call(body, out_shape=tuple(outs), in_specs=[SMEM_SPEC] * len(sc...  34.1 us
    ppermute x15, starting transfers between devices, swap_row(): return lax.ppermute(value, 'row', [(i, i ^ bits) for i in range(count)])  23.9 us
    unnamed x44, local copies, waits for them, and re-layouts  11.2 us
    ppermute x15, starting transfers between devices, swap_col(): return lax.ppermute(value, 'col', [(i, i ^ bits) for i in range(count)])  10.2 us
    ppermute x2, starting transfers between devices, beyond(): lax.ppermute(lax.slice_in_dim(potential, last, None, axis=dim), axis, for...  8.34 us
    ppermute x15, waiting for transfers between devices, swap_col(): return lax.ppermute(value, 'col', [(i, i ^ bits) for i in range(count)])  6.71 us
    ppermute x4, starting transfers between devices, along(): lax.ppermute(value, 'row', [(2 * a + x, 2 * b + x) for a, b in pairs for...  5.72 us
  transfers between devices with their start and end apart: 38, of which 18 were waited for; matrix products, arithmetic and copies ran while one was open for 3% of the time, Pallas kernels for 9%

profile of v2, /device:TPU:0, one launch (start us, length us, event | category | flops | bytes accessed | tf_op | source)
XLA Modules:
  0.0 178.0 jit_solution(16070746828359782139)
XLA Ops:
  0.5 1.8 shard_map.64
  4.4 5.3 %collective-permute-start.47 = (f32[1,4,512]{2,1,0:T(4,128)S(1)}, f32[1,4,512]{2,1,0:T(4,128)S(1)}, u32[]{:S(2)}, u32[]{:S(2)}) collective-permute-start(f32[1,4,512]{2,1,0:T(4,128)S(1)} %get-tuple-element.130), channel_id=1, source_target_pairs={{0,4},{4,8},{8,12},{12,16},{16,20},{20,24},{24,28},{1,5},{5,9},{9,... | collective-permute-start | bytes 24584 | tf_op jit(solution)/shard_map/ppermute | solution.py:199
  10.5 1.3 collective-permute-start.48
  11.8 3.0 %collective-permute-start.49 = (f32[2,1,512]{2,1,0:T(1,128)S(1)}, f32[2,1,512]{2,1,0:T(1,128)S(1)}, u32[]{:S(2)}, u32[]{:S(2)}) collective-permute-start(f32[2,1,512]{2,1,0:T(1,128)S(1)} %get-tuple-element.132), channel_id=1, source_target_pairs={{0,1},{1,2},{2,3},{4,5},{5,6},{6,7},{8,9},{9,10},{10,11},{12,13},{... | collective-permute-start | bytes 12296 | tf_op jit(solution)/shard_map/ppermute | solution.py:199
  16.7 2.9 %shard_map.66 = f32[384,128]{1,0:T(8,128)S(1)} custom-call(f32[2,4,512]{2,1,0:T(4,128)S(1)} %fusion.12.effective, bf16[2,4,384,512]{3,2,1,0:T(8,128)(2,1)} %basis.1), custom_call_target="tpu_custom_call" | custom-call | flops 402653184 | bytes 107479040 | tf_op jit(solution)/shard_map/pallas_call | solution.py:24
  19.6 1.7 collective-permute-start.50
  22.3 2.6 %collective-permute-start.51 = (f32[96,128]{1,0:T(8,128)S(1)}, f32[96,128]{1,0:T(8,128)S(1)}, u32[]{:S(2)}, u32[]{:S(2)}) collective-permute-start(f32[96,128]{1,0:T(8,128)S(1)} %slice_select_fusion.3), channel_id=1, source_target_pairs={{0,2},{1,3},{2,0},{3,1},{4,6},{5,7},{6,4},{7,5},{8,10},{9,11},{10,... | collective-permute-start | bytes 147464 | tf_op jit(solution)/shard_map/ppermute | solution.py:182
  24.8 1.6 collective-permute-start.39
  26.4 2.6 %collective-permute-start.41 = (bf16[1024,128]{1,0:T(8,128)(2,1)S(1)}, bf16[1024,128]{1,0:T(8,128)(2,1)S(1)}, u32[]{:S(2)}, u32[]{:S(2)}) collective-permute-start(bf16[1024,128]{1,0:T(8,128)(2,1)S(1)} %get-tuple-element.89), channel_id=1, source_target_pairs={{0,16},{4,20},{8,24},{12,28},{16,0},{20,4},{24,8},{28,12},{1,17},{... | collective-permute-start | bytes 786440 | tf_op jit(solution)/shard_map/ppermute | solution.py:177
  29.2 8.5 %collective-permute-done.39.rest_2_ = bf16[1024,128]{1,0:T(8,128)(2,1)S(1)} collective-permute-done((bf16[1024,128]{1,0:T(8,128)(2,1)S(1)}, bf16[1024,128]{1,0:T(8,128)(2,1)S(1)}, u32[]{:S(2)}, u32[]{:S(2)}) %collective-permute-start.39) | collective-permute-done | bytes 262176 | tf_op jit(solution)/shard_map/ppermute | solution.py:177
  37.8 10.0 %collective-permute-done.41.rest_4_ = bf16[1024,128]{1,0:T(8,128)(2,1)S(1)} collective-permute-done((bf16[1024,128]{1,0:T(8,128)(2,1)S(1)}, bf16[1024,128]{1,0:T(8,128)(2,1)S(1)}, u32[]{:S(2)}, u32[]{:S(2)}) %collective-permute-start.41) | collective-permute-done | bytes 262176 | tf_op jit(solution)/shard_map/ppermute | solution.py:177
  49.1 4.9 %collective-permute-start.52 = (bf16[1888,128]{1,0:T(8,128)(2,1)S(1)}, bf16[1888,128]{1,0:T(8,128)(2,1)S(1)}, u32[]{:S(2)}, u32[]{:S(2)}) collective-permute-start(bf16[1888,128]{1,0:T(8,128)(2,1)S(1)} %shard_map.67.rest_0_), channel_id=1, source_target_pairs={{0,8},{4,12},{8,0},{12,4},{16,24},{20,28},{24,16},{28,20},{1,9},{5... | collective-permute-start | bytes 1449992 | tf_op jit(solution)/shard_map/ppermute | solution.py:177
  53.9 1.4 collective-permute-start.53
  55.7 2.4 %collective-permute-start.38 = (bf16[1024,128]{1,0:T(8,128)(2,1)S(1)}, bf16[1024,128]{1,0:T(8,128)(2,1)S(1)}, u32[]{:S(2)}, u32[]{:S(2)}) collective-permute-start(bf16[1024,128]{1,0:T(8,128)(2,1)S(1)} %get-tuple-element.87.rest_0_), channel_id=1, source_target_pairs={{0,4},{4,0},{8,12},{12,8},{16,20},{20,16},{24,28},{28,24},{1,5},{5... | collective-permute-start | bytes 786440 | tf_op jit(solution)/shard_map/ppermute | solution.py:177
  58.1 5.7 %collective-permute-done.52.rest_0_ = bf16[1888,128]{1,0:T(8,128)(2,1)S(1)} collective-permute-done((bf16[1888,128]{1,0:T(8,128)(2,1)S(1)}, bf16[1888,128]{1,0:T(8,128)(2,1)S(1)}, u32[]{:S(2)}, u32[]{:S(2)}) %collective-permute-start.52) | collective-permute-done | bytes 483360 | tf_op jit(solution)/shard_map/ppermute | solution.py:177
  63.9 2.4 %collective-permute-start.42 = (bf16[1024,128]{1,0:T(8,128)(2,1)S(1)}, bf16[1024,128]{1,0:T(8,128)(2,1)S(1)}, u32[]{:S(2)}, u32[]{:S(2)}) collective-permute-start(bf16[1024,128]{1,0:T(8,128)(2,1)S(1)} %collective-permute-done.41.rest_4_), channel_id=1, source_target_pairs={{0,4},{4,0},{8,12},{12,8},{16,20},{20,16},{24,28},{28,24},{1,5},{5... | collective-permute-start | bytes 786440 | tf_op jit(solution)/shard_map/ppermute | solution.py:177
  68.0 3.0 %collective-permute-done.40.rest_3_ = bf16[1024,128]{1,0:T(8,128)(2,1)S(1)} collective-permute-done((bf16[1024,128]{1,0:T(8,128)(2,1)S(1)}, bf16[1024,128]{1,0:T(8,128)(2,1)S(1)}, u32[]{:S(2)}, u32[]{:S(2)}) %collective-permute-start.40) | collective-permute-done | bytes 262176 | tf_op jit(solution)/shard_map/ppermute | solution.py:177
  71.7 1.4 collective-permute-start.58
  73.1 3.5 %collective-permute-done.42.rest_5_ = bf16[1024,128]{1,0:T(8,128)(2,1)S(1)} collective-permute-done((bf16[1024,128]{1,0:T(8,128)(2,1)S(1)}, bf16[1024,128]{1,0:T(8,128)(2,1)S(1)}, u32[]{:S(2)}, u32[]{:S(2)}) %collective-permute-start.42) | collective-permute-done | bytes 262176 | tf_op jit(solution)/shard_map/ppermute | solution.py:177
  78.6 1.3 collective-permute-done.44.rest_7_
  80.6 1.3 collective-permute-start.60
  88.7 1.9 %shard_map.65.joined = bf16[384,3072]{1,0:T(8,128)(2,1)S(1)} custom-call(s32[2]{0:T(128)S(1)} %pad_add_fusion.1.info, s32[24,24]{1,0:T(8,128)S(1)} %copy-done.32, bf16[1024,128]{1,0:T(8,128)(2,1)S(1)} %get-tuple-element.87.rest_0_, bf16[1024,128]{1,0:T(8,128)(2,1)S(1)} %copy-done.25, bf16[1024,128]{1,0:T(8,128)(2,1)S(1)} %copy-done.19, ...), custom_call_target="tpu_custom_call" | custom-call | bytes 4456448 | tf_op jit(solution)/shard_map/pallas_call | solution.py:24
  94.1 1.6 collective-permute-start.64
  95.7 1.8 %shard_map.68.dense.rest_0_ = bf16[384,3072]{1,0:T(8,128)(2,1)S(1)} custom-call(s32[2]{0:T(128)S(1)} %pad_add_fusion.1.info, s32[24,24]{1,0:T(8,128)} %hmask.9, bf16[1888,128]{1,0:T(8,128)(2,1)S(1)} %shard_map.67.rest_0_, bf16[1888,128]{1,0:T(8,128)(2,1)S(1)} %collective-permute-done.55.rest_1_, bf16[1888,128]{1,0:T(8,128)(2,1)S(1)} %collective-permute-done.54.rest_2_, ...), custom_call_target="tpu_custom_call" | custom-call | bytes 4292608 | tf_op jit(solution)/shard_map/pallas_call | solution.py:24
  97.6 1.4 shard_map.69.rest_0_.rest_1_
  99.0 1.5 collective-permute-start.57
  100.5 1.8 %shard_map.70.dense.rest_0_ = bf16[384,3072]{1,0:T(8,128)(2,1)S(1)} custom-call(s32[2]{0:T(128)S(1)} %pad_add_fusion.1.info, s32[24,24]{1,0:T(8,128)} %hmask.9, bf16[1888,128]{1,0:T(8,128)(2,1)S(1)} %collective-permute-done.52.rest_0_, bf16[1888,128]{1,0:T(8,128)(2,1)S(1)} %collective-permute-done.61.rest_1_, ...), custom_call_target="tpu_custom_call" | custom-call | bytes 4292608 | tf_op jit(solution)/shard_map/pallas_call | solution.py:24
  102.4 1.4 shard_map.71.rest_2_.rest_1_
  103.8 3.9 %collective-permute-done.57.rest_1_ = bf16[384,384]{1,0:T(8,128)(2,1)S(1)} collective-permute-done((bf16[384,384]{1,0:T(8,128)(2,1)S(1)}, bf16[384,384]{1,0:T(8,128)(2,1)S(1)}, u32[]{:S(2)}, u32[]{:S(2)}) %collective-permute-start.57) | collective-permute-done | bytes 294944 | tf_op jit(solution)/shard_map/ppermute | solution.py:177
  110.6 1.5 collective-permute-start.63
  112.1 1.8 %shard_map.72.dense.rest_0_ = bf16[384,3072]{1,0:T(8,128)(2,1)S(1)} custom-call(s32[2]{0:T(128)S(1)} %pad_add_fusion.1.info, s32[24,24]{1,0:T(8,128)} %hmask.9, bf16[1888,128]{1,0:T(8,128)(2,1)S(1)} %broadcast_select_fusion.3.rest_0_, bf16[1888,128]{1,0:T(8,128)(2,1)S(1)} %collective-permute-done.66.rest_1_, ...), custom_call_target="tpu_custom_call" | custom-call | bytes 4292608 | tf_op jit(solution)/shard_map/pallas_call | solution.py:24
  113.9 1.4 shard_map.73.rest_4_.rest_1_
  116.2 4.2 %collective-permute-done.63.rest_3_ = bf16[384,384]{1,0:T(8,128)(2,1)S(1)} collective-permute-done((bf16[384,384]{1,0:T(8,128)(2,1)S(1)}, bf16[384,384]{1,0:T(8,128)(2,1)S(1)}, u32[]{:S(2)}, u32[]{:S(2)}) %collective-permute-start.63) | collective-permute-done | bytes 294944 | tf_op jit(solution)/shard_map/ppermute | solution.py:177
  120.5 2.5 %collective-permute-done.70.rest_2_ = bf16[1888,128]{1,0:T(8,128)(2,1)S(1)} collective-permute-done((bf16[1888,128]{1,0:T(8,128)(2,1)S(1)}, bf16[1888,128]{1,0:T(8,128)(2,1)S(1)}, u32[]{:S(2)}, u32[]{:S(2)}) %collective-permute-start.70) | collective-permute-done | bytes 483360 | tf_op jit(solution)/shard_map/ppermute | solution.py:182
  123.0 3.0 %collective-permute-done.68.rest_5_ = bf16[384,384]{1,0:T(8,128)(2,1)S(1)} collective-permute-done((bf16[384,384]{1,0:T(8,128)(2,1)S(1)}, bf16[384,384]{1,0:T(8,128)(2,1)S(1)}, u32[]{:S(2)}, u32[]{:S(2)}) %collective-permute-start.68) | collective-permute-done | bytes 294944 | tf_op jit(solution)/shard_map/ppermute | solution.py:177
  126.0 1.8 %collective-permute-done.71.rest_3_ = bf16[1888,128]{1,0:T(8,128)(2,1)S(1)} collective-permute-done((bf16[1888,128]{1,0:T(8,128)(2,1)S(1)}, bf16[1888,128]{1,0:T(8,128)(2,1)S(1)}, u32[]{:S(2)}, u32[]{:S(2)}) %collective-permute-start.71) | collective-permute-done | bytes 483360 | tf_op jit(solution)/shard_map/ppermute | solution.py:182
  127.9 1.8 %shard_map.74.dense.rest_0_ = bf16[384,3072]{1,0:T(8,128)(2,1)S(1)} custom-call(s32[2]{0:T(128)S(1)} %pad_add_fusion.1.info, s32[24,24]{1,0:T(8,128)} %hmask.9, bf16[1888,128]{1,0:T(8,128)(2,1)S(1)} %broadcast_select_fusion.2.rest_0_, bf16[1888,128]{1,0:T(8,128)(2,1)S(1)} %collective-permute-done.69.rest_1_, ...), custom_call_target="tpu_custom_call" | custom-call | bytes 4292608 | tf_op jit(solution)/shard_map/pallas_call | solution.py:24
  129.7 1.4 shard_map.75.rest_6_.rest_1_
  131.1 1.5 collective-permute-start.72
  132.7 7.6 %collective-permute-done.72.rest_7_ = bf16[384,384]{1,0:T(8,128)(2,1)S(1)} collective-permute-done((bf16[384,384]{1,0:T(8,128)(2,1)S(1)}, bf16[384,384]{1,0:T(8,128)(2,1)S(1)}, u32[]{:S(2)}, u32[]{:S(2)}) %collective-permute-start.72) | collective-permute-done | bytes 294944 | tf_op jit(solution)/shard_map/ppermute | solution.py:177
  141.0 2.9 %shard_map.80 = bf16[1024,128]{1,0:T(8,128)(2,1)} custom-call(s32[2]{0:T(128)S(1)} %pad_add_fusion.1.info, s32[24,24]{1,0:T(8,128)S(1)} %copy-done.32, bf16[384,3072]{1,0:T(8,128)(2,1)S(1)} %shard_map.76.joined, bf16[384,3072]{1,0:T(8,128)(2,1)S(1)} %copy-done.7, bf16[384,384]{1,0:T(8,128)(2,1)S(1)} %shard_map.75.rest_6_.rest_1_), custom_call_target="tpu_custom_call" | custom-call | flops 905969664 | bytes 5275648 | tf_op jit(solution)/shard_map/pallas_call | solution.py:24
  144.0 2.2 %shard_map.79 = bf16[1024,128]{1,0:T(8,128)(2,1)S(1)} custom-call(s32[2]{0:T(128)S(1)} %pad_add_fusion.1.info, s32[24,24]{1,0:T(8,128)S(1)} %copy-done.32, bf16[384,3072]{1,0:T(8,128)(2,1)S(1)} %shard_map.76.joined, bf16[384,3072]{1,0:T(8,128)(2,1)S(1)} %shard_map.72.dense.rest_0_, bf16[384,384]{1,0:T(8,128)(2,1)S(1)} %shard_map.73.rest_4_.rest_1_), custom_call_target="tpu_custom_call" | custom-call | flops 905969664 | bytes 5275648 | tf_op jit(solution)/shard_map/pallas_call | solution.py:24
  146.2 2.2 %shard_map.78 = bf16[1024,128]{1,0:T(8,128)(2,1)S(1)} custom-call(s32[2]{0:T(128)S(1)} %pad_add_fusion.1.info, s32[24,24]{1,0:T(8,128)S(1)} %copy-done.32, bf16[384,3072]{1,0:T(8,128)(2,1)S(1)} %shard_map.76.joined, bf16[384,3072]{1,0:T(8,128)(2,1)S(1)} %shard_map.70.dense.rest_0_, bf16[384,384]{1,0:T(8,128)(2,1)S(1)} %shard_map.71.rest_2_.rest_1_), custom_call_target="tpu_custom_call" | custom-call | flops 905969664 | bytes 5275648 | tf_op jit(solution)/shard_map/pallas_call | solution.py:24
  148.4 2.5 %collective-permute-start.75 = (bf16[1024,128]{1,0:T(8,128)(2,1)}, bf16[1024,128]{1,0:T(8,128)(2,1)S(1)}, u32[]{:S(2)}, u32[]{:S(2)}) collective-permute-start(bf16[1024,128]{1,0:T(8,128)(2,1)} %shard_map.80), channel_id=1, source_target_pairs={{0,24},{4,28},{8,16},{12,20},{16,8},{20,12},{24,0},{28,4},{1,25},{... | collective-permute-start | bytes 786440 | tf_op jit(solution)/shard_map/ppermute | solution.py:177
  156.8 1.7 copy-done.5
  158.5 2.2 %shard_map.77.rest_0_ = bf16[1024,128]{1,0:T(8,128)(2,1)S(1)} custom-call(s32[2]{0:T(128)S(1)} %pad_add_fusion.1.info, s32[24,24]{1,0:T(8,128)S(1)} %copy-done.32, bf16[384,3072]{1,0:T(8,128)(2,1)S(1)} %shard_map.76.joined, bf16[384,3072]{1,0:T(8,128)(2,1)S(1)} %copy-done.5, bf16[384,384]{1,0:T(8,128)(2,1)S(1)} %shard_map.69.rest_0_.rest_1_), custom_call_target="tpu_custom_call" | custom-call | flops 905969664 | bytes 168820736 | tf_op jit(solution)/shard_map/pallas_call | solution.py:24
  160.7 14.1 %collective-permute-done.74.rest_2_ = bf16[1024,128]{1,0:T(8,128)(2,1)} collective-permute-done((bf16[1024,128]{1,0:T(8,128)(2,1)S(1)}, bf16[1024,128]{1,0:T(8,128)(2,1)}, u32[]{:S(2)}, u32[]{:S(2)}) %collective-permute-start.74) | collective-permute-done | bytes 262176 | tf_op jit(solution)/shard_map/ppermute | solution.py:177
  174.8 3.0 %shard_map.81 = bf16[2,384,768]{2,1,0:T(8,128)(2,1)} custom-call(s32[2]{0:T(128)S(1)} %pad_add_fusion.1.info, s32[24,24]{1,0:T(8,128)S(1)} %copy-done.32, bf16[2,384,768]{2,1,0:T(8,128)(2,1)} %p.3, bf16[1024,128]{1,0:T(8,128)(2,1)S(1)} %shard_map.77.rest_0_, bf16[1024,128]{1,0:T(8,128)(2,1)} %collective-permute-done.73.rest_1_, ...), custom_call_target="tpu_custom_call" | custom-call | bytes 3407872 | tf_op jit(solution)/shard_map/pallas_call | solution.py:24
  (107 shorter events, 32.6 us)
Async XLA Ops:
  0.0 2.3 %collective-permute-start.45 = (bf16[384,768]{1,0:T(8,128)(2,1)}, bf16[384,768]{1,0:T(8,128)(2,1)S(1)}, u32[]{:S(2)}, u32[]{:S(2)}) collective-permute-start(bf16[384,768]{1,0:T(8,128)(2,1)} %h), channel_id=1, source_target_pairs={{0,1},{1,0},{2,3},{3,2},{4,5},{5,4},{6,7},{7,6},{8,9},{9,8},{10,11... | collective-permute-start | bytes 1769480 | tf_op jit(solution)/shard_map/ppermute | solution.py:182
  2.3 45.5 %copy-start.33 = (bf16[384,768]{1,0:T(8,128)(2,1)S(1)}, bf16[384,768]{1,0:T(8,128)(2,1)}, u32[]{:S(2)}) copy-start(bf16[384,768]{1,0:T(8,128)(2,1)} %h) | copy-start | bytes 1769476
  3.1 12.6 %collective-permute-start.46 = (f32[1,4,512]{2,1,0:T(4,128)S(1)}, f32[1,4,512]{2,1,0:T(4,128)S(1)}, u32[]{:S(2)}, u32[]{:S(2)}) collective-permute-start(f32[1,4,512]{2,1,0:T(4,128)S(1)} %get-tuple-element.129), channel_id=1, source_target_pairs={{4,0},{8,4},{12,8},{16,12},{20,16},{24,20},{28,24},{5,1},{9,5},{13... | collective-permute-start | bytes 24584 | tf_op jit(solution)/shard_map/ppermute | solution.py:200
  4.4 11.3 %collective-permute-start.47 = (f32[1,4,512]{2,1,0:T(4,128)S(1)}, f32[1,4,512]{2,1,0:T(4,128)S(1)}, u32[]{:S(2)}, u32[]{:S(2)}) collective-permute-start(f32[1,4,512]{2,1,0:T(4,128)S(1)} %get-tuple-element.130), channel_id=1, source_target_pairs={{0,4},{4,8},{8,12},{12,16},{16,20},{20,24},{24,28},{1,5},{5,9},{9,... | collective-permute-start | bytes 24584 | tf_op jit(solution)/shard_map/ppermute | solution.py:199
  10.5 4.4 %collective-permute-start.48 = (f32[2,1,512]{2,1,0:T(1,128)S(1)}, f32[2,1,512]{2,1,0:T(1,128)S(1)}, u32[]{:S(2)}, u32[]{:S(2)}) collective-permute-start(f32[2,1,512]{2,1,0:T(1,128)S(1)} %get-tuple-element.131), channel_id=1, source_target_pairs={{1,0},{2,1},{3,2},{5,4},{6,5},{7,6},{9,8},{10,9},{11,10},{13,12},{... | collective-permute-start | bytes 12296 | tf_op jit(solution)/shard_map/ppermute | solution.py:200
  11.8 3.8 %collective-permute-start.49 = (f32[2,1,512]{2,1,0:T(1,128)S(1)}, f32[2,1,512]{2,1,0:T(1,128)S(1)}, u32[]{:S(2)}, u32[]{:S(2)}) collective-permute-start(f32[2,1,512]{2,1,0:T(1,128)S(1)} %get-tuple-element.132), channel_id=1, source_target_pairs={{0,1},{1,2},{2,3},{4,5},{5,6},{6,7},{8,9},{9,10},{10,11},{12,13},{... | collective-permute-start | bytes 12296 | tf_op jit(solution)/shard_map/ppermute | solution.py:199
  16.7 65.3 %copy-start.32 = (s32[24,24]{1,0:T(8,128)S(1)}, s32[24,24]{1,0:T(8,128)}, u32[]{:S(2)}) copy-start(s32[24,24]{1,0:T(8,128)} %pmask.13) | copy-start | bytes 6916
  19.6 2.6 %collective-permute-start.50 = (f32[192,128]{1,0:T(8,128)S(1)}, f32[192,128]{1,0:T(8,128)S(1)}, u32[]{:S(2)}, u32[]{:S(2)}) collective-permute-start(f32[192,128]{1,0:T(8,128)S(1)} %slice_select_fusion.2), channel_id=1, source_target_pairs={{0,1},{1,0},{2,3},{3,2},{4,5},{5,4},{6,7},{7,6},{8,9},{9,8},{10,11... | collective-permute-start | bytes 294920 | tf_op jit(solution)/shard_map/ppermute | solution.py:182
  22.3 7.0 %collective-permute-start.51 = (f32[96,128]{1,0:T(8,128)S(1)}, f32[96,128]{1,0:T(8,128)S(1)}, u32[]{:S(2)}, u32[]{:S(2)}) collective-permute-start(f32[96,128]{1,0:T(8,128)S(1)} %slice_select_fusion.3), channel_id=1, source_target_pairs={{0,2},{1,3},{2,0},{3,1},{4,6},{5,7},{6,4},{7,5},{8,10},{9,11},{10,... | collective-permute-start | bytes 147464 | tf_op jit(solution)/shard_map/ppermute | solution.py:182
  24.8 13.0 %collective-permute-start.39 = (bf16[1024,128]{1,0:T(8,128)(2,1)S(1)}, bf16[1024,128]{1,0:T(8,128)(2,1)S(1)}, u32[]{:S(2)}, u32[]{:S(2)}) collective-permute-start(bf16[1024,128]{1,0:T(8,128)(2,1)S(1)} %get-tuple-element.88), channel_id=1, source_target_pairs={{0,8},{4,12},{8,0},{12,4},{16,24},{20,28},{24,16},{28,20},{1,9},{5... | collective-permute-start | bytes 786440 | tf_op jit(solution)/shard_map/ppermute | solution.py:177
  26.4 21.4 %collective-permute-start.41 = (bf16[1024,128]{1,0:T(8,128)(2,1)S(1)}, bf16[1024,128]{1,0:T(8,128)(2,1)S(1)}, u32[]{:S(2)}, u32[]{:S(2)}) collective-permute-start(bf16[1024,128]{1,0:T(8,128)(2,1)S(1)} %get-tuple-element.89), channel_id=1, source_target_pairs={{0,16},{4,20},{8,24},{12,28},{16,0},{20,4},{24,8},{28,12},{1,17},{... | collective-permute-start | bytes 786440 | tf_op jit(solution)/shard_map/ppermute | solution.py:177
  29.0 18.8 %collective-permute-start.43 = (bf16[1024,128]{1,0:T(8,128)(2,1)S(1)}, bf16[1024,128]{1,0:T(8,128)(2,1)S(1)}, u32[]{:S(2)}, u32[]{:S(2)}) collective-permute-start(bf16[1024,128]{1,0:T(8,128)(2,1)S(1)} %get-tuple-element.90), channel_id=1, source_target_pairs={{0,24},{4,28},{8,16},{12,20},{16,8},{20,12},{24,0},{28,4},{1,25},{... | collective-permute-start | bytes 786440 | tf_op jit(solution)/shard_map/ppermute | solution.py:177
  37.8 40.8 %copy-start.18 = (bf16[1024,128]{1,0:T(8,128)(2,1)}, bf16[1024,128]{1,0:T(8,128)(2,1)S(1)}, u32[]{:S(2)}) copy-start(bf16[1024,128]{1,0:T(8,128)(2,1)S(1)} %collective-permute-done.39.rest_2_) | copy-start | bytes 786436
  47.8 32.1 %copy-start.20 = (bf16[1024,128]{1,0:T(8,128)(2,1)}, bf16[1024,128]{1,0:T(8,128)(2,1)S(1)}, u32[]{:S(2)}) copy-start(bf16[1024,128]{1,0:T(8,128)(2,1)S(1)} %collective-permute-done.41.rest_4_) | copy-start | bytes 786436
  47.8 30.8 %copy-start.22 = (bf16[1024,128]{1,0:T(8,128)(2,1)}, bf16[1024,128]{1,0:T(8,128)(2,1)S(1)}, u32[]{:S(2)}) copy-start(bf16[1024,128]{1,0:T(8,128)(2,1)S(1)} %collective-permute-done.43.rest_6_) | copy-start | bytes 786436
  49.1 14.8 %collective-permute-start.52 = (bf16[1888,128]{1,0:T(8,128)(2,1)S(1)}, bf16[1888,128]{1,0:T(8,128)(2,1)S(1)}, u32[]{:S(2)}, u32[]{:S(2)}) collective-permute-start(bf16[1888,128]{1,0:T(8,128)(2,1)S(1)} %shard_map.67.rest_0_), channel_id=1, source_target_pairs={{0,8},{4,12},{8,0},{12,4},{16,24},{20,28},{24,16},{28,20},{1,9},{5... | collective-permute-start | bytes 1449992 | tf_op jit(solution)/shard_map/ppermute | solution.py:177
  53.9 12.3 %collective-permute-start.53 = (bf16[1888,128]{1,0:T(8,128)(2,1)S(1)}, bf16[1888,128]{1,0:T(8,128)(2,1)}, u32[]{:S(2)}, u32[]{:S(2)}) collective-permute-start(bf16[1888,128]{1,0:T(8,128)(2,1)S(1)} %shard_map.67.rest_0_), channel_id=1, source_target_pairs={{8,16},{12,20},{16,8},{20,12},{9,17},{13,21},{17,9},{21,13},{10,18... | collective-permute-start | bytes 1449992 | tf_op jit(solution)/shard_map/ppermute | solution.py:186
  55.4 11.4 %collective-permute-start.54 = (bf16[1888,128]{1,0:T(8,128)(2,1)S(1)}, bf16[1888,128]{1,0:T(8,128)(2,1)S(1)}, u32[]{:S(2)}, u32[]{:S(2)}) collective-permute-start(bf16[1888,128]{1,0:T(8,128)(2,1)S(1)} %shard_map.67.rest_0_), channel_id=1, source_target_pairs={{0,2},{1,3},{2,0},{3,1},{4,6},{5,7},{6,4},{7,5},{8,10},{9,11},{10,... | collective-permute-start | bytes 1449992 | tf_op jit(solution)/shard_map/ppermute | solution.py:182
  55.7 11.1 %collective-permute-start.38 = (bf16[1024,128]{1,0:T(8,128)(2,1)S(1)}, bf16[1024,128]{1,0:T(8,128)(2,1)S(1)}, u32[]{:S(2)}, u32[]{:S(2)}) collective-permute-start(bf16[1024,128]{1,0:T(8,128)(2,1)S(1)} %get-tuple-element.87.rest_0_), channel_id=1, source_target_pairs={{0,4},{4,0},{8,12},{12,8},{16,20},{20,16},{24,28},{28,24},{1,5},{5... | collective-permute-start | bytes 786440 | tf_op jit(solution)/shard_map/ppermute | solution.py:177
  58.1 12.8 %collective-permute-start.40 = (bf16[1024,128]{1,0:T(8,128)(2,1)S(1)}, bf16[1024,128]{1,0:T(8,128)(2,1)S(1)}, u32[]{:S(2)}, u32[]{:S(2)}) collective-permute-start(bf16[1024,128]{1,0:T(8,128)(2,1)S(1)} %collective-permute-done.39.rest_2_), channel_id=1, source_target_pairs={{0,4},{4,0},{8,12},{12,8},{16,20},{20,16},{24,28},{28,24},{1,5},{5... | collective-permute-start | bytes 786440 | tf_op jit(solution)/shard_map/ppermute | solution.py:177
  63.9 12.7 %collective-permute-start.42 = (bf16[1024,128]{1,0:T(8,128)(2,1)S(1)}, bf16[1024,128]{1,0:T(8,128)(2,1)S(1)}, u32[]{:S(2)}, u32[]{:S(2)}) collective-permute-start(bf16[1024,128]{1,0:T(8,128)(2,1)S(1)} %collective-permute-done.41.rest_4_), channel_id=1, source_target_pairs={{0,4},{4,0},{8,12},{12,8},{16,20},{20,16},{24,28},{28,24},{1,5},{5... | collective-permute-start | bytes 786440 | tf_op jit(solution)/shard_map/ppermute | solution.py:177
  66.3 13.7 %collective-permute-start.44 = (bf16[1024,128]{1,0:T(8,128)(2,1)S(1)}, bf16[1024,128]{1,0:T(8,128)(2,1)S(1)}, u32[]{:S(2)}, u32[]{:S(2)}) collective-permute-start(bf16[1024,128]{1,0:T(8,128)(2,1)S(1)} %collective-permute-done.43.rest_6_), channel_id=1, source_target_pairs={{0,4},{4,0},{8,12},{12,8},{16,20},{20,16},{24,28},{28,24},{1,5},{5... | collective-permute-start | bytes 786440 | tf_op jit(solution)/shard_map/ppermute | solution.py:177
  66.8 23.8 %collective-permute-start.55 = (bf16[1888,128]{1,0:T(8,128)(2,1)S(1)}, bf16[1888,128]{1,0:T(8,128)(2,1)S(1)}, u32[]{:S(2)}, u32[]{:S(2)}) collective-permute-start(bf16[1888,128]{1,0:T(8,128)(2,1)S(1)} %shard_map.67.rest_0_), channel_id=1, source_target_pairs={{0,1},{1,0},{2,3},{3,2},{4,5},{5,4},{6,7},{7,6},{8,9},{9,8},{10,11... | collective-permute-start | bytes 1449992 | tf_op jit(solution)/shard_map/ppermute | solution.py:182
  67.5 23.1 %collective-permute-start.56 = (bf16[1888,128]{1,0:T(8,128)(2,1)S(1)}, bf16[1888,128]{1,0:T(8,128)(2,1)S(1)}, u32[]{:S(2)}, u32[]{:S(2)}) collective-permute-start(bf16[1888,128]{1,0:T(8,128)(2,1)S(1)} %collective-permute-done.54.rest_2_), channel_id=1, source_target_pairs={{0,1},{1,0},{2,3},{3,2},{4,5},{5,4},{6,7},{7,6},{8,9},{9,8},{10,11... | collective-permute-start | bytes 1449992 | tf_op jit(solution)/shard_map/ppermute | solution.py:182
  71.7 18.9 %collective-permute-start.58 = (bf16[1888,128]{1,0:T(8,128)(2,1)S(1)}, bf16[1888,128]{1,0:T(8,128)(2,1)}, u32[]{:S(2)}, u32[]{:S(2)}) collective-permute-start(bf16[1888,128]{1,0:T(8,128)(2,1)S(1)} %collective-permute-done.52.rest_0_), channel_id=1, source_target_pairs={{8,16},{12,20},{16,8},{20,12},{9,17},{13,21},{17,9},{21,13},{10,18... | collective-permute-start | bytes 1449992 | tf_op jit(solution)/shard_map/ppermute | solution.py:186
  77.3 13.3 %collective-permute-start.59 = (bf16[1888,128]{1,0:T(8,128)(2,1)}, bf16[1888,128]{1,0:T(8,128)(2,1)}, u32[]{:S(2)}, u32[]{:S(2)}) collective-permute-start(bf16[1888,128]{1,0:T(8,128)(2,1)} %collective-permute-done.53), channel_id=1, source_target_pairs={{8,0},{12,4},{16,24},{20,28},{9,1},{13,5},{17,25},{21,29},{10,2},{... | collective-permute-start | bytes 1449992 | tf_op jit(solution)/shard_map/ppermute | solution.py:186
  80.6 10.8 %collective-permute-start.60 = (bf16[1888,128]{1,0:T(8,128)(2,1)S(1)}, bf16[1888,128]{1,0:T(8,128)(2,1)S(1)}, u32[]{:S(2)}, u32[]{:S(2)}) collective-permute-start(bf16[1888,128]{1,0:T(8,128)(2,1)S(1)} %collective-permute-done.52.rest_0_), channel_id=1, source_target_pairs={{0,2},{1,3},{2,0},{3,1},{4,6},{5,7},{6,4},{7,5},{8,10},{9,11},{10,... | collective-permute-start | bytes 1449992 | tf_op jit(solution)/shard_map/ppermute | solution.py:182
  91.4 9.1 %collective-permute-start.61 = (bf16[1888,128]{1,0:T(8,128)(2,1)S(1)}, bf16[1888,128]{1,0:T(8,128)(2,1)S(1)}, u32[]{:S(2)}, u32[]{:S(2)}) collective-permute-start(bf16[1888,128]{1,0:T(8,128)(2,1)S(1)} %collective-permute-done.52.rest_0_), channel_id=1, source_target_pairs={{0,1},{1,0},{2,3},{3,2},{4,5},{5,4},{6,7},{7,6},{8,9},{9,8},{10,11... | collective-permute-start | bytes 1449992 | tf_op jit(solution)/shard_map/ppermute | solution.py:182
  91.4 9.1 %collective-permute-start.62 = (bf16[1888,128]{1,0:T(8,128)(2,1)S(1)}, bf16[1888,128]{1,0:T(8,128)(2,1)S(1)}, u32[]{:S(2)}, u32[]{:S(2)}) collective-permute-start(bf16[1888,128]{1,0:T(8,128)(2,1)S(1)} %collective-permute-done.60.rest_2_), channel_id=1, source_target_pairs={{0,1},{1,0},{2,3},{3,2},{4,5},{5,4},{6,7},{7,6},{8,9},{9,8},{10,11... | collective-permute-start | bytes 1449992 | tf_op jit(solution)/shard_map/ppermute | solution.py:182
  93.0 14.7 %collective-permute-start.65 = (bf16[1888,128]{1,0:T(8,128)(2,1)S(1)}, bf16[1888,128]{1,0:T(8,128)(2,1)S(1)}, u32[]{:S(2)}, u32[]{:S(2)}) collective-permute-start(bf16[1888,128]{1,0:T(8,128)(2,1)S(1)} %broadcast_select_fusion.3.rest_0_), channel_id=1, source_target_pairs={{0,2},{1,3},{2,0},{3,1},{4,6},{5,7},{6,4},{7,5},{8,10},{9,11},{10,... | collective-permute-start | bytes 1449992 | tf_op jit(solution)/shard_map/ppermute | solution.py:182
  94.1 14.8 %collective-permute-start.64 = (bf16[1888,128]{1,0:T(8,128)(2,1)}, bf16[1888,128]{1,0:T(8,128)(2,1)S(1)}, u32[]{:S(2)}, u32[]{:S(2)}) collective-permute-start(bf16[1888,128]{1,0:T(8,128)(2,1)} %collective-permute-done.58), channel_id=1, source_target_pairs={{8,0},{12,4},{16,24},{20,28},{9,1},{13,5},{17,25},{21,29},{10,2},{... | collective-permute-start | bytes 1449992 | tf_op jit(solution)/shard_map/ppermute | solution.py:186
  99.0 8.7 %collective-permute-start.57 = (bf16[384,384]{1,0:T(8,128)(2,1)S(1)}, bf16[384,384]{1,0:T(8,128)(2,1)S(1)}, u32[]{:S(2)}, u32[]{:S(2)}) collective-permute-start(bf16[384,384]{1,0:T(8,128)(2,1)S(1)} %shard_map.69.rest_0_.rest_1_), channel_id=1, source_target_pairs={{0,4},{4,0},{8,12},{12,8},{16,20},{20,16},{24,28},{28,24},{1,5},{5... | collective-permute-start | bytes 884744 | tf_op jit(solution)/shard_map/ppermute | solution.py:177
  108.9 3.2 %collective-permute-start.66 = (bf16[1888,128]{1,0:T(8,128)(2,1)S(1)}, bf16[1888,128]{1,0:T(8,128)(2,1)S(1)}, u32[]{:S(2)}, u32[]{:S(2)}) collective-permute-start(bf16[1888,128]{1,0:T(8,128)(2,1)S(1)} %broadcast_select_fusion.3.rest_0_), channel_id=1, source_target_pairs={{0,1},{1,0},{2,3},{3,2},{4,5},{5,4},{6,7},{7,6},{8,9},{9,8},{10,11... | collective-permute-start | bytes 1449992 | tf_op jit(solution)/shard_map/ppermute | solution.py:182
  108.9 3.2 %collective-permute-start.67 = (bf16[1888,128]{1,0:T(8,128)(2,1)S(1)}, bf16[1888,128]{1,0:T(8,128)(2,1)S(1)}, u32[]{:S(2)}, u32[]{:S(2)}) collective-permute-start(bf16[1888,128]{1,0:T(8,128)(2,1)S(1)} %collective-permute-done.65.rest_2_), channel_id=1, source_target_pairs={{0,1},{1,0},{2,3},{3,2},{4,5},{5,4},{6,7},{7,6},{8,9},{9,8},{10,11... | collective-permute-start | bytes 1449992 | tf_op jit(solution)/shard_map/ppermute | solution.py:182
  109.5 11.0 %collective-permute-start.69 = (bf16[1888,128]{1,0:T(8,128)(2,1)S(1)}, bf16[1888,128]{1,0:T(8,128)(2,1)S(1)}, u32[]{:S(2)}, u32[]{:S(2)}) collective-permute-start(bf16[1888,128]{1,0:T(8,128)(2,1)S(1)} %broadcast_select_fusion.2.rest_0_), channel_id=1, source_target_pairs={{0,1},{1,0},{2,3},{3,2},{4,5},{5,4},{6,7},{7,6},{8,9},{9,8},{10,11... | collective-permute-start | bytes 1449992 | tf_op jit(solution)/shard_map/ppermute | solution.py:182
  109.5 13.5 %collective-permute-start.70 = (bf16[1888,128]{1,0:T(8,128)(2,1)S(1)}, bf16[1888,128]{1,0:T(8,128)(2,1)S(1)}, u32[]{:S(2)}, u32[]{:S(2)}) collective-permute-start(bf16[1888,128]{1,0:T(8,128)(2,1)S(1)} %broadcast_select_fusion.2.rest_0_), channel_id=1, source_target_pairs={{0,2},{1,3},{2,0},{3,1},{4,6},{5,7},{6,4},{7,5},{8,10},{9,11},{10,... | collective-permute-start | bytes 1449992 | tf_op jit(solution)/shard_map/ppermute | solution.py:182
  110.6 9.9 %collective-permute-start.63 = (bf16[384,384]{1,0:T(8,128)(2,1)S(1)}, bf16[384,384]{1,0:T(8,128)(2,1)S(1)}, u32[]{:S(2)}, u32[]{:S(2)}) collective-permute-start(bf16[384,384]{1,0:T(8,128)(2,1)S(1)} %shard_map.71.rest_2_.rest_1_), channel_id=1, source_target_pairs={{0,4},{4,0},{8,12},{12,8},{16,20},{20,16},{24,28},{28,24},{1,5},{5... | collective-permute-start | bytes 884744 | tf_op jit(solution)/shard_map/ppermute | solution.py:177
  115.3 10.7 %collective-permute-start.68 = (bf16[384,384]{1,0:T(8,128)(2,1)S(1)}, bf16[384,384]{1,0:T(8,128)(2,1)S(1)}, u32[]{:S(2)}, u32[]{:S(2)}) collective-permute-start(bf16[384,384]{1,0:T(8,128)(2,1)S(1)} %shard_map.73.rest_4_.rest_1_), channel_id=1, source_target_pairs={{0,4},{4,0},{8,12},{12,8},{16,20},{20,16},{24,28},{28,24},{1,5},{5... | collective-permute-start | bytes 884744 | tf_op jit(solution)/shard_map/ppermute | solution.py:177
  126.0 1.9 %collective-permute-start.71 = (bf16[1888,128]{1,0:T(8,128)(2,1)S(1)}, bf16[1888,128]{1,0:T(8,128)(2,1)S(1)}, u32[]{:S(2)}, u32[]{:S(2)}) collective-permute-start(bf16[1888,128]{1,0:T(8,128)(2,1)S(1)} %collective-permute-done.70.rest_2_), channel_id=1, source_target_pairs={{0,1},{1,0},{2,3},{3,2},{4,5},{5,4},{6,7},{7,6},{8,9},{9,8},{10,11... | collective-permute-start | bytes 1449992 | tf_op jit(solution)/shard_map/ppermute | solution.py:182
  129.7 1.4 copy-start.6
  131.1 9.1 %collective-permute-start.72 = (bf16[384,384]{1,0:T(8,128)(2,1)S(1)}, bf16[384,384]{1,0:T(8,128)(2,1)S(1)}, u32[]{:S(2)}, u32[]{:S(2)}) collective-permute-start(bf16[384,384]{1,0:T(8,128)(2,1)S(1)} %shard_map.75.rest_6_.rest_1_), channel_id=1, source_target_pairs={{0,4},{4,0},{8,12},{12,8},{16,20},{20,16},{24,28},{28,24},{1,5},{5... | collective-permute-start | bytes 884744 | tf_op jit(solution)/shard_map/ppermute | solution.py:177
  132.7 8.4 %copy-start.7 = (bf16[384,3072]{1,0:T(8,128)(2,1)S(1)}, bf16[384,3072]{1,0:T(8,128)(2,1)}, u32[]{:S(2)}) copy-start(bf16[384,3072]{1,0:T(8,128)(2,1)} %copy-done.6) | copy-start | bytes 7077892
  148.4 12.3 %collective-permute-start.75 = (bf16[1024,128]{1,0:T(8,128)(2,1)}, bf16[1024,128]{1,0:T(8,128)(2,1)S(1)}, u32[]{:S(2)}, u32[]{:S(2)}) collective-permute-start(bf16[1024,128]{1,0:T(8,128)(2,1)} %shard_map.80), channel_id=1, source_target_pairs={{0,24},{4,28},{8,16},{12,20},{16,8},{20,12},{24,0},{28,4},{1,25},{... | collective-permute-start | bytes 786440 | tf_op jit(solution)/shard_map/ppermute | solution.py:177
  151.0 23.9 %collective-permute-start.74 = (bf16[1024,128]{1,0:T(8,128)(2,1)S(1)}, bf16[1024,128]{1,0:T(8,128)(2,1)}, u32[]{:S(2)}, u32[]{:S(2)}) collective-permute-start(bf16[1024,128]{1,0:T(8,128)(2,1)S(1)} %shard_map.79), channel_id=1, source_target_pairs={{0,16},{4,20},{8,24},{12,28},{16,0},{20,4},{24,8},{28,12},{1,17},{... | collective-permute-start | bytes 786440 | tf_op jit(solution)/shard_map/ppermute | solution.py:177
  152.2 22.7 %collective-permute-start.73 = (bf16[1024,128]{1,0:T(8,128)(2,1)S(1)}, bf16[1024,128]{1,0:T(8,128)(2,1)}, u32[]{:S(2)}, u32[]{:S(2)}) collective-permute-start(bf16[1024,128]{1,0:T(8,128)(2,1)S(1)} %shard_map.78), channel_id=1, source_target_pairs={{0,8},{4,12},{8,0},{12,4},{16,24},{20,28},{24,16},{28,20},{1,9},{5... | collective-permute-start | bytes 786440 | tf_op jit(solution)/shard_map/ppermute | solution.py:177
  156.8 1.7 copy-start.5
  160.7 17.2 %copy-start.34 = (bf16[384,768]{1,0:T(8,128)(2,1)S(1)}, bf16[384,768]{1,0:T(8,128)(2,1)}, u32[]{:S(2)}) copy-start(bf16[384,768]{1,0:T(8,128)(2,1)} %h) | copy-start | bytes 1769476
  160.7 17.2 %copy-start.36 = (f32[2,4,512]{2,1,0:T(4,128)S(1)}, f32[2,4,512]{2,1,0:T(4,128)}, u32[]{:S(2)}) copy-start(f32[2,4,512]{2,1,0:T(4,128)} %param.8) | copy-start | bytes 49156
  (12 other events, 10.9 us)

commit v3 on v2

--- a/solution.py
+++ b/solution.py
@@ -16,20 +16,21 @@
 
 SMEM_SPEC = pl.BlockSpec(memory_space=pltpu.SMEM)
 VMEM_SPEC = pl.BlockSpec(memory_space=pltpu.VMEM)
-
-
-def call(body, scalars, arrays, outs, scratch=(), flops=0, weight=1):
-    moved = sum(a.size * a.dtype.itemsize for a in arrays)
+ANY_SPEC = pl.BlockSpec(memory_space=pl.ANY)
+
+
+def call(body, scalars, arrays, outs, scratch=(), flops=0, weight=1, left=()):
+    moved = sum(a.size * a.dtype.itemsize for a in (*arrays, *left))
     moved += sum(o.size * o.dtype.itemsize for o in outs)
     return pl.pallas_call(
         body,
         out_shape=tuple(outs),
-        in_specs=[SMEM_SPEC] * len(scalars) + [VMEM_SPEC] * len(arrays),
+        in_specs=[SMEM_SPEC] * len(scalars) + [VMEM_SPEC] * len(arrays) + [ANY_SPEC] * len(left),
         out_specs=tuple(VMEM_SPEC for _ in outs),
         scratch_shapes=list(scratch),
         compiler_params=pltpu.CompilerParams(vmem_limit_bytes=VMEM_BYTES),
         cost_estimate=pl.CostEstimate(flops=flops, bytes_accessed=weight * moved, transcendentals=0),
-    )(*scalars, *arrays)
+    )(*scalars, *arrays, *left)
 
 
 def shape(*dims, dtype=BF16):
@@ -90,33 +91,29 @@
     wide = BLK // zs
     for s in range(zs):
         for other in range(2):
-            piece = rest[2 * s + other]
+            piece, base = (rest[zs], s * 2 * cap * wide) if other else (rest[s], 0)
             row = info[0] ^ (2 * s + other)
             for k, j, keep, place in kept(pmask, row, info[1] * jb, kb, jb):
                 columns = pl.ds(pl.multiple_of((row * kb + k) * BLK, BLK), BLK)
                 for part in range(2):
-                    top = pl.multiple_of((2 * jnp.minimum(place, cap - 1) + part) * wide, wide)
+                    top = pl.multiple_of(base + (2 * jnp.minimum(place, cap - 1) + part) * wide, wide)
                     here = piece[pl.ds(top, wide), :]
                     rows = slice((part * jb + j) * wide, (part * jb + j + 1) * wide)
                     out[rows, columns] = jnp.where(keep, here, jnp.zeros_like(here))
 
 
-def join_kernel(zs, side, info, *rest):
-    out = rest[-1]
-    for i in range(2 * zs):
-        out[:, pl.ds(pl.multiple_of((info[0] ^ i) * side, side), side)] = rest[i][...]
-
-
 def spread_kernel(s, cap, kb, jb, info, hmask, *rest):
-    packed, (dense, diagonal, slots) = rest[:-3], rest[-3:]
+    (near, far, core), (dense, diagonal, slots) = rest[:-3], rest[-3:]
+    size = cap * BLK + kb * BLK // 4
     row = info[0] ^ (2 * s)
     part = kb * BLK // 4
     for m in range(4):
         col = info[1] ^ m
         start = pl.multiple_of(col % 2 * (cap * BLK), BLK)
-        slots[pl.ds(start, cap * BLK), :] = packed[m][: cap * BLK, :]
+        packed, base = ((near, 0), (core, 0), (far, 0), (core, size))[m]
+        slots[pl.ds(start, cap * BLK), :] = packed[base : base + cap * BLK, :]
         start = pl.multiple_of((2 * (col % 2) + col // 2) * part, part)
-        diagonal[pl.ds(start, part), :] = packed[m][cap * BLK :, :]
+        diagonal[pl.ds(start, part), :] = packed[base + cap * BLK : base + size, :]
         if m % 2 == 0:
             continue
         left = col // 2 * (2 * jb)
@@ -150,20 +147,28 @@
     ).astype(BF16)
 
 
-def second_kernel(slots, cap, zs, kb, jb, info, pmask, joined, *rest):
+def second_kernel(slots, cap, zs, kb, jb, info, pmask, *rest):
     half_square = 0.5 * TIME_STEP * TIME_STEP
     count = len(slots)
-    dense, first, packed, (change, room) = rest[:count], rest[count : 2 * count], rest[2 * count : -2], rest[-2:]
+    pieces, dense, packed = rest[: 2 * zs], rest[2 * zs : 2 * zs + count], rest[2 * zs + count : -5]
+    joined, held, change, room, arrived = rest[-5:]
+    copies = [pltpu.make_async_copy(dense[i], held.at[i], arrived.at[i]) for i in range(count)]
+    for copy in copies:
+        copy.start()
+    side = kb * BLK
+    for i in range(2 * zs):
+        joined[:, pl.ds(pl.multiple_of((info[0] ^ i) * side, side), side)] = pieces[i][...]
     wide = BLK // zs
     for i, s in enumerate(slots):
+        copies[i].wait()
         second = lax.dot_general(
-            joined[...], dense[i][...], (((1,), (1,)), ((), ())), preferred_element_type=F32
+            joined[...], held[i], (((1,), (1,)), ((), ())), preferred_element_type=F32
         )
         half = second.shape[0] // 2
         real, imag = slice(0, half), slice(half, 2 * half)
-        other = first[i]
-        change[i, real, :] = (TIME_STEP * other[imag, :].astype(F32) - half_square * second[real, :]).astype(BF16)
-        change[i, imag, :] = (-TIME_STEP * other[real, :].astype(F32) - half_square * second[imag, :]).astype(BF16)
+        first = pieces[2 * s]
+        change[i, real, :] = (TIME_STEP * first[imag, :].astype(F32) - half_square * second[real, :]).astype(BF16)
+        change[i, imag, :] = (-TIME_STEP * first[real, :].astype(F32) - half_square * second[imag, :]).astype(BF16)
         for k, j, _, place in kept(pmask, info[0] ^ (2 * s), info[1] * jb, kb, jb):
             for part in range(2):
                 top = pl.multiple_of((2 * place + part) * wide, wide)
@@ -208,7 +213,7 @@
     return potential + KAPPA * (beside - 6.0 * potential)
 
 
-def potential_blocks(potential, basis):
+def potential_blocks(potential, basis, gate):
     width_x, width_y, depth_z = potential.shape
     kb = basis.shape[2] // BLK
     effective = effective_potential(potential)
@@ -220,10 +225,14 @@
         flops=2 * basis.size * BLK,
         weight=32,
     )
-    for bits, side in ((1, lax.axis_index("col") % 2), (2, lax.axis_index("col") // 2)):
-        half = total.shape[0] // 2
-        low, high = total[:half], total[half:]
-        total = jnp.where(side == 0, low, high) + swap_col(jnp.where(side == 0, high, low), bits)
+    (total,) = after(gate, total)
+    part = total.shape[0] // 4
+
+    def of(col):
+        return lax.dynamic_slice_in_dim(total, (2 * (col % 2) + col // 2) * part, part, axis=0)
+
+    col = lax.axis_index("col")
+    total = of(col) + swap_col(of(col ^ 1), 1) + swap_col(of(col ^ 2), 2) + swap_col(of(col ^ 3), 3)
     factor = float(BLK * width_x * width_y * depth_z * lax.axis_size("col")) ** (-0.5)
     return (total * factor).astype(BF16)
 
@@ -248,11 +257,9 @@
     )
 
     mine = [pieces[s] if s == 0 else swap_row(pieces[s], 2 * s) for s in range(zs)]
-    theirs = [swap_row(piece, 1) for piece in mine]
+    theirs = swap_row(jnp.concatenate(mine), 1)
     hamiltonian_core = swap_col(hamiltonian, 1)
-    (potential,) = after((hamiltonian_core, *pieces), potential)
-    quarter = potential_blocks(potential, basis)
-    hamiltonian, quarter = after(tuple(mine[1:]), hamiltonian, quarter)
+    quarter = potential_blocks(potential, basis, (mine[1], mine[2], mine[3]))
     (own,) = call(
         functools.partial(pack_kernel, cap_h, kb, jb),
         [info, hmask],
@@ -261,11 +268,11 @@
         scratch=[pltpu.VMEM(((cap_h + 2) * BLK, BLK), BF16)],
     )
 
-    def spread(s, near, far, near_core, far_core):
+    def spread(s, near, far, core):
         return call(
             functools.partial(spread_kernel, s, cap_h, kb, jb),
             [info, hmask],
-            [near, near_core, far, far_core],
+            [near, far, core],
             [shape(side, order)],
             scratch=[pltpu.VMEM((side, BLK), BF16), pltpu.VMEM((2 * cap_h * BLK, BLK), BF16)],
         )[0]
@@ -279,65 +286,64 @@
     inner = (z == 1) | (z == 2)
     beside, over, own_y = swap_row(own, 2), along(own, middle), swap_col(own, 2)
 
+    def other_core(near, far):
+        return swap_col(jnp.concatenate([near, far]), 1)
+
     own, beside, over, own_y = after((over, own_y), own, beside, over, own_y)
-    over_beside, out_near = along(beside, middle), along(over, outward)
-    beside_y, own_core, own_y_core = swap_col(beside, 2), swap_col(own, 1), swap_col(own_y, 1)
+    over_beside, out_near, beside_y = along(beside, middle), along(over, outward), swap_col(beside, 2)
+    own_core = other_core(own, own_y)
     (joined,) = call(
         functools.partial(unpack_kernel, cap, zs, kb, jb),
         [info, pmask],
-        [piece for pair in zip(mine, theirs) for piece in pair],
+        [*mine, theirs],
         [shape(wide, order)],
     )
 
-    done = (out_near, beside_y, own_core, own_y_core, joined)
+    done = (out_near, beside_y, own_core, joined)
     beside, over, over_beside, out_near, beside_y = after(
         done, beside, over, over_beside, out_near, beside_y
     )
     slot_2 = jnp.where(inner, over_beside, out_near)
-    out_far, slot_2_y = along(over_beside, outward), swap_col(slot_2, 2)
-    beside_core, beside_y_core = swap_col(beside, 1), swap_col(beside_y, 1)
+    out_far, slot_2_y, beside_core = along(over_beside, outward), swap_col(slot_2, 2), other_core(beside, beside_y)
     dense, first, first_x = [None] * zs, [None] * zs, [None] * zs
-    dense[0] = spread(0, own, own_y, own_core, own_y_core)
+    dense[0] = spread(0, own, own_y, own_core)
     first[0] = multiply(dense[0])
     first_x[0] = swap_row(first[0], 1)
-    dense[1] = spread(1, beside, beside_y, beside_core, beside_y_core)
+    dense[1] = spread(1, beside, beside_y, beside_core)
     first[1] = multiply(dense[1])
 
     done = (out_far, slot_2_y, first[1], first_x[0])
     over, out_far, slot_2, slot_2_y = after(done, over, out_far, slot_2, slot_2_y)
     slot_3 = jnp.where(inner, over, out_far)
-    slot_3_y = swap_col(slot_3, 2)
-    slot_2_core, slot_2_y_core, slot_3_core = swap_col(slot_2, 1), swap_col(slot_2_y, 1), swap_col(slot_3, 1)
+    slot_3_y, slot_2_core = swap_col(slot_3, 2), other_core(slot_2, slot_2_y)
     first_x[1] = swap_row(first[1], 1)
-    dense[2] = spread(2, slot_2, slot_2_y, slot_2_core, slot_2_y_core)
+    dense[2] = spread(2, slot_2, slot_2_y, slot_2_core)
     first[2] = multiply(dense[2])
     first_x[2] = swap_row(first[2], 1)
 
-    (slot_3_y,) = after((slot_3_core, first_x[1], first_x[2]), slot_3_y)
-    slot_3_y_core = swap_col(slot_3_y, 1)
-    dense[3] = spread(3, slot_3, slot_3_y, slot_3_core, slot_3_y_core)
+    (slot_3_y,) = after((first_x[1], first[2]), slot_3_y)
+    slot_3_core = other_core(slot_3, slot_3_y)
+    dense[3] = spread(3, slot_3, slot_3_y, slot_3_core)
     first[3] = multiply(dense[3])
     first_x[3] = swap_row(first[3], 1)
-    (first_joined,) = call(
-        functools.partial(join_kernel, zs, side),
-        [info],
-        [f for pair in zip(first, first_x) for f in pair],
-        [shape(wide, order)],
-    )
-
+    everything = [f for pair in zip(first, first_x) for f in pair]
     result = [None] * zs
-    for slots in ((3,), (2,), (1,), (0,)):
+    for slots in ((3, 2, 1), (0,)):
+        count = len(slots)
         outs = call(
             functools.partial(second_kernel, slots, cap, zs, kb, jb),
             [info, pmask],
-            [first_joined, *(dense[s] for s in slots), *(first[s] for s in slots)],
-            [piece] * len(slots),
+            everything,
+            [piece] * count,
             scratch=[
-                pltpu.VMEM((len(slots), wide, side), BF16),
-                pltpu.VMEM((len(slots), 2 * (kb * jb + 1) * BLK // zs, BLK), BF16),
+                pltpu.VMEM((wide, order), BF16),
+                pltpu.VMEM((count, side, order), BF16),
+                pltpu.VMEM((count, wide, side), BF16),
+                pltpu.VMEM((count, 2 * (kb * jb + 1) * BLK // zs, BLK), BF16),
+                pltpu.SemaphoreType.DMA((count,)),
             ],
-            flops=2 * side * order * wide * len(slots),
-            weight=1 if slots[0] else 32,
+            flops=2 * side * order * wide * count,
+            left=[dense[s] for s in slots],
         )
         for s, out in zip(slots, outs):
             result[s] = out if s == 0 else swap_row(out, 2 * s)

time: 179 us -> 181 us (1.011); the launches traced: 178 us -> 182 us
  Pallas kernels: 34.1 us -> 49.5 us
  waiting for transfers between devices: 73.6 us -> 62.5 us
  other arithmetic: 4.04 us -> 9.6 us
  local copies, waits for them, and re-layouts: 13.7 us -> 9.76 us
  starting transfers between devices: 50.7 us -> 48.5 us
    pallas_call x18 -> x15, Pallas kernels: 34.1 us -> 49.5 us  [call(): pl.pallas_call(body, out_shape=tuple(outs), in_specs=[SMEM_SPEC] * len(sc...]
    ppermute x15 -> x12, waiting for transfers between devices: 64.9 us -> 51.1 us  [swap_row(): return lax.ppermute(value, 'row', [(i, i ^ bits) for i in range(count)])]
    unnamed x44 -> x74, local copies, waits for them, and re-layouts: 11.2 us -> 6.13 us
    ppermute x15 -> x12, starting transfers between devices: 10.2 us -> 7.03 us  [swap_col(): return lax.ppermute(value, 'col', [(i, i ^ bits) for i in range(count)])]
    reduce_sum x2, other arithmetic: 0.43 us -> 3.15 us  [most(): mask.reshape(mask.shape[0] // kb, kb, mask.shape[1] // width, width)]
    ppermute x15 -> x12, waiting for transfers between devices: 6.71 us -> 9 us  [swap_col(): return lax.ppermute(value, 'col', [(i, i ^ bits) for i in range(count)])]
    ppermute x15 -> x12, starting transfers between devices: 23.9 us -> 26.2 us  [swap_row(): return lax.ppermute(value, 'row', [(i, i ^ bits) for i in range(count)])]
  transfers between devices with their start and end apart: 38 -> 32, of which waited for: 18 -> 15; matrix products, arithmetic and copies ran while one was open for 3% -> 6% of each run, Pallas kernels for 9% -> 12%
where the time goes in v3:
time: 181 us; the launch traced here: 182 us
  waiting for transfers between devices  62.5 us (35%)
  Pallas kernels  49.5 us (27%)
  starting transfers between devices  48.5 us (27%)
  local copies, waits for them, and re-layouts  9.76 us (5%)
  other arithmetic  9.6 us (5%)
  between operations  2.12 us (1%)
    ppermute x12, waiting for transfers between devices, swap_row(): return lax.ppermute(value, 'row', [(i, i ^ bits) for i in range(count)])  51.1 us
    pallas_call x15, Pallas kernels, call(): pl.pallas_call(body, out_shape=tuple(outs), in_specs=[SMEM_SPEC] * len(sc...  49.5 us
    ppermute x12, starting transfers between devices, swap_row(): return lax.ppermute(value, 'row', [(i, i ^ bits) for i in range(count)])  26.2 us
    ppermute x12, waiting for transfers between devices, swap_col(): return lax.ppermute(value, 'col', [(i, i ^ bits) for i in range(count)])  9 us
    ppermute x2, starting transfers between devices, beyond(): lax.ppermute(lax.slice_in_dim(potential, last, None, axis=dim), axis, for...  8.5 us
    ppermute x12, starting transfers between devices, swap_col(): return lax.ppermute(value, 'col', [(i, i ^ bits) for i in range(count)])  7.03 us
    unnamed x74, local copies, waits for them, and re-layouts  6.13 us
    ppermute x4, starting transfers between devices, along(): lax.ppermute(value, 'row', [(2 * a + x, 2 * b + x) for a, b in pairs for...  4.2 us
  transfers between devices with their start and end apart: 32, of which 15 were waited for; matrix products, arithmetic and copies ran while one was open for 6% of the time, Pallas kernels for 12%

profile of v3, /device:TPU:0, one launch (start us, length us, event | category | flops | bytes accessed | tf_op | source)
XLA Modules:
  0.0 182.0 jit_solution(14782017022887327542)
XLA Ops:
  2.0 5.5 %collective-permute-start.38 = (f32[1,4,512]{2,1,0:T(4,128)S(1)}, f32[1,4,512]{2,1,0:T(4,128)S(1)}, u32[]{:S(2)}, u32[]{:S(2)}) collective-permute-start(f32[1,4,512]{2,1,0:T(4,128)S(1)} %get-tuple-element.139), channel_id=1, source_target_pairs={{0,4},{4,8},{8,12},{12,16},{16,20},{20,24},{24,28},{1,5},{5,9},{9,... | collective-permute-start | bytes 24584 | tf_op jit(solution)/shard_map/ppermute | solution.py:204
  8.3 1.3 collective-permute-start.39
  9.6 3.0 %collective-permute-start.40 = (f32[2,1,512]{2,1,0:T(1,128)S(1)}, f32[2,1,512]{2,1,0:T(1,128)S(1)}, u32[]{:S(2)}, u32[]{:S(2)}) collective-permute-start(f32[2,1,512]{2,1,0:T(1,128)S(1)} %get-tuple-element.141), channel_id=1, source_target_pairs={{0,1},{1,2},{2,3},{4,5},{5,6},{6,7},{8,9},{9,10},{10,11},{12,13},{... | collective-permute-start | bytes 12296 | tf_op jit(solution)/shard_map/ppermute | solution.py:204
  12.8 1.8 shard_map.64
  14.5 2.2 %collective-permute-start.32 = (bf16[1024,128]{1,0:T(8,128)(2,1)S(1)}, bf16[1024,128]{1,0:T(8,128)(2,1)S(1)}, u32[]{:S(2)}, u32[]{:S(2)}) collective-permute-start(bf16[1024,128]{1,0:T(8,128)(2,1)S(1)} %get-tuple-element.90), channel_id=1, source_target_pairs={{0,8},{4,12},{8,0},{12,4},{16,24},{20,28},{24,16},{28,20},{1,9},{5... | collective-permute-start | bytes 786440 | tf_op jit(solution)/shard_map/ppermute | solution.py:182
  16.7 2.6 %collective-permute-start.33 = (bf16[1024,128]{1,0:T(8,128)(2,1)S(1)}, bf16[1024,128]{1,0:T(8,128)(2,1)S(1)}, u32[]{:S(2)}, u32[]{:S(2)}) collective-permute-start(bf16[1024,128]{1,0:T(8,128)(2,1)S(1)} %get-tuple-element.91), channel_id=1, source_target_pairs={{0,16},{4,20},{8,24},{12,28},{16,0},{20,4},{24,8},{28,12},{1,17},{... | collective-permute-start | bytes 786440 | tf_op jit(solution)/shard_map/ppermute | solution.py:182
  21.0 2.9 %shard_map.66 = f32[384,128]{1,0:T(8,128)S(1)} custom-call(f32[2,4,512]{2,1,0:T(4,128)S(1)} %fusion.12.effective, bf16[2,4,384,512]{3,2,1,0:T(8,128)(2,1)} %basis.1), custom_call_target="tpu_custom_call" | custom-call | flops 402653184 | bytes 107479040 | tf_op jit(solution)/shard_map/pallas_call | solution.py:25
  24.0 4.7 %collective-permute-done.32.rest_1_ = bf16[1024,128]{1,0:T(8,128)(2,1)S(1)} collective-permute-done((bf16[1024,128]{1,0:T(8,128)(2,1)S(1)}, bf16[1024,128]{1,0:T(8,128)(2,1)S(1)}, u32[]{:S(2)}, u32[]{:S(2)}) %collective-permute-start.32) | collective-permute-done | bytes 262176 | tf_op jit(solution)/shard_map/ppermute | solution.py:182
  28.6 9.4 %collective-permute-done.33.rest_2_ = bf16[1024,128]{1,0:T(8,128)(2,1)S(1)} collective-permute-done((bf16[1024,128]{1,0:T(8,128)(2,1)S(1)}, bf16[1024,128]{1,0:T(8,128)(2,1)S(1)}, u32[]{:S(2)}, u32[]{:S(2)}) %collective-permute-start.33) | collective-permute-done | bytes 262176 | tf_op jit(solution)/shard_map/ppermute | solution.py:182
  38.2 1.6 collective-permute-start.42
  40.0 2.3 %collective-permute-done.42 = f32[96,128]{1,0:T(8,128)S(1)} collective-permute-done((f32[96,128]{1,0:T(8,128)S(1)}, f32[96,128]{1,0:T(8,128)S(1)}, u32[]{:S(2)}, u32[]{:S(2)}) %collective-permute-start.42) | collective-permute-done | bytes 49184 | tf_op jit(solution)/shard_map/ppermute | solution.py:187
  44.7 5.6 %collective-permute-start.44 = (bf16[1888,128]{1,0:T(8,128)(2,1)S(1)}, bf16[1888,128]{1,0:T(8,128)(2,1)S(1)}, u32[]{:S(2)}, u32[]{:S(2)}) collective-permute-start(bf16[1888,128]{1,0:T(8,128)(2,1)S(1)} %shard_map.67.rest_0_), channel_id=1, source_target_pairs={{0,8},{4,12},{8,0},{12,4},{16,24},{20,28},{24,16},{28,20},{1,9},{5... | collective-permute-start | bytes 1449992 | tf_op jit(solution)/shard_map/ppermute | solution.py:182
  52.2 2.5 %collective-permute-start.35 = (bf16[4096,128]{1,0:T(8,128)(2,1)S(1)}, bf16[4096,128]{1,0:T(8,128)(2,1)S(1)}, u32[]{:S(2)}, u32[]{:S(2)}) collective-permute-start(bf16[4096,128]{1,0:T(8,128)(2,1)S(1)} %pad_maximum_fusion.9), channel_id=1, source_target_pairs={{0,4},{4,0},{8,12},{12,8},{16,20},{20,16},{24,28},{28,24},{1,5},{5... | collective-permute-start | bytes 3145736 | tf_op jit(solution)/shard_map/ppermute | solution.py:182
  54.6 7.1 %collective-permute-done.44.rest_0_ = bf16[1888,128]{1,0:T(8,128)(2,1)S(1)} collective-permute-done((bf16[1888,128]{1,0:T(8,128)(2,1)S(1)}, bf16[1888,128]{1,0:T(8,128)(2,1)S(1)}, u32[]{:S(2)}, u32[]{:S(2)}) %collective-permute-start.44) | collective-permute-done | bytes 483360 | tf_op jit(solution)/shard_map/ppermute | solution.py:182
  61.7 2.2 %collective-permute-done.46.rest_1_ = bf16[1888,128]{1,0:T(8,128)(2,1)S(1)} collective-permute-done((bf16[1888,128]{1,0:T(8,128)(2,1)S(1)}, bf16[1888,128]{1,0:T(8,128)(2,1)S(1)}, u32[]{:S(2)}, u32[]{:S(2)}) %collective-permute-start.46) | collective-permute-done | bytes 483360 | tf_op jit(solution)/shard_map/ppermute | solution.py:187
  64.8 1.3 collective-permute-start.50
  67.1 10.5 %collective-permute-done.35.rest_4_ = bf16[4096,128]{1,0:T(8,128)(2,1)S(1)} collective-permute-done((bf16[4096,128]{1,0:T(8,128)(2,1)S(1)}, bf16[4096,128]{1,0:T(8,128)(2,1)S(1)}, u32[]{:S(2)}, u32[]{:S(2)}) %collective-permute-start.35) | collective-permute-done | bytes 1048608 | tf_op jit(solution)/shard_map/ppermute | solution.py:182
  77.6 1.9 %shard_map.65.joined = bf16[384,3072]{1,0:T(8,128)(2,1)S(1)} custom-call(s32[2]{0:T(128)S(1)} %pad_add_fusion.1.info, s32[24,24]{1,0:T(8,128)S(1)} %copy-done.46, bf16[1024,128]{1,0:T(8,128)(2,1)S(1)} %copy-done.27, bf16[1024,128]{1,0:T(8,128)(2,1)S(1)} %copy-done.29, bf16[1024,128]{1,0:T(8,128)(2,1)S(1)} %copy-done.31, bf16[1024,128]{1,0:T(8,128)(2,1)S(1)} %copy-done.33, ...), custom_call_target="tpu_custom_call" | custom-call | bytes 4456448 | tf_op jit(solution)/shard_map/pallas_call | solution.py:25
  79.5 2.4 %collective-permute-done.50 = bf16[1888,128]{1,0:T(8,128)(2,1)S(1)} collective-permute-done((bf16[1888,128]{1,0:T(8,128)(2,1)S(1)}, bf16[1888,128]{1,0:T(8,128)(2,1)S(1)}, u32[]{:S(2)}, u32[]{:S(2)}) %collective-permute-start.50) | collective-permute-done | bytes 483360 | tf_op jit(solution)/shard_map/ppermute | solution.py:191
  86.3 1.5 collective-permute-start.54
  88.9 1.7 shard_map.68.dense.rest_8_
  90.6 1.4 shard_map.69.rest_0_
  92.1 2.5 %collective-permute-start.48 = (bf16[384,384]{1,0:T(8,128)(2,1)S(1)}, bf16[384,384]{1,0:T(8,128)(2,1)S(1)}, u32[]{:S(2)}, u32[]{:S(2)}) collective-permute-start(bf16[384,384]{1,0:T(8,128)(2,1)S(1)} %shard_map.69.rest_0_), channel_id=1, source_target_pairs={{0,4},{4,0},{8,12},{12,8},{16,20},{20,16},{24,28},{28,24},{1,5},{5... | collective-permute-start | bytes 884744 | tf_op jit(solution)/shard_map/ppermute | solution.py:182
  94.5 2.2 %shard_map.70.dense.rest_10_ = bf16[384,3072]{1,0:T(8,128)(2,1)S(1)} custom-call(s32[2]{0:T(128)S(1)} %pad_add_fusion.1.info, s32[24,24]{1,0:T(8,128)S(1)} %copy-done.45, bf16[1888,128]{1,0:T(8,128)(2,1)S(1)} %collective-permute-done.44.rest_0_, bf16[1888,128]{1,0:T(8,128)(2,1)S(1)} %copy-done.23, bf16[3776,128]{1,0:T(8,128)(2,1)} %collective-permute-done.52.rest_2_), custom_call_target="tpu_custom_call" | custom-call | bytes 4292608 | tf_op jit(solution)/shard_map/pallas_call | solution.py:25
  96.7 1.4 shard_map.71.rest_2_
  98.2 3.8 %collective-permute-done.48.rest_1_ = bf16[384,384]{1,0:T(8,128)(2,1)S(1)} collective-permute-done((bf16[384,384]{1,0:T(8,128)(2,1)S(1)}, bf16[384,384]{1,0:T(8,128)(2,1)S(1)}, u32[]{:S(2)}, u32[]{:S(2)}) %collective-permute-start.48) | collective-permute-done | bytes 294944 | tf_op jit(solution)/shard_map/ppermute | solution.py:182
  103.3 2.1 %collective-permute-start.53 = (bf16[384,384]{1,0:T(8,128)(2,1)S(1)}, bf16[384,384]{1,0:T(8,128)(2,1)S(1)}, u32[]{:S(2)}, u32[]{:S(2)}) collective-permute-start(bf16[384,384]{1,0:T(8,128)(2,1)S(1)} %shard_map.71.rest_2_), channel_id=1, source_target_pairs={{0,4},{4,0},{8,12},{12,8},{16,20},{20,16},{24,28},{28,24},{1,5},{5... | collective-permute-start | bytes 884744 | tf_op jit(solution)/shard_map/ppermute | solution.py:182
  105.4 1.7 shard_map.72.dense.rest_9_
  107.1 1.4 shard_map.73.rest_4_
  108.6 4.2 %collective-permute-done.53.rest_3_ = bf16[384,384]{1,0:T(8,128)(2,1)S(1)} collective-permute-done((bf16[384,384]{1,0:T(8,128)(2,1)S(1)}, bf16[384,384]{1,0:T(8,128)(2,1)S(1)}, u32[]{:S(2)}, u32[]{:S(2)}) %collective-permute-start.53) | collective-permute-done | bytes 294944 | tf_op jit(solution)/shard_map/ppermute | solution.py:182
  112.8 2.9 %collective-permute-done.58.rest_1_ = bf16[1888,128]{1,0:T(8,128)(2,1)S(1)} collective-permute-done((bf16[1888,128]{1,0:T(8,128)(2,1)S(1)}, bf16[1888,128]{1,0:T(8,128)(2,1)S(1)}, u32[]{:S(2)}, u32[]{:S(2)}) %collective-permute-start.58) | collective-permute-done | bytes 483360 | tf_op jit(solution)/shard_map/ppermute | solution.py:187
  115.8 2.1 %collective-permute-start.57 = (bf16[384,384]{1,0:T(8,128)(2,1)S(1)}, bf16[384,384]{1,0:T(8,128)(2,1)S(1)}, u32[]{:S(2)}, u32[]{:S(2)}) collective-permute-start(bf16[384,384]{1,0:T(8,128)(2,1)S(1)} %shard_map.73.rest_4_), channel_id=1, source_target_pairs={{0,4},{4,0},{8,12},{12,8},{16,20},{20,16},{24,28},{28,24},{1,5},{5... | collective-permute-start | bytes 884744 | tf_op jit(solution)/shard_map/ppermute | solution.py:182
  118.4 1.7 shard_map.74.dense.rest_8_
  120.1 1.4 shard_map.75.rest_6_
  121.5 2.1 %collective-permute-start.60 = (bf16[384,384]{1,0:T(8,128)(2,1)S(1)}, bf16[384,384]{1,0:T(8,128)(2,1)S(1)}, u32[]{:S(2)}, u32[]{:S(2)}) collective-permute-start(bf16[384,384]{1,0:T(8,128)(2,1)S(1)} %shard_map.75.rest_6_), channel_id=1, source_target_pairs={{0,4},{4,0},{8,12},{12,8},{16,20},{20,16},{24,28},{28,24},{1,5},{5... | collective-permute-start | bytes 884744 | tf_op jit(solution)/shard_map/ppermute | solution.py:182
  123.6 2.2 %collective-permute-done.57.rest_5_ = bf16[384,384]{1,0:T(8,128)(2,1)S(1)} collective-permute-done((bf16[384,384]{1,0:T(8,128)(2,1)S(1)}, bf16[384,384]{1,0:T(8,128)(2,1)S(1)}, u32[]{:S(2)}, u32[]{:S(2)}) %collective-permute-start.57) | collective-permute-done | bytes 294944 | tf_op jit(solution)/shard_map/ppermute | solution.py:182
  125.8 6.1 %collective-permute-done.60.rest_7_ = bf16[384,384]{1,0:T(8,128)(2,1)S(1)} collective-permute-done((bf16[384,384]{1,0:T(8,128)(2,1)S(1)}, bf16[384,384]{1,0:T(8,128)(2,1)S(1)}, u32[]{:S(2)}, u32[]{:S(2)}) %collective-permute-start.60) | collective-permute-done | bytes 294944 | tf_op jit(solution)/shard_map/ppermute | solution.py:182
  131.9 23.3 %shard_map.77 = (bf16[1024,128]{1,0:T(8,128)(2,1)}, bf16[1024,128]{1,0:T(8,128)(2,1)}, bf16[1024,128]{1,0:T(8,128)(2,1)}) custom-call(s32[2]{0:T(128)S(1)} %pad_add_fusion.1.info, s32[24,24]{1,0:T(8,128)S(1)} %copy-done.47, bf16[384,384]{1,0:T(8,128)(2,1)S(1)} %shard_map.69.rest_0_, bf16[384,384]{1,0:T(8,128)(2,1)S(1)} %collective-permute-done.48.rest_1_, ...), custom_call_target="tpu_custom_call" | custom-call | flops 2717908992 | bytes 10223616 | tf_op jit(solution)/shard_map/pallas_call | solution.py:25
  155.2 2.2 %collective-permute-start.61 = (bf16[1024,128]{1,0:T(8,128)(2,1)}, bf16[1024,128]{1,0:T(8,128)(2,1)}, u32[]{:S(2)}, u32[]{:S(2)}) collective-permute-start(bf16[1024,128]{1,0:T(8,128)(2,1)} %get-tuple-element.108), channel_id=1, source_target_pairs={{0,8},{4,12},{8,0},{12,4},{16,24},{20,28},{24,16},{28,20},{1,9},{5... | collective-permute-start | bytes 786440 | tf_op jit(solution)/shard_map/ppermute | solution.py:182
  158.4 1.4 collective-permute-start.63
  159.8 1.4 reshape.6
  161.9 1.6 reduce_sum.18
  163.5 1.5 reduce_sum.19
  165.1 1.4 reduce_max.18
  166.4 1.4 reduce_max.19
  172.9 2.9 %shard_map.76.rest_0_ = bf16[1024,128]{1,0:T(8,128)(2,1)S(1)} custom-call(s32[2]{0:T(128)S(1)} %pad_add_fusion.1.info, s32[24,24]{1,0:T(8,128)} %pmask.9, bf16[384,384]{1,0:T(8,128)(2,1)S(1)} %copy-done.25, bf16[384,384]{1,0:T(8,128)(2,1)S(1)} %copy-done.37, bf16[384,384]{1,0:T(8,128)(2,1)S(1)} %shard_map.71.rest_2_, ...), custom_call_target="tpu_custom_call" | custom-call | flops 905969664 | bytes 4980736 | tf_op jit(solution)/shard_map/pallas_call | solution.py:25
  175.9 3.2 %collective-permute-done.62.rest_2_ = bf16[1024,128]{1,0:T(8,128)(2,1)} collective-permute-done((bf16[1024,128]{1,0:T(8,128)(2,1)}, bf16[1024,128]{1,0:T(8,128)(2,1)}, u32[]{:S(2)}, u32[]{:S(2)}) %collective-permute-start.62) | collective-permute-done | bytes 262176 | tf_op jit(solution)/shard_map/ppermute | solution.py:182
  179.1 2.7 %shard_map.78 = bf16[2,384,768]{2,1,0:T(8,128)(2,1)} custom-call(s32[2]{0:T(128)S(1)} %pad_add_fusion.1.info, s32[24,24]{1,0:T(8,128)S(1)} %copy-done.48, bf16[2,384,768]{2,1,0:T(8,128)(2,1)S(1)} %copy-done.42, bf16[1024,128]{1,0:T(8,128)(2,1)S(1)} %shard_map.76.rest_0_, bf16[1024,128]{1,0:T(8,128)(2,1)} %collective-permute-done.61.rest_1_, ...), custom_call_target="tpu_custom_call" | custom-call | bytes 3407872 | tf_op jit(solution)/shard_map/pallas_call | solution.py:25
  (125 shorter events, 24.0 us)
Async XLA Ops:
  0.7 18.6 %collective-permute-start.37 = (f32[1,4,512]{2,1,0:T(4,128)S(1)}, f32[1,4,512]{2,1,0:T(4,128)S(1)}, u32[]{:S(2)}, u32[]{:S(2)}) collective-permute-start(f32[1,4,512]{2,1,0:T(4,128)S(1)} %get-tuple-element.138), channel_id=1, source_target_pairs={{4,0},{8,4},{12,8},{16,12},{20,16},{24,20},{28,24},{5,1},{9,5},{13... | collective-permute-start | bytes 24584 | tf_op jit(solution)/shard_map/ppermute | solution.py:205
  2.0 18.0 %collective-permute-start.38 = (f32[1,4,512]{2,1,0:T(4,128)S(1)}, f32[1,4,512]{2,1,0:T(4,128)S(1)}, u32[]{:S(2)}, u32[]{:S(2)}) collective-permute-start(f32[1,4,512]{2,1,0:T(4,128)S(1)} %get-tuple-element.139), channel_id=1, source_target_pairs={{0,4},{4,8},{8,12},{12,16},{16,20},{20,24},{24,28},{1,5},{5,9},{9,... | collective-permute-start | bytes 24584 | tf_op jit(solution)/shard_map/ppermute | solution.py:204
  8.3 8.4 %collective-permute-start.39 = (f32[2,1,512]{2,1,0:T(1,128)S(1)}, f32[2,1,512]{2,1,0:T(1,128)S(1)}, u32[]{:S(2)}, u32[]{:S(2)}) collective-permute-start(f32[2,1,512]{2,1,0:T(1,128)S(1)} %get-tuple-element.140), channel_id=1, source_target_pairs={{1,0},{2,1},{3,2},{5,4},{6,5},{7,6},{9,8},{10,9},{11,10},{13,12},{... | collective-permute-start | bytes 12296 | tf_op jit(solution)/shard_map/ppermute | solution.py:205
  9.6 9.7 %collective-permute-start.40 = (f32[2,1,512]{2,1,0:T(1,128)S(1)}, f32[2,1,512]{2,1,0:T(1,128)S(1)}, u32[]{:S(2)}, u32[]{:S(2)}) collective-permute-start(f32[2,1,512]{2,1,0:T(1,128)S(1)} %get-tuple-element.141), channel_id=1, source_target_pairs={{0,1},{1,2},{2,3},{4,5},{5,6},{6,7},{8,9},{9,10},{10,11},{12,13},{... | collective-permute-start | bytes 12296 | tf_op jit(solution)/shard_map/ppermute | solution.py:204
  14.5 37.5 %copy-start.26 = (bf16[1024,128]{1,0:T(8,128)(2,1)}, bf16[1024,128]{1,0:T(8,128)(2,1)S(1)}, u32[]{:S(2)}) copy-start(bf16[1024,128]{1,0:T(8,128)(2,1)S(1)} %get-tuple-element.89.rest_0_) | copy-start | bytes 786436
  14.5 14.1 %collective-permute-start.32 = (bf16[1024,128]{1,0:T(8,128)(2,1)S(1)}, bf16[1024,128]{1,0:T(8,128)(2,1)S(1)}, u32[]{:S(2)}, u32[]{:S(2)}) collective-permute-start(bf16[1024,128]{1,0:T(8,128)(2,1)S(1)} %get-tuple-element.90), channel_id=1, source_target_pairs={{0,8},{4,12},{8,0},{12,4},{16,24},{20,28},{24,16},{28,20},{1,9},{5... | collective-permute-start | bytes 786440 | tf_op jit(solution)/shard_map/ppermute | solution.py:182
  16.7 21.4 %collective-permute-start.33 = (bf16[1024,128]{1,0:T(8,128)(2,1)S(1)}, bf16[1024,128]{1,0:T(8,128)(2,1)S(1)}, u32[]{:S(2)}, u32[]{:S(2)}) collective-permute-start(bf16[1024,128]{1,0:T(8,128)(2,1)S(1)} %get-tuple-element.91), channel_id=1, source_target_pairs={{0,16},{4,20},{8,24},{12,28},{16,0},{20,4},{24,8},{28,12},{1,17},{... | collective-permute-start | bytes 786440 | tf_op jit(solution)/shard_map/ppermute | solution.py:182
  19.3 18.8 %collective-permute-start.34 = (bf16[1024,128]{1,0:T(8,128)(2,1)S(1)}, bf16[1024,128]{1,0:T(8,128)(2,1)S(1)}, u32[]{:S(2)}, u32[]{:S(2)}) collective-permute-start(bf16[1024,128]{1,0:T(8,128)(2,1)S(1)} %get-tuple-element.92), channel_id=1, source_target_pairs={{0,24},{4,28},{8,16},{12,20},{16,8},{20,12},{24,0},{28,4},{1,25},{... | collective-permute-start | bytes 786440 | tf_op jit(solution)/shard_map/ppermute | solution.py:182
  19.3 24.2 %collective-permute-start.36 = (bf16[384,768]{1,0:T(8,128)(2,1)}, bf16[384,768]{1,0:T(8,128)(2,1)S(1)}, u32[]{:S(2)}, u32[]{:S(2)}) collective-permute-start(bf16[384,768]{1,0:T(8,128)(2,1)} %h.1), channel_id=1, source_target_pairs={{0,1},{1,0},{2,3},{3,2},{4,5},{5,4},{6,7},{7,6},{8,9},{9,8},{10,11... | collective-permute-start | bytes 1769480 | tf_op jit(solution)/shard_map/ppermute | solution.py:187
  21.0 22.5 %copy-start.44 = (bf16[384,768]{1,0:T(8,128)(2,1)S(1)}, bf16[384,768]{1,0:T(8,128)(2,1)}, u32[]{:S(2)}) copy-start(bf16[384,768]{1,0:T(8,128)(2,1)} %h.1) | copy-start | bytes 1769476
  21.0 22.5 %copy-start.45 = (s32[24,24]{1,0:T(8,128)S(1)}, s32[24,24]{1,0:T(8,128)}, u32[]{:S(2)}) copy-start(s32[24,24]{1,0:T(8,128)} %hmask.9) | copy-start | bytes 6916
  28.6 23.5 %copy-start.28 = (bf16[1024,128]{1,0:T(8,128)(2,1)}, bf16[1024,128]{1,0:T(8,128)(2,1)S(1)}, u32[]{:S(2)}) copy-start(bf16[1024,128]{1,0:T(8,128)(2,1)S(1)} %collective-permute-done.32.rest_1_) | copy-start | bytes 786436
  38.1 14.1 %copy-start.32 = (bf16[1024,128]{1,0:T(8,128)(2,1)}, bf16[1024,128]{1,0:T(8,128)(2,1)S(1)}, u32[]{:S(2)}) copy-start(bf16[1024,128]{1,0:T(8,128)(2,1)S(1)} %collective-permute-done.34.rest_3_) | copy-start | bytes 786436
  38.1 1.9 %collective-permute-start.41 = (f32[96,128]{1,0:T(8,128)S(1)}, f32[96,128]{1,0:T(8,128)S(1)}, u32[]{:S(2)}, u32[]{:S(2)}) collective-permute-start(f32[96,128]{1,0:T(8,128)S(1)} %get-tuple-element.135), channel_id=1, source_target_pairs={{0,1},{1,0},{2,3},{3,2},{4,5},{5,4},{6,7},{7,6},{8,9},{9,8},{10,11... | collective-permute-start | bytes 147464 | tf_op jit(solution)/shard_map/ppermute | solution.py:187
  38.2 4.2 %collective-permute-start.42 = (f32[96,128]{1,0:T(8,128)S(1)}, f32[96,128]{1,0:T(8,128)S(1)}, u32[]{:S(2)}, u32[]{:S(2)}) collective-permute-start(f32[96,128]{1,0:T(8,128)S(1)} %get-tuple-element.137), channel_id=1, source_target_pairs={{0,2},{1,3},{2,0},{3,1},{4,6},{5,7},{6,4},{7,5},{8,10},{9,11},{10,... | collective-permute-start | bytes 147464 | tf_op jit(solution)/shard_map/ppermute | solution.py:187
  39.8 3.7 %collective-permute-start.43 = (f32[96,128]{1,0:T(8,128)S(1)}, f32[96,128]{1,0:T(8,128)S(1)}, u32[]{:S(2)}, u32[]{:S(2)}) collective-permute-start(f32[96,128]{1,0:T(8,128)S(1)} %get-tuple-element.136), channel_id=1, source_target_pairs={{0,3},{1,2},{2,1},{3,0},{4,7},{5,6},{6,5},{7,4},{8,11},{9,10},{10,... | collective-permute-start | bytes 147464 | tf_op jit(solution)/shard_map/ppermute | solution.py:187
  44.7 17.1 %collective-permute-start.44 = (bf16[1888,128]{1,0:T(8,128)(2,1)S(1)}, bf16[1888,128]{1,0:T(8,128)(2,1)S(1)}, u32[]{:S(2)}, u32[]{:S(2)}) collective-permute-start(bf16[1888,128]{1,0:T(8,128)(2,1)S(1)} %shard_map.67.rest_0_), channel_id=1, source_target_pairs={{0,8},{4,12},{8,0},{12,4},{16,24},{20,28},{24,16},{28,20},{1,9},{5... | collective-permute-start | bytes 1449992 | tf_op jit(solution)/shard_map/ppermute | solution.py:182
  50.2 11.5 %collective-permute-start.45 = (bf16[1888,128]{1,0:T(8,128)(2,1)S(1)}, bf16[1888,128]{1,0:T(8,128)(2,1)S(1)}, u32[]{:S(2)}, u32[]{:S(2)}) collective-permute-start(bf16[1888,128]{1,0:T(8,128)(2,1)S(1)} %shard_map.67.rest_0_), channel_id=1, source_target_pairs={{8,16},{12,20},{16,8},{20,12},{9,17},{13,21},{17,9},{21,13},{10,18... | collective-permute-start | bytes 1449992 | tf_op jit(solution)/shard_map/ppermute | solution.py:191
  50.9 13.0 %collective-permute-start.46 = (bf16[1888,128]{1,0:T(8,128)(2,1)S(1)}, bf16[1888,128]{1,0:T(8,128)(2,1)S(1)}, u32[]{:S(2)}, u32[]{:S(2)}) collective-permute-start(bf16[1888,128]{1,0:T(8,128)(2,1)S(1)} %shard_map.67.rest_0_), channel_id=1, source_target_pairs={{0,2},{1,3},{2,0},{3,1},{4,6},{5,7},{6,4},{7,5},{8,10},{9,11},{10,... | collective-permute-start | bytes 1449992 | tf_op jit(solution)/shard_map/ppermute | solution.py:187
  52.0 25.5 %copy-start.46 = (s32[24,24]{1,0:T(8,128)S(1)}, s32[24,24]{1,0:T(8,128)}, u32[]{:S(2)}) copy-start(s32[24,24]{1,0:T(8,128)} %pmask.9) | copy-start | bytes 6916
  52.1 25.4 %copy-start.27 = (bf16[1024,128]{1,0:T(8,128)(2,1)S(1)}, bf16[1024,128]{1,0:T(8,128)(2,1)}, u32[]{:S(2)}) copy-start(bf16[1024,128]{1,0:T(8,128)(2,1)} %copy-done.26) | copy-start | bytes 786436
  52.2 25.4 %collective-permute-start.35 = (bf16[4096,128]{1,0:T(8,128)(2,1)S(1)}, bf16[4096,128]{1,0:T(8,128)(2,1)S(1)}, u32[]{:S(2)}, u32[]{:S(2)}) collective-permute-start(bf16[4096,128]{1,0:T(8,128)(2,1)S(1)} %pad_maximum_fusion.9), channel_id=1, source_target_pairs={{0,4},{4,0},{8,12},{12,8},{16,20},{20,16},{24,28},{28,24},{1,5},{5... | collective-permute-start | bytes 3145736 | tf_op jit(solution)/shard_map/ppermute | solution.py:182
  54.6 22.9 %copy-start.29 = (bf16[1024,128]{1,0:T(8,128)(2,1)S(1)}, bf16[1024,128]{1,0:T(8,128)(2,1)}, u32[]{:S(2)}) copy-start(bf16[1024,128]{1,0:T(8,128)(2,1)} %copy-done.28) | copy-start | bytes 786436
  54.6 22.9 %copy-start.31 = (bf16[1024,128]{1,0:T(8,128)(2,1)S(1)}, bf16[1024,128]{1,0:T(8,128)(2,1)}, u32[]{:S(2)}) copy-start(bf16[1024,128]{1,0:T(8,128)(2,1)} %copy-done.30) | copy-start | bytes 786436
  54.6 22.9 %copy-start.33 = (bf16[1024,128]{1,0:T(8,128)(2,1)S(1)}, bf16[1024,128]{1,0:T(8,128)(2,1)}, u32[]{:S(2)}) copy-start(bf16[1024,128]{1,0:T(8,128)(2,1)} %copy-done.32) | copy-start | bytes 786436
  61.7 17.8 %copy-start.53 = (bf16[1888,128]{1,0:T(8,128)(2,1)}, bf16[1888,128]{1,0:T(8,128)(2,1)S(1)}, u32[]{:S(2)}) copy-start(bf16[1888,128]{1,0:T(8,128)(2,1)S(1)} %collective-permute-done.45) | copy-start | bytes 1449988
  64.0 18.0 %collective-permute-start.47 = (bf16[3776,128]{1,0:T(8,128)(2,1)S(1)}, bf16[3776,128]{1,0:T(8,128)(2,1)S(1)}, u32[]{:S(2)}, u32[]{:S(2)}) collective-permute-start(bf16[3776,128]{1,0:T(8,128)(2,1)S(1)} %pad_maximum_fusion.10), channel_id=1, source_target_pairs={{0,1},{1,0},{2,3},{3,2},{4,5},{5,4},{6,7},{7,6},{8,9},{9,8},{10,11... | collective-permute-start | bytes 2899976 | tf_op jit(solution)/shard_map/ppermute | solution.py:187
  64.1 15.4 %collective-permute-start.49 = (bf16[1888,128]{1,0:T(8,128)(2,1)S(1)}, bf16[1888,128]{1,0:T(8,128)(2,1)S(1)}, u32[]{:S(2)}, u32[]{:S(2)}) collective-permute-start(bf16[1888,128]{1,0:T(8,128)(2,1)S(1)} %collective-permute-done.44.rest_0_), channel_id=1, source_target_pairs={{8,16},{12,20},{16,8},{20,12},{9,17},{13,21},{17,9},{21,13},{10,18... | collective-permute-start | bytes 1449992 | tf_op jit(solution)/shard_map/ppermute | solution.py:191
  64.8 17.2 %collective-permute-start.50 = (bf16[1888,128]{1,0:T(8,128)(2,1)S(1)}, bf16[1888,128]{1,0:T(8,128)(2,1)S(1)}, u32[]{:S(2)}, u32[]{:S(2)}) collective-permute-start(bf16[1888,128]{1,0:T(8,128)(2,1)S(1)} %collective-permute-done.45), channel_id=1, source_target_pairs={{8,0},{12,4},{16,24},{20,28},{9,1},{13,5},{17,25},{21,29},{10,2},{... | collective-permute-start | bytes 1449992 | tf_op jit(solution)/shard_map/ppermute | solution.py:191
  66.1 15.9 %collective-permute-start.51 = (bf16[1888,128]{1,0:T(8,128)(2,1)S(1)}, bf16[1888,128]{1,0:T(8,128)(2,1)S(1)}, u32[]{:S(2)}, u32[]{:S(2)}) collective-permute-start(bf16[1888,128]{1,0:T(8,128)(2,1)S(1)} %collective-permute-done.44.rest_0_), channel_id=1, source_target_pairs={{0,2},{1,3},{2,0},{3,1},{4,6},{5,7},{6,4},{7,5},{8,10},{9,11},{10,... | collective-permute-start | bytes 1449992 | tf_op jit(solution)/shard_map/ppermute | solution.py:187
  84.2 10.4 %collective-permute-start.52 = (bf16[3776,128]{1,0:T(8,128)(2,1)}, bf16[3776,128]{1,0:T(8,128)(2,1)}, u32[]{:S(2)}, u32[]{:S(2)}) collective-permute-start(bf16[3776,128]{1,0:T(8,128)(2,1)} %pad_maximum_fusion.11), channel_id=1, source_target_pairs={{0,1},{1,0},{2,3},{3,2},{4,5},{5,4},{6,7},{7,6},{8,9},{9,8},{10,11... | collective-permute-start | bytes 2899976 | tf_op jit(solution)/shard_map/ppermute | solution.py:187
  85.4 16.6 %collective-permute-start.55 = (bf16[1888,128]{1,0:T(8,128)(2,1)S(1)}, bf16[1888,128]{1,0:T(8,128)(2,1)S(1)}, u32[]{:S(2)}, u32[]{:S(2)}) collective-permute-start(bf16[1888,128]{1,0:T(8,128)(2,1)S(1)} %broadcast_select_fusion.3.rest_0_), channel_id=1, source_target_pairs={{0,2},{1,3},{2,0},{3,1},{4,6},{5,7},{6,4},{7,5},{8,10},{9,11},{10,... | collective-permute-start | bytes 1449992 | tf_op jit(solution)/shard_map/ppermute | solution.py:187
  86.3 15.6 %collective-permute-start.54 = (bf16[1888,128]{1,0:T(8,128)(2,1)}, bf16[1888,128]{1,0:T(8,128)(2,1)S(1)}, u32[]{:S(2)}, u32[]{:S(2)}) collective-permute-start(bf16[1888,128]{1,0:T(8,128)(2,1)} %copy-done.55), channel_id=1, source_target_pairs={{8,0},{12,4},{16,24},{20,28},{9,1},{13,5},{17,25},{21,29},{10,2},{... | collective-permute-start | bytes 1449992 | tf_op jit(solution)/shard_map/ppermute | solution.py:191
  92.1 39.8 %copy-start.24 = (bf16[384,384]{1,0:T(8,128)(2,1)}, bf16[384,384]{1,0:T(8,128)(2,1)S(1)}, u32[]{:S(2)}) copy-start(bf16[384,384]{1,0:T(8,128)(2,1)S(1)} %shard_map.69.rest_0_) | copy-start | bytes 884740
  92.1 9.9 %collective-permute-start.48 = (bf16[384,384]{1,0:T(8,128)(2,1)S(1)}, bf16[384,384]{1,0:T(8,128)(2,1)S(1)}, u32[]{:S(2)}, u32[]{:S(2)}) collective-permute-start(bf16[384,384]{1,0:T(8,128)(2,1)S(1)} %shard_map.69.rest_0_), channel_id=1, source_target_pairs={{0,4},{4,0},{8,12},{12,8},{16,20},{20,16},{24,28},{28,24},{1,5},{5... | collective-permute-start | bytes 884744 | tf_op jit(solution)/shard_map/ppermute | solution.py:182
  101.9 29.9 %copy-start.36 = (bf16[384,384]{1,0:T(8,128)(2,1)}, bf16[384,384]{1,0:T(8,128)(2,1)S(1)}, u32[]{:S(2)}) copy-start(bf16[384,384]{1,0:T(8,128)(2,1)S(1)} %collective-permute-done.48.rest_1_) | copy-start | bytes 884740
  102.0 3.4 %collective-permute-start.56 = (bf16[3776,128]{1,0:T(8,128)(2,1)S(1)}, bf16[3776,128]{1,0:T(8,128)(2,1)S(1)}, u32[]{:S(2)}, u32[]{:S(2)}) collective-permute-start(bf16[3776,128]{1,0:T(8,128)(2,1)S(1)} %pad_maximum_fusion.12), channel_id=1, source_target_pairs={{0,1},{1,0},{2,3},{3,2},{4,5},{5,4},{6,7},{7,6},{8,9},{9,8},{10,11... | collective-permute-start | bytes 2899976 | tf_op jit(solution)/shard_map/ppermute | solution.py:187
  102.2 13.5 %collective-permute-start.58 = (bf16[1888,128]{1,0:T(8,128)(2,1)S(1)}, bf16[1888,128]{1,0:T(8,128)(2,1)S(1)}, u32[]{:S(2)}, u32[]{:S(2)}) collective-permute-start(bf16[1888,128]{1,0:T(8,128)(2,1)S(1)} %broadcast_select_fusion.2.rest_0_), channel_id=1, source_target_pairs={{0,2},{1,3},{2,0},{3,1},{4,6},{5,7},{6,4},{7,5},{8,10},{9,11},{10,... | collective-permute-start | bytes 1449992 | tf_op jit(solution)/shard_map/ppermute | solution.py:187
  103.3 9.4 %collective-permute-start.53 = (bf16[384,384]{1,0:T(8,128)(2,1)S(1)}, bf16[384,384]{1,0:T(8,128)(2,1)S(1)}, u32[]{:S(2)}, u32[]{:S(2)}) collective-permute-start(bf16[384,384]{1,0:T(8,128)(2,1)S(1)} %shard_map.71.rest_2_), channel_id=1, source_target_pairs={{0,4},{4,0},{8,12},{12,8},{16,20},{20,16},{24,28},{28,24},{1,5},{5... | collective-permute-start | bytes 884744 | tf_op jit(solution)/shard_map/ppermute | solution.py:182
  115.8 2.6 %collective-permute-start.59 = (bf16[3776,128]{1,0:T(8,128)(2,1)S(1)}, bf16[3776,128]{1,0:T(8,128)(2,1)S(1)}, u32[]{:S(2)}, u32[]{:S(2)}) collective-permute-start(bf16[3776,128]{1,0:T(8,128)(2,1)S(1)} %pad_maximum_fusion.13), channel_id=1, source_target_pairs={{0,1},{1,0},{2,3},{3,2},{4,5},{5,4},{6,7},{7,6},{8,9},{9,8},{10,11... | collective-permute-start | bytes 2899976 | tf_op jit(solution)/shard_map/ppermute | solution.py:187
  115.8 10.0 %collective-permute-start.57 = (bf16[384,384]{1,0:T(8,128)(2,1)S(1)}, bf16[384,384]{1,0:T(8,128)(2,1)S(1)}, u32[]{:S(2)}, u32[]{:S(2)}) collective-permute-start(bf16[384,384]{1,0:T(8,128)(2,1)S(1)} %shard_map.73.rest_4_), channel_id=1, source_target_pairs={{0,4},{4,0},{8,12},{12,8},{16,20},{20,16},{24,28},{28,24},{1,5},{5... | collective-permute-start | bytes 884744 | tf_op jit(solution)/shard_map/ppermute | solution.py:182
  121.5 47.6 %copy-start.9 = (bf16[384,3072]{1,0:T(8,128)(2,1)S(1)}, bf16[384,3072]{1,0:T(8,128)(2,1)}, u32[]{:S(2)}) copy-start(bf16[384,3072]{1,0:T(8,128)(2,1)} %copy-done.8) | copy-start | bytes 7077892
  121.5 10.4 %collective-permute-start.60 = (bf16[384,384]{1,0:T(8,128)(2,1)S(1)}, bf16[384,384]{1,0:T(8,128)(2,1)S(1)}, u32[]{:S(2)}, u32[]{:S(2)}) collective-permute-start(bf16[384,384]{1,0:T(8,128)(2,1)S(1)} %shard_map.75.rest_6_), channel_id=1, source_target_pairs={{0,4},{4,0},{8,12},{12,8},{16,20},{20,16},{24,28},{28,24},{1,5},{5... | collective-permute-start | bytes 884744 | tf_op jit(solution)/shard_map/ppermute | solution.py:182
  125.8 29.4 %copy-start.38 = (bf16[384,384]{1,0:T(8,128)(2,1)}, bf16[384,384]{1,0:T(8,128)(2,1)S(1)}, u32[]{:S(2)}) copy-start(bf16[384,384]{1,0:T(8,128)(2,1)S(1)} %collective-permute-done.57.rest_5_) | copy-start | bytes 884740
  131.9 23.3 %copy-start.40 = (bf16[384,384]{1,0:T(8,128)(2,1)}, bf16[384,384]{1,0:T(8,128)(2,1)S(1)}, u32[]{:S(2)}) copy-start(bf16[384,384]{1,0:T(8,128)(2,1)S(1)} %collective-permute-done.60.rest_7_) | copy-start | bytes 884740
  155.2 20.7 %collective-permute-start.61 = (bf16[1024,128]{1,0:T(8,128)(2,1)}, bf16[1024,128]{1,0:T(8,128)(2,1)}, u32[]{:S(2)}, u32[]{:S(2)}) collective-permute-start(bf16[1024,128]{1,0:T(8,128)(2,1)} %get-tuple-element.108), channel_id=1, source_target_pairs={{0,8},{4,12},{8,0},{12,4},{16,24},{20,28},{24,16},{28,20},{1,9},{5... | collective-permute-start | bytes 786440 | tf_op jit(solution)/shard_map/ppermute | solution.py:182
  157.4 21.7 %collective-permute-start.62 = (bf16[1024,128]{1,0:T(8,128)(2,1)}, bf16[1024,128]{1,0:T(8,128)(2,1)}, u32[]{:S(2)}, u32[]{:S(2)}) collective-permute-start(bf16[1024,128]{1,0:T(8,128)(2,1)} %get-tuple-element.109), channel_id=1, source_target_pairs={{0,16},{4,20},{8,24},{12,28},{16,0},{20,4},{24,8},{28,12},{1,17},{... | collective-permute-start | bytes 786440 | tf_op jit(solution)/shard_map/ppermute | solution.py:182
  158.4 20.6 %collective-permute-start.63 = (bf16[1024,128]{1,0:T(8,128)(2,1)}, bf16[1024,128]{1,0:T(8,128)(2,1)}, u32[]{:S(2)}, u32[]{:S(2)}) collective-permute-start(bf16[1024,128]{1,0:T(8,128)(2,1)} %get-tuple-element.110), channel_id=1, source_target_pairs={{0,24},{4,28},{8,16},{12,20},{16,8},{20,12},{24,0},{28,4},{1,25},{... | collective-permute-start | bytes 786440 | tf_op jit(solution)/shard_map/ppermute | solution.py:182
  (21 other events, 74.9 us)

commit v4 on v3

--- a/solution.py
+++ b/solution.py
@@ -16,21 +16,20 @@
 
 SMEM_SPEC = pl.BlockSpec(memory_space=pltpu.SMEM)
 VMEM_SPEC = pl.BlockSpec(memory_space=pltpu.VMEM)
-ANY_SPEC = pl.BlockSpec(memory_space=pl.ANY)
-
-
-def call(body, scalars, arrays, outs, scratch=(), flops=0, weight=1, left=()):
-    moved = sum(a.size * a.dtype.itemsize for a in (*arrays, *left))
+
+
+def call(body, scalars, arrays, outs, scratch=(), flops=0, weight=1):
+    moved = sum(a.size * a.dtype.itemsize for a in arrays)
     moved += sum(o.size * o.dtype.itemsize for o in outs)
     return pl.pallas_call(
         body,
         out_shape=tuple(outs),
-        in_specs=[SMEM_SPEC] * len(scalars) + [VMEM_SPEC] * len(arrays) + [ANY_SPEC] * len(left),
+        in_specs=[SMEM_SPEC] * len(scalars) + [VMEM_SPEC] * len(arrays),
         out_specs=tuple(VMEM_SPEC for _ in outs),
         scratch_shapes=list(scratch),
         compiler_params=pltpu.CompilerParams(vmem_limit_bytes=VMEM_BYTES),
         cost_estimate=pl.CostEstimate(flops=flops, bytes_accessed=weight * moved, transcendentals=0),
-    )(*scalars, *arrays, *left)
+    )(*scalars, *arrays)
 
 
 def shape(*dims, dtype=BF16):
@@ -100,6 +99,12 @@
                     here = piece[pl.ds(top, wide), :]
                     rows = slice((part * jb + j) * wide, (part * jb + j + 1) * wide)
                     out[rows, columns] = jnp.where(keep, here, jnp.zeros_like(here))
+
+
+def join_kernel(zs, side, info, *rest):
+    out = rest[-1]
+    for i in range(2 * zs):
+        out[:, pl.ds(pl.multiple_of((info[0] ^ i) * side, side), side)] = rest[i][...]
 
 
 def spread_kernel(s, cap, kb, jb, info, hmask, *rest):
@@ -147,28 +152,20 @@
     ).astype(BF16)
 
 
-def second_kernel(slots, cap, zs, kb, jb, info, pmask, *rest):
+def second_kernel(slots, cap, zs, kb, jb, info, pmask, joined, *rest):
     half_square = 0.5 * TIME_STEP * TIME_STEP
     count = len(slots)
-    pieces, dense, packed = rest[: 2 * zs], rest[2 * zs : 2 * zs + count], rest[2 * zs + count : -5]
-    joined, held, change, room, arrived = rest[-5:]
-    copies = [pltpu.make_async_copy(dense[i], held.at[i], arrived.at[i]) for i in range(count)]
-    for copy in copies:
-        copy.start()
-    side = kb * BLK
-    for i in range(2 * zs):
-        joined[:, pl.ds(pl.multiple_of((info[0] ^ i) * side, side), side)] = pieces[i][...]
+    dense, first, packed, (change, room) = rest[:count], rest[count : 2 * count], rest[2 * count : -2], rest[-2:]
     wide = BLK // zs
     for i, s in enumerate(slots):
-        copies[i].wait()
         second = lax.dot_general(
-            joined[...], held[i], (((1,), (1,)), ((), ())), preferred_element_type=F32
+            joined[...], dense[i][...], (((1,), (1,)), ((), ())), preferred_element_type=F32
         )
         half = second.shape[0] // 2
         real, imag = slice(0, half), slice(half, 2 * half)
-        first = pieces[2 * s]
-        change[i, real, :] = (TIME_STEP * first[imag, :].astype(F32) - half_square * second[real, :]).astype(BF16)
-        change[i, imag, :] = (-TIME_STEP * first[real, :].astype(F32) - half_square * second[imag, :]).astype(BF16)
+        other = first[i]
+        change[i, real, :] = (TIME_STEP * other[imag, :].astype(F32) - half_square * second[real, :]).astype(BF16)
+        change[i, imag, :] = (-TIME_STEP * other[real, :].astype(F32) - half_square * second[imag, :]).astype(BF16)
         for k, j, _, place in kept(pmask, info[0] ^ (2 * s), info[1] * jb, kb, jb):
             for part in range(2):
                 top = pl.multiple_of((2 * place + part) * wide, wide)
@@ -299,15 +296,16 @@
         [shape(wide, order)],
     )
 
-    done = (out_near, beside_y, own_core, joined)
-    beside, over, over_beside, out_near, beside_y = after(
-        done, beside, over, over_beside, out_near, beside_y
-    )
-    slot_2 = jnp.where(inner, over_beside, out_near)
-    out_far, slot_2_y, beside_core = along(over_beside, outward), swap_col(slot_2, 2), other_core(beside, beside_y)
     dense, first, first_x = [None] * zs, [None] * zs, [None] * zs
     dense[0] = spread(0, own, own_y, own_core)
     first[0] = multiply(dense[0])
+
+    done = (out_near, beside_y, first[0])
+    beside, over, over_beside, out_near, beside_y = after(
+        done, beside, over, over_beside, out_near, beside_y
+    )
+    slot_2 = jnp.where(inner, over_beside, out_near)
+    out_far, slot_2_y, beside_core = along(over_beside, outward), swap_col(slot_2, 2), other_core(beside, beside_y)
     first_x[0] = swap_row(first[0], 1)
     dense[1] = spread(1, beside, beside_y, beside_core)
     first[1] = multiply(dense[1])
@@ -326,24 +324,25 @@
     dense[3] = spread(3, slot_3, slot_3_y, slot_3_core)
     first[3] = multiply(dense[3])
     first_x[3] = swap_row(first[3], 1)
-    everything = [f for pair in zip(first, first_x) for f in pair]
+    (first_joined,) = call(
+        functools.partial(join_kernel, zs, side),
+        [info],
+        [f for pair in zip(first, first_x) for f in pair],
+        [shape(wide, order)],
+    )
+
     result = [None] * zs
-    for slots in ((3, 2, 1), (0,)):
-        count = len(slots)
+    for slots in ((3,), (2,), (1,), (0,)):
         outs = call(
             functools.partial(second_kernel, slots, cap, zs, kb, jb),
             [info, pmask],
-            everything,
-            [piece] * count,
+            [first_joined, *(dense[s] for s in slots), *(first[s] for s in slots)],
+            [piece] * len(slots),
             scratch=[
-                pltpu.VMEM((wide, order), BF16),
-                pltpu.VMEM((count, side, order), BF16),
-                pltpu.VMEM((count, wide, side), BF16),
-                pltpu.VMEM((count, 2 * (kb * jb + 1) * BLK // zs, BLK), BF16),
-                pltpu.SemaphoreType.DMA((count,)),
+                pltpu.VMEM((len(slots), wide, side), BF16),
+                pltpu.VMEM((len(slots), 2 * (kb * jb + 1) * BLK // zs, BLK), BF16),
             ],
-            flops=2 * side * order * wide * count,
-            left=[dense[s] for s in slots],
+            flops=2 * side * order * wide * len(slots),
         )
         for s, out in zip(slots, outs):
             result[s] = out if s == 0 else swap_row(out, 2 * s)

time: 181 us -> 169 us (0.934); the launches traced: 182 us -> 168 us
  Pallas kernels: 49.5 us -> 34.5 us
  waiting for transfers between devices: 62.5 us -> 73.4 us
  other arithmetic: 9.6 us -> 5.35 us
  local copies, waits for them, and re-layouts: 9.76 us -> 6.12 us
    pallas_call x15 -> x18, Pallas kernels: 49.5 us -> 34.5 us  [call(): pl.pallas_call(body, out_shape=tuple(outs), in_specs=[SMEM_SPEC] * len(sc...]
    ppermute x12, waiting for transfers between devices: 51.1 us -> 58.7 us  [swap_row(): return lax.ppermute(value, 'row', [(i, i ^ bits) for i in range(count)])]
    reduce_sum x2, other arithmetic: 3.15 us -> 0.43 us  [most(): mask.reshape(mask.shape[0] // kb, kb, mask.shape[1] // width, width)]
    unnamed x74 -> x30, local copies, waits for them, and re-layouts: 6.13 us -> 3.71 us
    ppermute x12, waiting for transfers between devices: 9 us -> 11.4 us  [swap_col(): return lax.ppermute(value, 'col', [(i, i ^ bits) for i in range(count)])]
  transfers between devices with their start and end apart: 32 -> 32, of which waited for: 15 -> 16; matrix products, arithmetic and copies ran while one was open for 6% -> 3% of each run, Pallas kernels for 12% -> 13%
where the time goes in v4:
time: 169 us; the launch traced here: 168 us
  waiting for transfers between devices  73.4 us (43%)
  starting transfers between devices  46.7 us (28%)
  Pallas kernels  34.5 us (20%)
  local copies, waits for them, and re-layouts  6.12 us (4%)
  other arithmetic  5.35 us (3%)
  between operations  1.77 us (1%)
    ppermute x12, waiting for transfers between devices, swap_row(): return lax.ppermute(value, 'row', [(i, i ^ bits) for i in range(count)])  58.7 us
    pallas_call x18, Pallas kernels, call(): pl.pallas_call(body, out_shape=tuple(outs), in_specs=[SMEM_SPEC] * len(sc...  34.5 us
    ppermute x12, starting transfers between devices, swap_row(): return lax.ppermute(value, 'row', [(i, i ^ bits) for i in range(count)])  24.4 us
    ppermute x12, waiting for transfers between devices, swap_col(): return lax.ppermute(value, 'col', [(i, i ^ bits) for i in range(count)])  11.4 us
    ppermute x2, starting transfers between devices, beyond(): lax.ppermute(lax.slice_in_dim(potential, last, None, axis=dim), axis, for...  8.5 us
    ppermute x12, starting transfers between devices, swap_col(): return lax.ppermute(value, 'col', [(i, i ^ bits) for i in range(count)])  7.04 us
    ppermute x4, starting transfers between devices, along(): lax.ppermute(value, 'row', [(2 * a + x, 2 * b + x) for a, b in pairs for...  4.23 us
    unnamed x30, local copies, waits for them, and re-layouts  3.71 us
  transfers between devices with their start and end apart: 32, of which 16 were waited for; matrix products, arithmetic and copies ran while one was open for 3% of the time, Pallas kernels for 13%

profile of v4, /device:TPU:0, one launch (start us, length us, event | category | flops | bytes accessed | tf_op | source)
XLA Modules:
  0.0 167.9 jit_solution(17302530027296497671)
XLA Ops:
  0.7 1.3 collective-permute-start.37
  2.0 5.5 %collective-permute-start.38 = (f32[1,4,512]{2,1,0:T(4,128)S(1)}, f32[1,4,512]{2,1,0:T(4,128)S(1)}, u32[]{:S(2)}, u32[]{:S(2)}) collective-permute-start(f32[1,4,512]{2,1,0:T(4,128)S(1)} %get-tuple-element.130), channel_id=1, source_target_pairs={{0,4},{4,8},{8,12},{12,16},{16,20},{20,24},{24,28},{1,5},{5,9},{9,... | collective-permute-start | bytes 24584 | tf_op jit(solution)/shard_map/ppermute | solution.py:201
  8.3 1.3 collective-permute-start.39
  9.6 3.0 %collective-permute-start.40 = (f32[2,1,512]{2,1,0:T(1,128)S(1)}, f32[2,1,512]{2,1,0:T(1,128)S(1)}, u32[]{:S(2)}, u32[]{:S(2)}) collective-permute-start(f32[2,1,512]{2,1,0:T(1,128)S(1)} %get-tuple-element.132), channel_id=1, source_target_pairs={{0,1},{1,2},{2,3},{4,5},{5,6},{6,7},{8,9},{9,10},{10,11},{12,13},{... | collective-permute-start | bytes 12296 | tf_op jit(solution)/shard_map/ppermute | solution.py:201
  12.8 1.8 %shard_map.64 = (bf16[1024,128]{1,0:T(8,128)(2,1)S(1)}, bf16[1024,128]{1,0:T(8,128)(2,1)S(1)}, bf16[1024,128]{1,0:T(8,128)(2,1)S(1)}, bf16[1024,128]{1,0:T(8,128)(2,1)S(1)}) custom-call(s32[2]{0:T(128)S(1)} %pad_add_fusion.1.info, s32[24,24]{1,0:T(8,128)} %pmask.13, bf16[2,384,768]{2,1,0:T(8,128)(2,1)} %p.3), custom_call_target="tpu_custom_call" | custom-call | bytes 2228224 | tf_op jit(solution)/shard_map/pallas_call | solution.py:24
  14.5 2.2 %collective-permute-start.32 = (bf16[1024,128]{1,0:T(8,128)(2,1)S(1)}, bf16[1024,128]{1,0:T(8,128)(2,1)S(1)}, u32[]{:S(2)}, u32[]{:S(2)}) collective-permute-start(bf16[1024,128]{1,0:T(8,128)(2,1)S(1)} %get-tuple-element.84), channel_id=1, source_target_pairs={{0,8},{4,12},{8,0},{12,4},{16,24},{20,28},{24,16},{28,20},{1,9},{5... | collective-permute-start | bytes 786440 | tf_op jit(solution)/shard_map/ppermute | solution.py:179
  16.7 2.6 %collective-permute-start.33 = (bf16[1024,128]{1,0:T(8,128)(2,1)S(1)}, bf16[1024,128]{1,0:T(8,128)(2,1)S(1)}, u32[]{:S(2)}, u32[]{:S(2)}) collective-permute-start(bf16[1024,128]{1,0:T(8,128)(2,1)S(1)} %get-tuple-element.85), channel_id=1, source_target_pairs={{0,16},{4,20},{8,24},{12,28},{16,0},{20,4},{24,8},{28,12},{1,17},{... | collective-permute-start | bytes 786440 | tf_op jit(solution)/shard_map/ppermute | solution.py:179
  21.0 2.9 %shard_map.66 = f32[384,128]{1,0:T(8,128)S(1)} custom-call(f32[2,4,512]{2,1,0:T(4,128)S(1)} %fusion.12.effective, bf16[2,4,384,512]{3,2,1,0:T(8,128)(2,1)} %basis.1), custom_call_target="tpu_custom_call" | custom-call | flops 402653184 | bytes 107479040 | tf_op jit(solution)/shard_map/pallas_call | solution.py:24
  23.9 4.7 %collective-permute-done.32.rest_1_ = bf16[1024,128]{1,0:T(8,128)(2,1)S(1)} collective-permute-done((bf16[1024,128]{1,0:T(8,128)(2,1)S(1)}, bf16[1024,128]{1,0:T(8,128)(2,1)S(1)}, u32[]{:S(2)}, u32[]{:S(2)}) %collective-permute-start.32) | collective-permute-done | bytes 262176 | tf_op jit(solution)/shard_map/ppermute | solution.py:179
  28.6 9.4 %collective-permute-done.33.rest_2_ = bf16[1024,128]{1,0:T(8,128)(2,1)S(1)} collective-permute-done((bf16[1024,128]{1,0:T(8,128)(2,1)S(1)}, bf16[1024,128]{1,0:T(8,128)(2,1)S(1)}, u32[]{:S(2)}, u32[]{:S(2)}) %collective-permute-start.33) | collective-permute-done | bytes 262176 | tf_op jit(solution)/shard_map/ppermute | solution.py:179
  38.2 1.6 collective-permute-start.42
  40.0 2.3 %collective-permute-done.42 = f32[96,128]{1,0:T(8,128)S(1)} collective-permute-done((f32[96,128]{1,0:T(8,128)S(1)}, f32[96,128]{1,0:T(8,128)S(1)}, u32[]{:S(2)}, u32[]{:S(2)}) %collective-permute-start.42) | collective-permute-done | bytes 49184 | tf_op jit(solution)/shard_map/ppermute | solution.py:184
  44.8 5.6 %collective-permute-start.44 = (bf16[1888,128]{1,0:T(8,128)(2,1)S(1)}, bf16[1888,128]{1,0:T(8,128)(2,1)S(1)}, u32[]{:S(2)}, u32[]{:S(2)}) collective-permute-start(bf16[1888,128]{1,0:T(8,128)(2,1)S(1)} %shard_map.67.rest_0_), channel_id=1, source_target_pairs={{0,8},{4,12},{8,0},{12,4},{16,24},{20,28},{24,16},{28,20},{1,9},{5... | collective-permute-start | bytes 1449992 | tf_op jit(solution)/shard_map/ppermute | solution.py:179
  52.2 2.5 %collective-permute-start.35 = (bf16[4096,128]{1,0:T(8,128)(2,1)S(1)}, bf16[4096,128]{1,0:T(8,128)(2,1)S(1)}, u32[]{:S(2)}, u32[]{:S(2)}) collective-permute-start(bf16[4096,128]{1,0:T(8,128)(2,1)S(1)} %pad_maximum_fusion.9), channel_id=1, source_target_pairs={{0,4},{4,0},{8,12},{12,8},{16,20},{20,16},{24,28},{28,24},{1,5},{5... | collective-permute-start | bytes 3145736 | tf_op jit(solution)/shard_map/ppermute | solution.py:179
  54.7 7.1 %collective-permute-done.44.rest_0_ = bf16[1888,128]{1,0:T(8,128)(2,1)S(1)} collective-permute-done((bf16[1888,128]{1,0:T(8,128)(2,1)S(1)}, bf16[1888,128]{1,0:T(8,128)(2,1)S(1)}, u32[]{:S(2)}, u32[]{:S(2)}) %collective-permute-start.44) | collective-permute-done | bytes 483360 | tf_op jit(solution)/shard_map/ppermute | solution.py:179
  61.9 2.2 %collective-permute-done.46.rest_1_ = bf16[1888,128]{1,0:T(8,128)(2,1)S(1)} collective-permute-done((bf16[1888,128]{1,0:T(8,128)(2,1)S(1)}, bf16[1888,128]{1,0:T(8,128)(2,1)S(1)}, u32[]{:S(2)}, u32[]{:S(2)}) %collective-permute-start.46) | collective-permute-done | bytes 483360 | tf_op jit(solution)/shard_map/ppermute | solution.py:184
  64.9 1.3 collective-permute-start.50
  67.2 10.4 %collective-permute-done.35.rest_4_ = bf16[4096,128]{1,0:T(8,128)(2,1)S(1)} collective-permute-done((bf16[4096,128]{1,0:T(8,128)(2,1)S(1)}, bf16[4096,128]{1,0:T(8,128)(2,1)S(1)}, u32[]{:S(2)}, u32[]{:S(2)}) %collective-permute-start.35) | collective-permute-done | bytes 1048608 | tf_op jit(solution)/shard_map/ppermute | solution.py:179
  77.6 1.9 %shard_map.65.joined = bf16[384,3072]{1,0:T(8,128)(2,1)S(1)} custom-call(s32[2]{0:T(128)S(1)} %pad_add_fusion.1.info, s32[24,24]{1,0:T(8,128)S(1)} %copy-done.14, bf16[1024,128]{1,0:T(8,128)(2,1)S(1)} %get-tuple-element.83.rest_0_, bf16[1024,128]{1,0:T(8,128)(2,1)S(1)} %collective-permute-done.32.rest_1_, bf16[1024,128]{1,0:T(8,128)(2,1)S(1)} %copy-done.11, ...), custom_call_target="tpu_custom_call" | custom-call | bytes 4456448 | tf_op jit(solution)/shard_map/pallas_call | solution.py:24
  79.6 1.8 %shard_map.68.dense.rest_0_ = bf16[384,3072]{1,0:T(8,128)(2,1)S(1)} custom-call(s32[2]{0:T(128)S(1)} %pad_add_fusion.1.info, s32[24,24]{1,0:T(8,128)} %hmask.9, bf16[1888,128]{1,0:T(8,128)(2,1)S(1)} %shard_map.67.rest_0_, bf16[1888,128]{1,0:T(8,128)(2,1)S(1)} %collective-permute-done.46.rest_1_, bf16[3776,128]{1,0:T(8,128)(2,1)S(1)} %collective-permute-done.47.rest_2_), custom_call_target="tpu_custom_call" | custom-call | bytes 4292608 | tf_op jit(solution)/shard_map/pallas_call | solution.py:24
  81.4 1.4 shard_map.69.rest_0_.rest_1_
  87.2 1.6 collective-permute-start.54
  88.8 1.8 %collective-permute-start.48 = (bf16[384,384]{1,0:T(8,128)(2,1)S(1)}, bf16[384,384]{1,0:T(8,128)(2,1)S(1)}, u32[]{:S(2)}, u32[]{:S(2)}) collective-permute-start(bf16[384,384]{1,0:T(8,128)(2,1)S(1)} %shard_map.69.rest_0_.rest_1_), channel_id=1, source_target_pairs={{0,4},{4,0},{8,12},{12,8},{16,20},{20,16},{24,28},{28,24},{1,5},{5... | collective-permute-start | bytes 884744 | tf_op jit(solution)/shard_map/ppermute | solution.py:179
  91.6 2.2 %shard_map.70.dense.rest_0_ = bf16[384,3072]{1,0:T(8,128)(2,1)S(1)} custom-call(s32[2]{0:T(128)S(1)} %pad_add_fusion.1.info, s32[24,24]{1,0:T(8,128)} %hmask.9, bf16[1888,128]{1,0:T(8,128)(2,1)S(1)} %collective-permute-done.44.rest_0_, bf16[1888,128]{1,0:T(8,128)(2,1)S(1)} %copy-done.9, bf16[3776,128]{1,0:T(8,128)(2,1)} %collective-permute-done.52.rest_2_), custom_call_target="tpu_custom_call" | custom-call | bytes 4292608 | tf_op jit(solution)/shard_map/pallas_call | solution.py:24
  93.8 1.4 shard_map.71.rest_2_.rest_1_
  95.2 2.8 %collective-permute-done.48.rest_1_ = bf16[384,384]{1,0:T(8,128)(2,1)S(1)} collective-permute-done((bf16[384,384]{1,0:T(8,128)(2,1)S(1)}, bf16[384,384]{1,0:T(8,128)(2,1)S(1)}, u32[]{:S(2)}, u32[]{:S(2)}) %collective-permute-start.48) | collective-permute-done | bytes 294944 | tf_op jit(solution)/shard_map/ppermute | solution.py:179
  98.0 1.6 collective-permute-done.55.rest_1_
  99.6 3.4 %collective-permute-done.54 = bf16[1888,128]{1,0:T(8,128)(2,1)S(1)} collective-permute-done((bf16[1888,128]{1,0:T(8,128)(2,1)}, bf16[1888,128]{1,0:T(8,128)(2,1)S(1)}, u32[]{:S(2)}, u32[]{:S(2)}) %collective-permute-start.54) | collective-permute-done | bytes 483360 | tf_op jit(solution)/shard_map/ppermute | solution.py:188
  104.2 1.7 %collective-permute-start.53 = (bf16[384,384]{1,0:T(8,128)(2,1)S(1)}, bf16[384,384]{1,0:T(8,128)(2,1)S(1)}, u32[]{:S(2)}, u32[]{:S(2)}) collective-permute-start(bf16[384,384]{1,0:T(8,128)(2,1)S(1)} %shard_map.71.rest_2_.rest_1_), channel_id=1, source_target_pairs={{0,4},{4,0},{8,12},{12,8},{16,20},{20,16},{24,28},{28,24},{1,5},{5... | collective-permute-start | bytes 884744 | tf_op jit(solution)/shard_map/ppermute | solution.py:179
  105.9 1.8 %shard_map.72.dense.rest_0_ = bf16[384,3072]{1,0:T(8,128)(2,1)S(1)} custom-call(s32[2]{0:T(128)S(1)} %pad_add_fusion.1.info, s32[24,24]{1,0:T(8,128)} %hmask.9, bf16[1888,128]{1,0:T(8,128)(2,1)S(1)} %broadcast_select_fusion.3.rest_0_, bf16[1888,128]{1,0:T(8,128)(2,1)S(1)} %collective-permute-done.55.rest_1_, ...), custom_call_target="tpu_custom_call" | custom-call | bytes 4292608 | tf_op jit(solution)/shard_map/pallas_call | solution.py:24
  107.7 1.4 shard_map.73.rest_4_.rest_1_
  109.1 4.1 %collective-permute-done.53.rest_3_ = bf16[384,384]{1,0:T(8,128)(2,1)S(1)} collective-permute-done((bf16[384,384]{1,0:T(8,128)(2,1)S(1)}, bf16[384,384]{1,0:T(8,128)(2,1)S(1)}, u32[]{:S(2)}, u32[]{:S(2)}) %collective-permute-start.53) | collective-permute-done | bytes 294944 | tf_op jit(solution)/shard_map/ppermute | solution.py:179
  113.3 3.4 %collective-permute-done.58.rest_1_ = bf16[1888,128]{1,0:T(8,128)(2,1)S(1)} collective-permute-done((bf16[1888,128]{1,0:T(8,128)(2,1)S(1)}, bf16[1888,128]{1,0:T(8,128)(2,1)S(1)}, u32[]{:S(2)}, u32[]{:S(2)}) %collective-permute-start.58) | collective-permute-done | bytes 483360 | tf_op jit(solution)/shard_map/ppermute | solution.py:184
  116.8 1.8 %collective-permute-start.57 = (bf16[384,384]{1,0:T(8,128)(2,1)S(1)}, bf16[384,384]{1,0:T(8,128)(2,1)S(1)}, u32[]{:S(2)}, u32[]{:S(2)}) collective-permute-start(bf16[384,384]{1,0:T(8,128)(2,1)S(1)} %shard_map.73.rest_4_.rest_1_), channel_id=1, source_target_pairs={{0,4},{4,0},{8,12},{12,8},{16,20},{20,16},{24,28},{28,24},{1,5},{5... | collective-permute-start | bytes 884744 | tf_op jit(solution)/shard_map/ppermute | solution.py:179
  119.3 1.8 %shard_map.74.dense.rest_0_ = bf16[384,3072]{1,0:T(8,128)(2,1)S(1)} custom-call(s32[2]{0:T(128)S(1)} %pad_add_fusion.1.info, s32[24,24]{1,0:T(8,128)} %hmask.9, bf16[1888,128]{1,0:T(8,128)(2,1)S(1)} %broadcast_select_fusion.2.rest_0_, bf16[1888,128]{1,0:T(8,128)(2,1)S(1)} %collective-permute-done.58.rest_1_, ...), custom_call_target="tpu_custom_call" | custom-call | bytes 4292608 | tf_op jit(solution)/shard_map/pallas_call | solution.py:24
  121.2 1.4 shard_map.75.rest_6_.rest_1_
  122.6 1.8 %collective-permute-start.60 = (bf16[384,384]{1,0:T(8,128)(2,1)S(1)}, bf16[384,384]{1,0:T(8,128)(2,1)S(1)}, u32[]{:S(2)}, u32[]{:S(2)}) collective-permute-start(bf16[384,384]{1,0:T(8,128)(2,1)S(1)} %shard_map.75.rest_6_.rest_1_), channel_id=1, source_target_pairs={{0,4},{4,0},{8,12},{12,8},{16,20},{20,16},{24,28},{28,24},{1,5},{5... | collective-permute-start | bytes 884744 | tf_op jit(solution)/shard_map/ppermute | solution.py:179
  124.4 2.3 %collective-permute-done.57.rest_5_ = bf16[384,384]{1,0:T(8,128)(2,1)S(1)} collective-permute-done((bf16[384,384]{1,0:T(8,128)(2,1)S(1)}, bf16[384,384]{1,0:T(8,128)(2,1)S(1)}, u32[]{:S(2)}, u32[]{:S(2)}) %collective-permute-start.57) | collective-permute-done | bytes 294944 | tf_op jit(solution)/shard_map/ppermute | solution.py:179
  126.7 5.9 %collective-permute-done.60.rest_7_ = bf16[384,384]{1,0:T(8,128)(2,1)S(1)} collective-permute-done((bf16[384,384]{1,0:T(8,128)(2,1)S(1)}, bf16[384,384]{1,0:T(8,128)(2,1)S(1)}, u32[]{:S(2)}, u32[]{:S(2)}) %collective-permute-start.60) | collective-permute-done | bytes 294944 | tf_op jit(solution)/shard_map/ppermute | solution.py:179
  133.3 2.9 %shard_map.80 = bf16[1024,128]{1,0:T(8,128)(2,1)} custom-call(s32[2]{0:T(128)S(1)} %pad_add_fusion.1.info, s32[24,24]{1,0:T(8,128)S(1)} %copy-done.14, bf16[384,3072]{1,0:T(8,128)(2,1)S(1)} %shard_map.76.joined, bf16[384,3072]{1,0:T(8,128)(2,1)S(1)} %shard_map.74.dense.rest_0_, bf16[384,384]{1,0:T(8,128)(2,1)S(1)} %shard_map.75.rest_6_.rest_1_), custom_call_target="tpu_custom_call" | custom-call | flops 905969664 | bytes 5275648 | tf_op jit(solution)/shard_map/pallas_call | solution.py:24
  136.3 2.2 %shard_map.79 = bf16[1024,128]{1,0:T(8,128)(2,1)S(1)} custom-call(s32[2]{0:T(128)S(1)} %pad_add_fusion.1.info, s32[24,24]{1,0:T(8,128)S(1)} %copy-done.14, bf16[384,3072]{1,0:T(8,128)(2,1)S(1)} %shard_map.76.joined, bf16[384,3072]{1,0:T(8,128)(2,1)S(1)} %shard_map.72.dense.rest_0_, bf16[384,384]{1,0:T(8,128)(2,1)S(1)} %shard_map.73.rest_4_.rest_1_), custom_call_target="tpu_custom_call" | custom-call | flops 905969664 | bytes 5275648 | tf_op jit(solution)/shard_map/pallas_call | solution.py:24
  138.5 2.2 %shard_map.78 = bf16[1024,128]{1,0:T(8,128)(2,1)S(1)} custom-call(s32[2]{0:T(128)S(1)} %pad_add_fusion.1.info, s32[24,24]{1,0:T(8,128)S(1)} %copy-done.14, bf16[384,3072]{1,0:T(8,128)(2,1)S(1)} %shard_map.76.joined, bf16[384,3072]{1,0:T(8,128)(2,1)S(1)} %shard_map.70.dense.rest_0_, bf16[384,384]{1,0:T(8,128)(2,1)S(1)} %shard_map.71.rest_2_.rest_1_), custom_call_target="tpu_custom_call" | custom-call | flops 905969664 | bytes 5275648 | tf_op jit(solution)/shard_map/pallas_call | solution.py:24
  140.7 2.1 %collective-permute-start.63 = (bf16[1024,128]{1,0:T(8,128)(2,1)}, bf16[1024,128]{1,0:T(8,128)(2,1)S(1)}, u32[]{:S(2)}, u32[]{:S(2)}) collective-permute-start(bf16[1024,128]{1,0:T(8,128)(2,1)} %shard_map.80), channel_id=1, source_target_pairs={{0,24},{4,28},{8,16},{12,20},{16,8},{20,12},{24,0},{28,4},{1,25},{... | collective-permute-start | bytes 786440 | tf_op jit(solution)/shard_map/ppermute | solution.py:179
  142.8 2.3 %collective-permute-start.61 = (bf16[1024,128]{1,0:T(8,128)(2,1)S(1)}, bf16[1024,128]{1,0:T(8,128)(2,1)}, u32[]{:S(2)}, u32[]{:S(2)}) collective-permute-start(bf16[1024,128]{1,0:T(8,128)(2,1)S(1)} %shard_map.78), channel_id=1, source_target_pairs={{0,8},{4,12},{8,0},{12,4},{16,24},{20,28},{24,16},{28,20},{1,9},{5... | collective-permute-start | bytes 786440 | tf_op jit(solution)/shard_map/ppermute | solution.py:179
  149.1 1.7 copy-done.7
  150.7 2.2 %shard_map.77.rest_0_ = bf16[1024,128]{1,0:T(8,128)(2,1)S(1)} custom-call(s32[2]{0:T(128)S(1)} %pad_add_fusion.1.info, s32[24,24]{1,0:T(8,128)S(1)} %copy-done.14, bf16[384,3072]{1,0:T(8,128)(2,1)S(1)} %shard_map.76.joined, bf16[384,3072]{1,0:T(8,128)(2,1)S(1)} %copy-done.7, bf16[384,384]{1,0:T(8,128)(2,1)S(1)} %shard_map.69.rest_0_.rest_1_), custom_call_target="tpu_custom_call" | custom-call | flops 905969664 | bytes 5275648 | tf_op jit(solution)/shard_map/pallas_call | solution.py:24
  153.0 11.9 %collective-permute-done.62.rest_2_ = bf16[1024,128]{1,0:T(8,128)(2,1)} collective-permute-done((bf16[1024,128]{1,0:T(8,128)(2,1)S(1)}, bf16[1024,128]{1,0:T(8,128)(2,1)}, u32[]{:S(2)}, u32[]{:S(2)}) %collective-permute-start.62) | collective-permute-done | bytes 262176 | tf_op jit(solution)/shard_map/ppermute | solution.py:179
  164.9 3.0 %shard_map.81 = bf16[2,384,768]{2,1,0:T(8,128)(2,1)} custom-call(s32[2]{0:T(128)S(1)} %pad_add_fusion.1.info, s32[24,24]{1,0:T(8,128)S(1)} %copy-done.14, bf16[2,384,768]{2,1,0:T(8,128)(2,1)} %p.3, bf16[1024,128]{1,0:T(8,128)(2,1)S(1)} %shard_map.77.rest_0_, bf16[1024,128]{1,0:T(8,128)(2,1)} %collective-permute-done.61.rest_1_, ...), custom_call_target="tpu_custom_call" | custom-call | bytes 3407872 | tf_op jit(solution)/shard_map/pallas_call | solution.py:24
  (84 shorter events, 20.6 us)
Async XLA Ops:
  0.7 18.6 %collective-permute-start.37 = (f32[1,4,512]{2,1,0:T(4,128)S(1)}, f32[1,4,512]{2,1,0:T(4,128)S(1)}, u32[]{:S(2)}, u32[]{:S(2)}) collective-permute-start(f32[1,4,512]{2,1,0:T(4,128)S(1)} %get-tuple-element.129), channel_id=1, source_target_pairs={{4,0},{8,4},{12,8},{16,12},{20,16},{24,20},{28,24},{5,1},{9,5},{13... | collective-permute-start | bytes 24584 | tf_op jit(solution)/shard_map/ppermute | solution.py:202
  2.0 17.9 %collective-permute-start.38 = (f32[1,4,512]{2,1,0:T(4,128)S(1)}, f32[1,4,512]{2,1,0:T(4,128)S(1)}, u32[]{:S(2)}, u32[]{:S(2)}) collective-permute-start(f32[1,4,512]{2,1,0:T(4,128)S(1)} %get-tuple-element.130), channel_id=1, source_target_pairs={{0,4},{4,8},{8,12},{12,16},{16,20},{20,24},{24,28},{1,5},{5,9},{9,... | collective-permute-start | bytes 24584 | tf_op jit(solution)/shard_map/ppermute | solution.py:201
  8.3 8.4 %collective-permute-start.39 = (f32[2,1,512]{2,1,0:T(1,128)S(1)}, f32[2,1,512]{2,1,0:T(1,128)S(1)}, u32[]{:S(2)}, u32[]{:S(2)}) collective-permute-start(f32[2,1,512]{2,1,0:T(1,128)S(1)} %get-tuple-element.131), channel_id=1, source_target_pairs={{1,0},{2,1},{3,2},{5,4},{6,5},{7,6},{9,8},{10,9},{11,10},{13,12},{... | collective-permute-start | bytes 12296 | tf_op jit(solution)/shard_map/ppermute | solution.py:202
  9.6 9.7 %collective-permute-start.40 = (f32[2,1,512]{2,1,0:T(1,128)S(1)}, f32[2,1,512]{2,1,0:T(1,128)S(1)}, u32[]{:S(2)}, u32[]{:S(2)}) collective-permute-start(f32[2,1,512]{2,1,0:T(1,128)S(1)} %get-tuple-element.132), channel_id=1, source_target_pairs={{0,1},{1,2},{2,3},{4,5},{5,6},{6,7},{8,9},{9,10},{10,11},{12,13},{... | collective-permute-start | bytes 12296 | tf_op jit(solution)/shard_map/ppermute | solution.py:201
  14.5 14.1 %collective-permute-start.32 = (bf16[1024,128]{1,0:T(8,128)(2,1)S(1)}, bf16[1024,128]{1,0:T(8,128)(2,1)S(1)}, u32[]{:S(2)}, u32[]{:S(2)}) collective-permute-start(bf16[1024,128]{1,0:T(8,128)(2,1)S(1)} %get-tuple-element.84), channel_id=1, source_target_pairs={{0,8},{4,12},{8,0},{12,4},{16,24},{20,28},{24,16},{28,20},{1,9},{5... | collective-permute-start | bytes 786440 | tf_op jit(solution)/shard_map/ppermute | solution.py:179
  16.7 21.4 %collective-permute-start.33 = (bf16[1024,128]{1,0:T(8,128)(2,1)S(1)}, bf16[1024,128]{1,0:T(8,128)(2,1)S(1)}, u32[]{:S(2)}, u32[]{:S(2)}) collective-permute-start(bf16[1024,128]{1,0:T(8,128)(2,1)S(1)} %get-tuple-element.85), channel_id=1, source_target_pairs={{0,16},{4,20},{8,24},{12,28},{16,0},{20,4},{24,8},{28,12},{1,17},{... | collective-permute-start | bytes 786440 | tf_op jit(solution)/shard_map/ppermute | solution.py:179
  19.3 18.8 %collective-permute-start.34 = (bf16[1024,128]{1,0:T(8,128)(2,1)S(1)}, bf16[1024,128]{1,0:T(8,128)(2,1)S(1)}, u32[]{:S(2)}, u32[]{:S(2)}) collective-permute-start(bf16[1024,128]{1,0:T(8,128)(2,1)S(1)} %get-tuple-element.86), channel_id=1, source_target_pairs={{0,24},{4,28},{8,16},{12,20},{16,8},{20,12},{24,0},{28,4},{1,25},{... | collective-permute-start | bytes 786440 | tf_op jit(solution)/shard_map/ppermute | solution.py:179
  19.3 24.2 %collective-permute-start.36 = (bf16[384,768]{1,0:T(8,128)(2,1)}, bf16[384,768]{1,0:T(8,128)(2,1)S(1)}, u32[]{:S(2)}, u32[]{:S(2)}) collective-permute-start(bf16[384,768]{1,0:T(8,128)(2,1)} %h.1), channel_id=1, source_target_pairs={{0,1},{1,0},{2,3},{3,2},{4,5},{5,4},{6,7},{7,6},{8,9},{9,8},{10,11... | collective-permute-start | bytes 1769480 | tf_op jit(solution)/shard_map/ppermute | solution.py:184
  21.0 22.5 %copy-start.15 = (bf16[384,768]{1,0:T(8,128)(2,1)S(1)}, bf16[384,768]{1,0:T(8,128)(2,1)}, u32[]{:S(2)}) copy-start(bf16[384,768]{1,0:T(8,128)(2,1)} %h.1) | copy-start | bytes 1769476
  38.1 14.2 %copy-start.10 = (bf16[1024,128]{1,0:T(8,128)(2,1)}, bf16[1024,128]{1,0:T(8,128)(2,1)S(1)}, u32[]{:S(2)}) copy-start(bf16[1024,128]{1,0:T(8,128)(2,1)S(1)} %collective-permute-done.33.rest_2_) | copy-start | bytes 786436
  38.1 14.2 %copy-start.12 = (bf16[1024,128]{1,0:T(8,128)(2,1)}, bf16[1024,128]{1,0:T(8,128)(2,1)S(1)}, u32[]{:S(2)}) copy-start(bf16[1024,128]{1,0:T(8,128)(2,1)S(1)} %collective-permute-done.34.rest_3_) | copy-start | bytes 786436
  38.1 1.9 %collective-permute-start.41 = (f32[96,128]{1,0:T(8,128)S(1)}, f32[96,128]{1,0:T(8,128)S(1)}, u32[]{:S(2)}, u32[]{:S(2)}) collective-permute-start(f32[96,128]{1,0:T(8,128)S(1)} %get-tuple-element.126), channel_id=1, source_target_pairs={{0,1},{1,0},{2,3},{3,2},{4,5},{5,4},{6,7},{7,6},{8,9},{9,8},{10,11... | collective-permute-start | bytes 147464 | tf_op jit(solution)/shard_map/ppermute | solution.py:184
  38.2 4.2 %collective-permute-start.42 = (f32[96,128]{1,0:T(8,128)S(1)}, f32[96,128]{1,0:T(8,128)S(1)}, u32[]{:S(2)}, u32[]{:S(2)}) collective-permute-start(f32[96,128]{1,0:T(8,128)S(1)} %get-tuple-element.128), channel_id=1, source_target_pairs={{0,2},{1,3},{2,0},{3,1},{4,6},{5,7},{6,4},{7,5},{8,10},{9,11},{10,... | collective-permute-start | bytes 147464 | tf_op jit(solution)/shard_map/ppermute | solution.py:184
  39.8 3.7 %collective-permute-start.43 = (f32[96,128]{1,0:T(8,128)S(1)}, f32[96,128]{1,0:T(8,128)S(1)}, u32[]{:S(2)}, u32[]{:S(2)}) collective-permute-start(f32[96,128]{1,0:T(8,128)S(1)} %get-tuple-element.127), channel_id=1, source_target_pairs={{0,3},{1,2},{2,1},{3,0},{4,7},{5,6},{6,5},{7,4},{8,11},{9,10},{10,... | collective-permute-start | bytes 147464 | tf_op jit(solution)/shard_map/ppermute | solution.py:184
  44.8 17.1 %collective-permute-start.44 = (bf16[1888,128]{1,0:T(8,128)(2,1)S(1)}, bf16[1888,128]{1,0:T(8,128)(2,1)S(1)}, u32[]{:S(2)}, u32[]{:S(2)}) collective-permute-start(bf16[1888,128]{1,0:T(8,128)(2,1)S(1)} %shard_map.67.rest_0_), channel_id=1, source_target_pairs={{0,8},{4,12},{8,0},{12,4},{16,24},{20,28},{24,16},{28,20},{1,9},{5... | collective-permute-start | bytes 1449992 | tf_op jit(solution)/shard_map/ppermute | solution.py:179
  50.4 11.5 %collective-permute-start.45 = (bf16[1888,128]{1,0:T(8,128)(2,1)S(1)}, bf16[1888,128]{1,0:T(8,128)(2,1)S(1)}, u32[]{:S(2)}, u32[]{:S(2)}) collective-permute-start(bf16[1888,128]{1,0:T(8,128)(2,1)S(1)} %shard_map.67.rest_0_), channel_id=1, source_target_pairs={{8,16},{12,20},{16,8},{20,12},{9,17},{13,21},{17,9},{21,13},{10,18... | collective-permute-start | bytes 1449992 | tf_op jit(solution)/shard_map/ppermute | solution.py:188
  51.1 13.0 %collective-permute-start.46 = (bf16[1888,128]{1,0:T(8,128)(2,1)S(1)}, bf16[1888,128]{1,0:T(8,128)(2,1)S(1)}, u32[]{:S(2)}, u32[]{:S(2)}) collective-permute-start(bf16[1888,128]{1,0:T(8,128)(2,1)S(1)} %shard_map.67.rest_0_), channel_id=1, source_target_pairs={{0,2},{1,3},{2,0},{3,1},{4,6},{5,7},{6,4},{7,5},{8,10},{9,11},{10,... | collective-permute-start | bytes 1449992 | tf_op jit(solution)/shard_map/ppermute | solution.py:184
  52.1 25.5 %copy-start.14 = (s32[24,24]{1,0:T(8,128)S(1)}, s32[24,24]{1,0:T(8,128)}, u32[]{:S(2)}) copy-start(s32[24,24]{1,0:T(8,128)} %pmask.13) | copy-start | bytes 6916
  52.2 25.4 %collective-permute-start.35 = (bf16[4096,128]{1,0:T(8,128)(2,1)S(1)}, bf16[4096,128]{1,0:T(8,128)(2,1)S(1)}, u32[]{:S(2)}, u32[]{:S(2)}) collective-permute-start(bf16[4096,128]{1,0:T(8,128)(2,1)S(1)} %pad_maximum_fusion.9), channel_id=1, source_target_pairs={{0,4},{4,0},{8,12},{12,8},{16,20},{20,16},{24,28},{28,24},{1,5},{5... | collective-permute-start | bytes 3145736 | tf_op jit(solution)/shard_map/ppermute | solution.py:179
  54.7 22.9 %copy-start.11 = (bf16[1024,128]{1,0:T(8,128)(2,1)S(1)}, bf16[1024,128]{1,0:T(8,128)(2,1)}, u32[]{:S(2)}) copy-start(bf16[1024,128]{1,0:T(8,128)(2,1)} %copy-done.10) | copy-start | bytes 786436
  54.7 22.9 %copy-start.13 = (bf16[1024,128]{1,0:T(8,128)(2,1)S(1)}, bf16[1024,128]{1,0:T(8,128)(2,1)}, u32[]{:S(2)}) copy-start(bf16[1024,128]{1,0:T(8,128)(2,1)} %copy-done.12) | copy-start | bytes 786436
  61.9 17.7 %copy-start.18 = (bf16[1888,128]{1,0:T(8,128)(2,1)}, bf16[1888,128]{1,0:T(8,128)(2,1)S(1)}, u32[]{:S(2)}) copy-start(bf16[1888,128]{1,0:T(8,128)(2,1)S(1)} %collective-permute-done.45) | copy-start | bytes 1449988
  64.1 15.4 %collective-permute-start.47 = (bf16[3776,128]{1,0:T(8,128)(2,1)S(1)}, bf16[3776,128]{1,0:T(8,128)(2,1)S(1)}, u32[]{:S(2)}, u32[]{:S(2)}) collective-permute-start(bf16[3776,128]{1,0:T(8,128)(2,1)S(1)} %pad_maximum_fusion.10), channel_id=1, source_target_pairs={{0,1},{1,0},{2,3},{3,2},{4,5},{5,4},{6,7},{7,6},{8,9},{9,8},{10,11... | collective-permute-start | bytes 2899976 | tf_op jit(solution)/shard_map/ppermute | solution.py:184
  64.2 18.7 %collective-permute-start.49 = (bf16[1888,128]{1,0:T(8,128)(2,1)S(1)}, bf16[1888,128]{1,0:T(8,128)(2,1)S(1)}, u32[]{:S(2)}, u32[]{:S(2)}) collective-permute-start(bf16[1888,128]{1,0:T(8,128)(2,1)S(1)} %collective-permute-done.44.rest_0_), channel_id=1, source_target_pairs={{8,16},{12,20},{16,8},{20,12},{9,17},{13,21},{17,9},{21,13},{10,18... | collective-permute-start | bytes 1449992 | tf_op jit(solution)/shard_map/ppermute | solution.py:188
  64.9 18.0 %collective-permute-start.50 = (bf16[1888,128]{1,0:T(8,128)(2,1)S(1)}, bf16[1888,128]{1,0:T(8,128)(2,1)S(1)}, u32[]{:S(2)}, u32[]{:S(2)}) collective-permute-start(bf16[1888,128]{1,0:T(8,128)(2,1)S(1)} %collective-permute-done.45), channel_id=1, source_target_pairs={{8,0},{12,4},{16,24},{20,28},{9,1},{13,5},{17,25},{21,29},{10,2},{... | collective-permute-start | bytes 1449992 | tf_op jit(solution)/shard_map/ppermute | solution.py:188
  66.2 16.7 %collective-permute-start.51 = (bf16[1888,128]{1,0:T(8,128)(2,1)S(1)}, bf16[1888,128]{1,0:T(8,128)(2,1)S(1)}, u32[]{:S(2)}, u32[]{:S(2)}) collective-permute-start(bf16[1888,128]{1,0:T(8,128)(2,1)S(1)} %collective-permute-done.44.rest_0_), channel_id=1, source_target_pairs={{0,2},{1,3},{2,0},{3,1},{4,6},{5,7},{6,4},{7,5},{8,10},{9,11},{10,... | collective-permute-start | bytes 1449992 | tf_op jit(solution)/shard_map/ppermute | solution.py:184
  81.4 1.4 copy-start.6
  82.9 1.1 copy-start.20
  82.9 1.3 copy-start.21
  84.2 0.8 copy-start.8
  85.0 5.6 %collective-permute-start.52 = (bf16[3776,128]{1,0:T(8,128)(2,1)}, bf16[3776,128]{1,0:T(8,128)(2,1)}, u32[]{:S(2)}, u32[]{:S(2)}) collective-permute-start(bf16[3776,128]{1,0:T(8,128)(2,1)} %pad_maximum_fusion.11), channel_id=1, source_target_pairs={{0,1},{1,0},{2,3},{3,2},{4,5},{5,4},{6,7},{7,6},{8,9},{9,8},{10,11... | collective-permute-start | bytes 2899976 | tf_op jit(solution)/shard_map/ppermute | solution.py:184
  86.1 13.5 %collective-permute-start.55 = (bf16[1888,128]{1,0:T(8,128)(2,1)S(1)}, bf16[1888,128]{1,0:T(8,128)(2,1)S(1)}, u32[]{:S(2)}, u32[]{:S(2)}) collective-permute-start(bf16[1888,128]{1,0:T(8,128)(2,1)S(1)} %broadcast_select_fusion.3.rest_0_), channel_id=1, source_target_pairs={{0,2},{1,3},{2,0},{3,1},{4,6},{5,7},{6,4},{7,5},{8,10},{9,11},{10,... | collective-permute-start | bytes 1449992 | tf_op jit(solution)/shard_map/ppermute | solution.py:184
  87.2 15.7 %collective-permute-start.54 = (bf16[1888,128]{1,0:T(8,128)(2,1)}, bf16[1888,128]{1,0:T(8,128)(2,1)S(1)}, u32[]{:S(2)}, u32[]{:S(2)}) collective-permute-start(bf16[1888,128]{1,0:T(8,128)(2,1)} %copy-done.20), channel_id=1, source_target_pairs={{8,0},{12,4},{16,24},{20,28},{9,1},{13,5},{17,25},{21,29},{10,2},{... | collective-permute-start | bytes 1449992 | tf_op jit(solution)/shard_map/ppermute | solution.py:188
  88.8 9.2 %collective-permute-start.48 = (bf16[384,384]{1,0:T(8,128)(2,1)S(1)}, bf16[384,384]{1,0:T(8,128)(2,1)S(1)}, u32[]{:S(2)}, u32[]{:S(2)}) collective-permute-start(bf16[384,384]{1,0:T(8,128)(2,1)S(1)} %shard_map.69.rest_0_.rest_1_), channel_id=1, source_target_pairs={{0,4},{4,0},{8,12},{12,8},{16,20},{20,16},{24,28},{28,24},{1,5},{5... | collective-permute-start | bytes 884744 | tf_op jit(solution)/shard_map/ppermute | solution.py:179
  90.6 1.0 copy-start.9
  95.2 7.9 %copy-start.19 = (bf16[1888,128]{1,0:T(8,128)(2,1)S(1)}, bf16[1888,128]{1,0:T(8,128)(2,1)}, u32[]{:S(2)}) copy-start(bf16[1888,128]{1,0:T(8,128)(2,1)} %copy-done.18) | copy-start | bytes 1449988
  103.0 2.9 %collective-permute-start.56 = (bf16[3776,128]{1,0:T(8,128)(2,1)S(1)}, bf16[3776,128]{1,0:T(8,128)(2,1)S(1)}, u32[]{:S(2)}, u32[]{:S(2)}) collective-permute-start(bf16[3776,128]{1,0:T(8,128)(2,1)S(1)} %pad_maximum_fusion.12), channel_id=1, source_target_pairs={{0,1},{1,0},{2,3},{3,2},{4,5},{5,4},{6,7},{7,6},{8,9},{9,8},{10,11... | collective-permute-start | bytes 2899976 | tf_op jit(solution)/shard_map/ppermute | solution.py:184
  103.2 13.5 %collective-permute-start.58 = (bf16[1888,128]{1,0:T(8,128)(2,1)S(1)}, bf16[1888,128]{1,0:T(8,128)(2,1)S(1)}, u32[]{:S(2)}, u32[]{:S(2)}) collective-permute-start(bf16[1888,128]{1,0:T(8,128)(2,1)S(1)} %broadcast_select_fusion.2.rest_0_), channel_id=1, source_target_pairs={{0,2},{1,3},{2,0},{3,1},{4,6},{5,7},{6,4},{7,5},{8,10},{9,11},{10,... | collective-permute-start | bytes 1449992 | tf_op jit(solution)/shard_map/ppermute | solution.py:184
  104.2 9.1 %collective-permute-start.53 = (bf16[384,384]{1,0:T(8,128)(2,1)S(1)}, bf16[384,384]{1,0:T(8,128)(2,1)S(1)}, u32[]{:S(2)}, u32[]{:S(2)}) collective-permute-start(bf16[384,384]{1,0:T(8,128)(2,1)S(1)} %shard_map.71.rest_2_.rest_1_), channel_id=1, source_target_pairs={{0,4},{4,0},{8,12},{12,8},{16,20},{20,16},{24,28},{28,24},{1,5},{5... | collective-permute-start | bytes 884744 | tf_op jit(solution)/shard_map/ppermute | solution.py:179
  116.7 2.6 %collective-permute-start.59 = (bf16[3776,128]{1,0:T(8,128)(2,1)S(1)}, bf16[3776,128]{1,0:T(8,128)(2,1)S(1)}, u32[]{:S(2)}, u32[]{:S(2)}) collective-permute-start(bf16[3776,128]{1,0:T(8,128)(2,1)S(1)} %pad_maximum_fusion.13), channel_id=1, source_target_pairs={{0,1},{1,0},{2,3},{3,2},{4,5},{5,4},{6,7},{7,6},{8,9},{9,8},{10,11... | collective-permute-start | bytes 2899976 | tf_op jit(solution)/shard_map/ppermute | solution.py:184
  116.8 9.9 %collective-permute-start.57 = (bf16[384,384]{1,0:T(8,128)(2,1)S(1)}, bf16[384,384]{1,0:T(8,128)(2,1)S(1)}, u32[]{:S(2)}, u32[]{:S(2)}) collective-permute-start(bf16[384,384]{1,0:T(8,128)(2,1)S(1)} %shard_map.73.rest_4_.rest_1_), channel_id=1, source_target_pairs={{0,4},{4,0},{8,12},{12,8},{16,20},{20,16},{24,28},{28,24},{1,5},{5... | collective-permute-start | bytes 884744 | tf_op jit(solution)/shard_map/ppermute | solution.py:179
  122.6 10.0 %collective-permute-start.60 = (bf16[384,384]{1,0:T(8,128)(2,1)S(1)}, bf16[384,384]{1,0:T(8,128)(2,1)S(1)}, u32[]{:S(2)}, u32[]{:S(2)}) collective-permute-start(bf16[384,384]{1,0:T(8,128)(2,1)S(1)} %shard_map.75.rest_6_.rest_1_), channel_id=1, source_target_pairs={{0,4},{4,0},{8,12},{12,8},{16,20},{20,16},{24,28},{28,24},{1,5},{5... | collective-permute-start | bytes 884744 | tf_op jit(solution)/shard_map/ppermute | solution.py:179
  140.7 12.3 %collective-permute-start.63 = (bf16[1024,128]{1,0:T(8,128)(2,1)}, bf16[1024,128]{1,0:T(8,128)(2,1)S(1)}, u32[]{:S(2)}, u32[]{:S(2)}) collective-permute-start(bf16[1024,128]{1,0:T(8,128)(2,1)} %shard_map.80), channel_id=1, source_target_pairs={{0,24},{4,28},{8,16},{12,20},{16,8},{20,12},{24,0},{28,4},{1,25},{... | collective-permute-start | bytes 786440 | tf_op jit(solution)/shard_map/ppermute | solution.py:179
  142.8 22.1 %collective-permute-start.62 = (bf16[1024,128]{1,0:T(8,128)(2,1)S(1)}, bf16[1024,128]{1,0:T(8,128)(2,1)}, u32[]{:S(2)}, u32[]{:S(2)}) collective-permute-start(bf16[1024,128]{1,0:T(8,128)(2,1)S(1)} %shard_map.79), channel_id=1, source_target_pairs={{0,16},{4,20},{8,24},{12,28},{16,0},{20,4},{24,8},{28,12},{1,17},{... | collective-permute-start | bytes 786440 | tf_op jit(solution)/shard_map/ppermute | solution.py:179
  142.8 22.1 %collective-permute-start.61 = (bf16[1024,128]{1,0:T(8,128)(2,1)S(1)}, bf16[1024,128]{1,0:T(8,128)(2,1)}, u32[]{:S(2)}, u32[]{:S(2)}) collective-permute-start(bf16[1024,128]{1,0:T(8,128)(2,1)S(1)} %shard_map.78), channel_id=1, source_target_pairs={{0,8},{4,12},{8,0},{12,4},{16,24},{20,28},{24,16},{28,20},{1,9},{5... | collective-permute-start | bytes 786440 | tf_op jit(solution)/shard_map/ppermute | solution.py:179
  149.1 1.7 copy-start.7
  153.0 15.0 %copy-start.16 = (f32[2,4,512]{2,1,0:T(4,128)S(1)}, f32[2,4,512]{2,1,0:T(4,128)}, u32[]{:S(2)}) copy-start(f32[2,4,512]{2,1,0:T(4,128)} %param.8) | copy-start | bytes 49156

commit v5 on v4

--- a/solution.py
+++ b/solution.py
@@ -108,17 +108,15 @@
 
 
 def spread_kernel(s, cap, kb, jb, info, hmask, *rest):
-    (near, far, core), (dense, diagonal, slots) = rest[:-3], rest[-3:]
-    size = cap * BLK + kb * BLK // 4
+    packed, (dense, diagonal, slots) = rest[:-3], rest[-3:]
     row = info[0] ^ (2 * s)
     part = kb * BLK // 4
     for m in range(4):
         col = info[1] ^ m
         start = pl.multiple_of(col % 2 * (cap * BLK), BLK)
-        packed, base = ((near, 0), (core, 0), (far, 0), (core, size))[m]
-        slots[pl.ds(start, cap * BLK), :] = packed[base : base + cap * BLK, :]
+        slots[pl.ds(start, cap * BLK), :] = packed[m][: cap * BLK, :]
         start = pl.multiple_of((2 * (col % 2) + col // 2) * part, part)
-        diagonal[pl.ds(start, part), :] = packed[base + cap * BLK : base + size, :]
+        diagonal[pl.ds(start, part), :] = packed[m][cap * BLK :, :]
         if m % 2 == 0:
             continue
         left = col // 2 * (2 * jb)
@@ -265,11 +263,11 @@
         scratch=[pltpu.VMEM(((cap_h + 2) * BLK, BLK), BF16)],
     )
 
-    def spread(s, near, far, core):
+    def spread(s, near, near_core, far, far_core):
         return call(
             functools.partial(spread_kernel, s, cap_h, kb, jb),
             [info, hmask],
-            [near, far, core],
+            [near, near_core, far, far_core],
             [shape(side, order)],
             scratch=[pltpu.VMEM((side, BLK), BF16), pltpu.VMEM((2 * cap_h * BLK, BLK), BF16)],
         )[0]
@@ -283,12 +281,9 @@
     inner = (z == 1) | (z == 2)
     beside, over, own_y = swap_row(own, 2), along(own, middle), swap_col(own, 2)
 
-    def other_core(near, far):
-        return swap_col(jnp.concatenate([near, far]), 1)
-
     own, beside, over, own_y = after((over, own_y), own, beside, over, own_y)
     over_beside, out_near, beside_y = along(beside, middle), along(over, outward), swap_col(beside, 2)
-    own_core = other_core(own, own_y)
+    own_core, own_y_core = swap_col(own, 1), swap_col(own_y, 1)
     (joined,) = call(
         functools.partial(unpack_kernel, cap, zs, kb, jb),
         [info, pmask],
@@ -297,7 +292,7 @@
     )
 
     dense, first, first_x = [None] * zs, [None] * zs, [None] * zs
-    dense[0] = spread(0, own, own_y, own_core)
+    dense[0] = spread(0, own, own_core, own_y, own_y_core)
     first[0] = multiply(dense[0])
 
     done = (out_near, beside_y, first[0])
@@ -305,23 +300,25 @@
         done, beside, over, over_beside, out_near, beside_y
     )
     slot_2 = jnp.where(inner, over_beside, out_near)
-    out_far, slot_2_y, beside_core = along(over_beside, outward), swap_col(slot_2, 2), other_core(beside, beside_y)
+    out_far, slot_2_y = along(over_beside, outward), swap_col(slot_2, 2)
+    beside_core, beside_y_core = swap_col(beside, 1), swap_col(beside_y, 1)
     first_x[0] = swap_row(first[0], 1)
-    dense[1] = spread(1, beside, beside_y, beside_core)
+    dense[1] = spread(1, beside, beside_core, beside_y, beside_y_core)
     first[1] = multiply(dense[1])
 
     done = (out_far, slot_2_y, first[1], first_x[0])
     over, out_far, slot_2, slot_2_y = after(done, over, out_far, slot_2, slot_2_y)
     slot_3 = jnp.where(inner, over, out_far)
-    slot_3_y, slot_2_core = swap_col(slot_3, 2), other_core(slot_2, slot_2_y)
+    slot_3_y, slot_2_y_core = swap_col(slot_3, 2), swap_col(slot_2_y, 1)
+    slot_2_core, slot_3_core = swap_col(slot_2, 1), swap_col(slot_3, 1)
     first_x[1] = swap_row(first[1], 1)
-    dense[2] = spread(2, slot_2, slot_2_y, slot_2_core)
+    dense[2] = spread(2, slot_2, slot_2_core, slot_2_y, slot_2_y_core)
     first[2] = multiply(dense[2])
     first_x[2] = swap_row(first[2], 1)
 
-    (slot_3_y,) = after((first_x[1], first[2]), slot_3_y)
-    slot_3_core = other_core(slot_3, slot_3_y)
-    dense[3] = spread(3, slot_3, slot_3_y, slot_3_core)
+    (slot_3_y,) = after((first_x[1], first[2], slot_3_core), slot_3_y)
+    slot_3_y_core = swap_col(slot_3_y, 1)
+    dense[3] = spread(3, slot_3, slot_3_core, slot_3_y, slot_3_y_core)
     first[3] = multiply(dense[3])
     first_x[3] = swap_row(first[3], 1)
     (first_joined,) = call(

time: 169 us -> 162 us (0.959)
  starting transfers between devices: 46.7 us -> 40.7 us
  local copies, waits for them, and re-layouts: 6.12 us -> 4.09 us
    ppermute x12, starting transfers between devices: 24.4 us -> 16.8 us  [swap_row(): return lax.ppermute(value, 'row', [(i, i ^ bits) for i in range(count)])]
    ppermute x12, waiting for transfers between devices: 58.7 us -> 51.5 us  [swap_row(): return lax.ppermute(value, 'row', [(i, i ^ bits) for i in range(count)])]
    ppermute x4, waiting for transfers between devices: 3.37 us -> 10.4 us  [along(): lax.ppermute(value, 'row', [(2 * a + x, 2 * b + x) for a, b in pairs for...]
    ppermute x12 -> x16, starting transfers between devices: 7.04 us -> 9.75 us  [swap_col(): return lax.ppermute(value, 'col', [(i, i ^ bits) for i in range(count)])]
    ppermute x2, starting transfers between devices: 8.5 us -> 5.82 us  [beyond(): lax.ppermute(lax.slice_in_dim(potential, last, None, axis=dim), axis, for...]
    unnamed x30 -> x10, local copies, waits for them, and re-layouts: 3.71 us -> 1.68 us
    ppermute x12 -> x16, waiting for transfers between devices: 11.4 us -> 12.1 us  [swap_col(): return lax.ppermute(value, 'col', [(i, i ^ bits) for i in range(count)])]
  transfers between devices with their start and end apart: 32 -> 36, of which waited for: 16 -> 17; matrix products, arithmetic and copies ran while one was open for 3% -> 5% of each run, Pallas kernels for 13% -> 14%
where the time goes in v5:
time: 162 us; the launch traced here: 161 us
  waiting for transfers between devices  74.1 us (46%)
  starting transfers between devices  40.7 us (25%)
  Pallas kernels  35 us (22%)
  other arithmetic  5.1 us (3%)
  local copies, waits for them, and re-layouts  4.09 us (3%)
  between operations  1.78 us (1%)
    ppermute x12, waiting for transfers between devices, swap_row(): return lax.ppermute(value, 'row', [(i, i ^ bits) for i in range(count)])  51.5 us
    pallas_call x18, Pallas kernels, call(): pl.pallas_call(body, out_shape=tuple(outs), in_specs=[SMEM_SPEC] * len(sc...  35 us
    ppermute x12, starting transfers between devices, swap_row(): return lax.ppermute(value, 'row', [(i, i ^ bits) for i in range(count)])  16.8 us
    ppermute x16, waiting for transfers between devices, swap_col(): return lax.ppermute(value, 'col', [(i, i ^ bits) for i in range(count)])  12.1 us
    ppermute x4, waiting for transfers between devices, along(): lax.ppermute(value, 'row', [(2 * a + x, 2 * b + x) for a, b in pairs for...  10.4 us
    ppermute x16, starting transfers between devices, swap_col(): return lax.ppermute(value, 'col', [(i, i ^ bits) for i in range(count)])  9.75 us
    ppermute x2, starting transfers between devices, beyond(): lax.ppermute(lax.slice_in_dim(potential, last, None, axis=dim), axis, for...  5.82 us
    ppermute x4, starting transfers between devices, along(): lax.ppermute(value, 'row', [(2 * a + x, 2 * b + x) for a, b in pairs for...  5.73 us
  transfers between devices with their start and end apart: 36, of which 17 were waited for; matrix products, arithmetic and copies ran while one was open for 5% of the time, Pallas kernels for 14%

profile of v5, /device:TPU:0, one launch (start us, length us, event | category | flops | bytes accessed | tf_op | source)
XLA Modules:
  0.0 160.6 jit_solution(17200757965591631017)
XLA Ops:
  0.1 1.8 %shard_map.64 = (bf16[1024,128]{1,0:T(8,128)(2,1)S(1)}, bf16[1024,128]{1,0:T(8,128)(2,1)S(1)}, bf16[1024,128]{1,0:T(8,128)(2,1)S(1)}, bf16[1024,128]{1,0:T(8,128)(2,1)S(1)}) custom-call(s32[2]{0:T(128)S(1)} %pad_add_fusion.1.info, s32[24,24]{1,0:T(8,128)} %pmask.13, bf16[2,384,768]{2,1,0:T(8,128)(2,1)} %p.3), custom_call_target="tpu_custom_call" | custom-call | bytes 2228224 | tf_op jit(solution)/shard_map/pallas_call | solution.py:24
  1.8 3.1 %collective-permute-start.36 = (bf16[1024,128]{1,0:T(8,128)(2,1)S(1)}, bf16[1024,128]{1,0:T(8,128)(2,1)S(1)}, u32[]{:S(2)}, u32[]{:S(2)}) collective-permute-start(bf16[1024,128]{1,0:T(8,128)(2,1)S(1)} %get-tuple-element.84), channel_id=1, source_target_pairs={{0,8},{4,12},{8,0},{12,4},{16,24},{20,28},{24,16},{28,20},{1,9},{5... | collective-permute-start | bytes 786440 | tf_op jit(solution)/shard_map/ppermute | solution.py:177
  4.9 2.6 %collective-permute-start.37 = (bf16[1024,128]{1,0:T(8,128)(2,1)S(1)}, bf16[1024,128]{1,0:T(8,128)(2,1)S(1)}, u32[]{:S(2)}, u32[]{:S(2)}) collective-permute-start(bf16[1024,128]{1,0:T(8,128)(2,1)S(1)} %get-tuple-element.85), channel_id=1, source_target_pairs={{0,16},{4,20},{8,24},{12,28},{16,0},{20,4},{24,8},{28,12},{1,17},{... | collective-permute-start | bytes 786440 | tf_op jit(solution)/shard_map/ppermute | solution.py:177
  8.2 1.3 collective-permute-start.41
  10.4 4.5 %collective-permute-start.42 = (f32[1,4,512]{2,1,0:T(4,128)S(1)}, f32[1,4,512]{2,1,0:T(4,128)S(1)}, u32[]{:S(2)}, u32[]{:S(2)}) collective-permute-start(f32[1,4,512]{2,1,0:T(4,128)S(1)} %get-tuple-element.130), channel_id=1, source_target_pairs={{0,4},{4,8},{8,12},{12,16},{16,20},{20,24},{24,28},{1,5},{5,9},{9,... | collective-permute-start | bytes 24584 | tf_op jit(solution)/shard_map/ppermute | solution.py:199
  15.0 1.2 collective-permute-done.36.rest_1_
  16.2 1.3 collective-permute-start.43
  17.5 8.8 %collective-permute-done.37.rest_2_ = bf16[1024,128]{1,0:T(8,128)(2,1)S(1)} collective-permute-done((bf16[1024,128]{1,0:T(8,128)(2,1)S(1)}, bf16[1024,128]{1,0:T(8,128)(2,1)S(1)}, u32[]{:S(2)}, u32[]{:S(2)}) %collective-permute-start.37) | collective-permute-done | bytes 262176 | tf_op jit(solution)/shard_map/ppermute | solution.py:177
  26.3 1.3 collective-permute-start.44
  28.6 2.3 %collective-permute-start.40 = (bf16[384,768]{1,0:T(8,128)(2,1)}, bf16[384,768]{1,0:T(8,128)(2,1)S(1)}, u32[]{:S(2)}, u32[]{:S(2)}) collective-permute-start(bf16[384,768]{1,0:T(8,128)(2,1)} %h.1), channel_id=1, source_target_pairs={{0,1},{1,0},{2,3},{3,2},{4,5},{5,4},{6,7},{7,6},{8,9},{9,8},{10,11... | collective-permute-start | bytes 1769480 | tf_op jit(solution)/shard_map/ppermute | solution.py:182
  30.9 1.5 collective-permute-start.39
  33.4 2.9 %shard_map.66 = f32[384,128]{1,0:T(8,128)S(1)} custom-call(f32[2,4,512]{2,1,0:T(4,128)S(1)} %fusion.12.effective, bf16[2,4,384,512]{3,2,1,0:T(8,128)(2,1)} %basis.1), custom_call_target="tpu_custom_call" | custom-call | flops 402653184 | bytes 107479040 | tf_op jit(solution)/shard_map/pallas_call | solution.py:24
  36.8 1.4 collective-permute-start.47
  38.3 2.7 %collective-permute-done.46 = f32[96,128]{1,0:T(8,128)S(1)} collective-permute-done((f32[96,128]{1,0:T(8,128)S(1)}, f32[96,128]{1,0:T(8,128)S(1)}, u32[]{:S(2)}, u32[]{:S(2)}) %collective-permute-start.46) | collective-permute-done | bytes 49184 | tf_op jit(solution)/shard_map/ppermute | solution.py:182
  41.2 1.5 shard_map.67.rest_0_
  42.7 2.1 %collective-permute-start.48 = (bf16[1888,128]{1,0:T(8,128)(2,1)S(1)}, bf16[1888,128]{1,0:T(8,128)(2,1)S(1)}, u32[]{:S(2)}, u32[]{:S(2)}) collective-permute-start(bf16[1888,128]{1,0:T(8,128)(2,1)S(1)} %shard_map.67.rest_0_), channel_id=1, source_target_pairs={{0,8},{4,12},{8,0},{12,4},{16,24},{20,28},{24,16},{28,20},{1,9},{5... | collective-permute-start | bytes 1449992 | tf_op jit(solution)/shard_map/ppermute | solution.py:177
  44.8 1.4 collective-permute-start.49
  47.0 9.4 %collective-permute-done.48.rest_0_ = bf16[1888,128]{1,0:T(8,128)(2,1)S(1)} collective-permute-done((bf16[1888,128]{1,0:T(8,128)(2,1)S(1)}, bf16[1888,128]{1,0:T(8,128)(2,1)S(1)}, u32[]{:S(2)}, u32[]{:S(2)}) %collective-permute-start.48) | collective-permute-done | bytes 483360 | tf_op jit(solution)/shard_map/ppermute | solution.py:177
  56.3 3.0 %collective-permute-done.50.rest_2_ = bf16[1888,128]{1,0:T(8,128)(2,1)} collective-permute-done((bf16[1888,128]{1,0:T(8,128)(2,1)S(1)}, bf16[1888,128]{1,0:T(8,128)(2,1)}, u32[]{:S(2)}, u32[]{:S(2)}) %collective-permute-start.50) | collective-permute-done | bytes 483360 | tf_op jit(solution)/shard_map/ppermute | solution.py:182
  59.9 1.4 collective-permute-start.54
  61.3 1.3 collective-permute-start.55
  63.7 1.9 %shard_map.65.joined = bf16[384,3072]{1,0:T(8,128)(2,1)S(1)} custom-call(s32[2]{0:T(128)S(1)} %pad_add_fusion.1.info, s32[24,24]{1,0:T(8,128)S(1)} %copy-done.10, bf16[1024,128]{1,0:T(8,128)(2,1)S(1)} %get-tuple-element.83.rest_0_, bf16[1024,128]{1,0:T(8,128)(2,1)S(1)} %collective-permute-done.36.rest_1_, ...), custom_call_target="tpu_custom_call" | custom-call | bytes 4456448 | tf_op jit(solution)/shard_map/pallas_call | solution.py:24
  65.6 2.3 %shard_map.68.dense.rest_0_ = bf16[384,3072]{1,0:T(8,128)(2,1)S(1)} custom-call(s32[2]{0:T(128)S(1)} %pad_add_fusion.1.info, s32[24,24]{1,0:T(8,128)} %hmask.9, bf16[1888,128]{1,0:T(8,128)(2,1)S(1)} %shard_map.67.rest_0_, bf16[1888,128]{1,0:T(8,128)(2,1)} %collective-permute-done.51.rest_1_, bf16[1888,128]{1,0:T(8,128)(2,1)} %collective-permute-done.50.rest_2_, ...), custom_call_target="tpu_custom_call" | custom-call | bytes 4292608 | tf_op jit(solution)/shard_map/pallas_call | solution.py:24
  67.9 1.4 shard_map.69.rest_0_.rest_1_
  69.3 7.5 %collective-permute-done.55 = bf16[1888,128]{1,0:T(8,128)(2,1)} collective-permute-done((bf16[1888,128]{1,0:T(8,128)(2,1)}, bf16[1888,128]{1,0:T(8,128)(2,1)}, u32[]{:S(2)}, u32[]{:S(2)}) %collective-permute-start.55) | collective-permute-done | bytes 483360 | tf_op jit(solution)/shard_map/ppermute | solution.py:186
  79.5 1.6 collective-permute-start.60
  81.9 2.0 %shard_map.70.dense.rest_0_ = bf16[384,3072]{1,0:T(8,128)(2,1)S(1)} custom-call(s32[2]{0:T(128)S(1)} %pad_add_fusion.1.info, s32[24,24]{1,0:T(8,128)} %hmask.9, bf16[1888,128]{1,0:T(8,128)(2,1)S(1)} %collective-permute-done.48.rest_0_, bf16[1888,128]{1,0:T(8,128)(2,1)S(1)} %collective-permute-done.57.rest_1_, ...), custom_call_target="tpu_custom_call" | custom-call | bytes 4292608 | tf_op jit(solution)/shard_map/pallas_call | solution.py:24
  84.0 1.4 shard_map.71.rest_2_.rest_1_
  85.4 4.5 %collective-permute-done.53.rest_1_ = bf16[384,384]{1,0:T(8,128)(2,1)S(1)} collective-permute-done((bf16[384,384]{1,0:T(8,128)(2,1)S(1)}, bf16[384,384]{1,0:T(8,128)(2,1)S(1)}, u32[]{:S(2)}, u32[]{:S(2)}) %collective-permute-start.53) | collective-permute-done | bytes 294944 | tf_op jit(solution)/shard_map/ppermute | solution.py:177
  89.8 1.6 %collective-permute-done.61.rest_2_ = bf16[1888,128]{1,0:T(8,128)(2,1)S(1)} collective-permute-done((bf16[1888,128]{1,0:T(8,128)(2,1)S(1)}, bf16[1888,128]{1,0:T(8,128)(2,1)S(1)}, u32[]{:S(2)}, u32[]{:S(2)}) %collective-permute-start.61) | collective-permute-done | bytes 483360 | tf_op jit(solution)/shard_map/ppermute | solution.py:182
  91.5 2.8 %collective-permute-done.60 = bf16[1888,128]{1,0:T(8,128)(2,1)S(1)} collective-permute-done((bf16[1888,128]{1,0:T(8,128)(2,1)}, bf16[1888,128]{1,0:T(8,128)(2,1)S(1)}, u32[]{:S(2)}, u32[]{:S(2)}) %collective-permute-start.60) | collective-permute-done | bytes 483360 | tf_op jit(solution)/shard_map/ppermute | solution.py:186
  96.9 1.8 %shard_map.72.dense.rest_0_ = bf16[384,3072]{1,0:T(8,128)(2,1)S(1)} custom-call(s32[2]{0:T(128)S(1)} %pad_add_fusion.1.info, s32[24,24]{1,0:T(8,128)} %hmask.9, bf16[1888,128]{1,0:T(8,128)(2,1)S(1)} %broadcast_select_fusion.3.rest_0_, bf16[1888,128]{1,0:T(8,128)(2,1)S(1)} %collective-permute-done.62.rest_1_, ...), custom_call_target="tpu_custom_call" | custom-call | bytes 4292608 | tf_op jit(solution)/shard_map/pallas_call | solution.py:24
  98.7 1.4 shard_map.73.rest_4_.rest_1_
  100.1 5.0 %collective-permute-done.59.rest_3_ = bf16[384,384]{1,0:T(8,128)(2,1)S(1)} collective-permute-done((bf16[384,384]{1,0:T(8,128)(2,1)S(1)}, bf16[384,384]{1,0:T(8,128)(2,1)S(1)}, u32[]{:S(2)}, u32[]{:S(2)}) %collective-permute-start.59) | collective-permute-done | bytes 294944 | tf_op jit(solution)/shard_map/ppermute | solution.py:177
  105.1 3.3 %collective-permute-done.66.rest_2_ = bf16[1888,128]{1,0:T(8,128)(2,1)S(1)} collective-permute-done((bf16[1888,128]{1,0:T(8,128)(2,1)S(1)}, bf16[1888,128]{1,0:T(8,128)(2,1)S(1)}, u32[]{:S(2)}, u32[]{:S(2)}) %collective-permute-start.66) | collective-permute-done | bytes 483360 | tf_op jit(solution)/shard_map/ppermute | solution.py:182
  110.3 1.8 %shard_map.74.dense.rest_0_ = bf16[384,3072]{1,0:T(8,128)(2,1)S(1)} custom-call(s32[2]{0:T(128)S(1)} %pad_add_fusion.1.info, s32[24,24]{1,0:T(8,128)} %hmask.9, bf16[1888,128]{1,0:T(8,128)(2,1)S(1)} %broadcast_select_fusion.2.rest_0_, bf16[1888,128]{1,0:T(8,128)(2,1)S(1)} %collective-permute-done.65.rest_1_, ...), custom_call_target="tpu_custom_call" | custom-call | bytes 4292608 | tf_op jit(solution)/shard_map/pallas_call | solution.py:24
  112.1 1.4 shard_map.75.rest_6_.rest_1_
  114.4 3.9 %collective-permute-done.64.rest_5_ = bf16[384,384]{1,0:T(8,128)(2,1)S(1)} collective-permute-done((bf16[384,384]{1,0:T(8,128)(2,1)S(1)}, bf16[384,384]{1,0:T(8,128)(2,1)S(1)}, u32[]{:S(2)}, u32[]{:S(2)}) %collective-permute-start.64) | collective-permute-done | bytes 294944 | tf_op jit(solution)/shard_map/ppermute | solution.py:177
  118.2 5.9 %collective-permute-done.68.rest_7_ = bf16[384,384]{1,0:T(8,128)(2,1)S(1)} collective-permute-done((bf16[384,384]{1,0:T(8,128)(2,1)S(1)}, bf16[384,384]{1,0:T(8,128)(2,1)S(1)}, u32[]{:S(2)}, u32[]{:S(2)}) %collective-permute-start.68) | collective-permute-done | bytes 294944 | tf_op jit(solution)/shard_map/ppermute | solution.py:177
  124.9 2.9 %shard_map.80 = bf16[1024,128]{1,0:T(8,128)(2,1)} custom-call(s32[2]{0:T(128)S(1)} %pad_add_fusion.1.info, s32[24,24]{1,0:T(8,128)S(1)} %copy-done.10, bf16[384,3072]{1,0:T(8,128)(2,1)S(1)} %shard_map.76.joined, bf16[384,3072]{1,0:T(8,128)(2,1)S(1)} %copy-done.7, bf16[384,384]{1,0:T(8,128)(2,1)S(1)} %shard_map.75.rest_6_.rest_1_), custom_call_target="tpu_custom_call" | custom-call | flops 905969664 | bytes 5275648 | tf_op jit(solution)/shard_map/pallas_call | solution.py:24
  127.9 2.2 %shard_map.79 = bf16[1024,128]{1,0:T(8,128)(2,1)S(1)} custom-call(s32[2]{0:T(128)S(1)} %pad_add_fusion.1.info, s32[24,24]{1,0:T(8,128)S(1)} %copy-done.10, bf16[384,3072]{1,0:T(8,128)(2,1)S(1)} %shard_map.76.joined, bf16[384,3072]{1,0:T(8,128)(2,1)S(1)} %shard_map.72.dense.rest_0_, bf16[384,384]{1,0:T(8,128)(2,1)S(1)} %shard_map.73.rest_4_.rest_1_), custom_call_target="tpu_custom_call" | custom-call | flops 905969664 | bytes 5275648 | tf_op jit(solution)/shard_map/pallas_call | solution.py:24
  130.1 2.2 %shard_map.78 = bf16[1024,128]{1,0:T(8,128)(2,1)S(1)} custom-call(s32[2]{0:T(128)S(1)} %pad_add_fusion.1.info, s32[24,24]{1,0:T(8,128)S(1)} %copy-done.10, bf16[384,3072]{1,0:T(8,128)(2,1)S(1)} %shard_map.76.joined, bf16[384,3072]{1,0:T(8,128)(2,1)S(1)} %shard_map.70.dense.rest_0_, bf16[384,384]{1,0:T(8,128)(2,1)S(1)} %shard_map.71.rest_2_.rest_1_), custom_call_target="tpu_custom_call" | custom-call | flops 905969664 | bytes 5275648 | tf_op jit(solution)/shard_map/pallas_call | solution.py:24
  132.4 2.6 %collective-permute-start.71 = (bf16[1024,128]{1,0:T(8,128)(2,1)}, bf16[1024,128]{1,0:T(8,128)(2,1)S(1)}, u32[]{:S(2)}, u32[]{:S(2)}) collective-permute-start(bf16[1024,128]{1,0:T(8,128)(2,1)} %shard_map.80), channel_id=1, source_target_pairs={{0,24},{4,28},{8,16},{12,20},{16,8},{20,12},{24,0},{28,4},{1,25},{... | collective-permute-start | bytes 786440 | tf_op jit(solution)/shard_map/ppermute | solution.py:177
  135.0 1.8 %collective-permute-start.69 = (bf16[1024,128]{1,0:T(8,128)(2,1)S(1)}, bf16[1024,128]{1,0:T(8,128)(2,1)}, u32[]{:S(2)}, u32[]{:S(2)}) collective-permute-start(bf16[1024,128]{1,0:T(8,128)(2,1)S(1)} %shard_map.78), channel_id=1, source_target_pairs={{0,8},{4,12},{8,0},{12,4},{16,24},{20,28},{24,16},{28,20},{1,9},{5... | collective-permute-start | bytes 786440 | tf_op jit(solution)/shard_map/ppermute | solution.py:177
  140.8 1.7 %copy-done.5 = bf16[384,3072]{1,0:T(8,128)(2,1)S(1)} copy-done((bf16[384,3072]{1,0:T(8,128)(2,1)S(1)}, bf16[384,3072]{1,0:T(8,128)(2,1)}, u32[]{:S(2)}) %copy-start.5) | copy-done | bytes 2359320
  142.5 2.2 %shard_map.77.rest_0_ = bf16[1024,128]{1,0:T(8,128)(2,1)S(1)} custom-call(s32[2]{0:T(128)S(1)} %pad_add_fusion.1.info, s32[24,24]{1,0:T(8,128)S(1)} %copy-done.10, bf16[384,3072]{1,0:T(8,128)(2,1)S(1)} %shard_map.76.joined, bf16[384,3072]{1,0:T(8,128)(2,1)S(1)} %copy-done.5, bf16[384,384]{1,0:T(8,128)(2,1)S(1)} %shard_map.69.rest_0_.rest_1_), custom_call_target="tpu_custom_call" | custom-call | flops 905969664 | bytes 5275648 | tf_op jit(solution)/shard_map/pallas_call | solution.py:24
  144.7 12.9 %collective-permute-done.70.rest_2_ = bf16[1024,128]{1,0:T(8,128)(2,1)} collective-permute-done((bf16[1024,128]{1,0:T(8,128)(2,1)S(1)}, bf16[1024,128]{1,0:T(8,128)(2,1)}, u32[]{:S(2)}, u32[]{:S(2)}) %collective-permute-start.70) | collective-permute-done | bytes 262176 | tf_op jit(solution)/shard_map/ppermute | solution.py:177
  157.6 3.0 %shard_map.81 = bf16[2,384,768]{2,1,0:T(8,128)(2,1)} custom-call(s32[2]{0:T(128)S(1)} %pad_add_fusion.1.info, s32[24,24]{1,0:T(8,128)S(1)} %copy-done.10, bf16[2,384,768]{2,1,0:T(8,128)(2,1)} %p.3, bf16[1024,128]{1,0:T(8,128)(2,1)S(1)} %shard_map.77.rest_0_, bf16[1024,128]{1,0:T(8,128)(2,1)} %collective-permute-done.69.rest_1_, ...), custom_call_target="tpu_custom_call" | custom-call | bytes 3407872 | tf_op jit(solution)/shard_map/pallas_call | solution.py:24
  (68 shorter events, 18.9 us)
Async XLA Ops:
  1.8 14.3 %collective-permute-start.36 = (bf16[1024,128]{1,0:T(8,128)(2,1)S(1)}, bf16[1024,128]{1,0:T(8,128)(2,1)S(1)}, u32[]{:S(2)}, u32[]{:S(2)}) collective-permute-start(bf16[1024,128]{1,0:T(8,128)(2,1)S(1)} %get-tuple-element.84), channel_id=1, source_target_pairs={{0,8},{4,12},{8,0},{12,4},{16,24},{20,28},{24,16},{28,20},{1,9},{5... | collective-permute-start | bytes 786440 | tf_op jit(solution)/shard_map/ppermute | solution.py:177
  4.9 21.4 %collective-permute-start.37 = (bf16[1024,128]{1,0:T(8,128)(2,1)S(1)}, bf16[1024,128]{1,0:T(8,128)(2,1)S(1)}, u32[]{:S(2)}, u32[]{:S(2)}) collective-permute-start(bf16[1024,128]{1,0:T(8,128)(2,1)S(1)} %get-tuple-element.85), channel_id=1, source_target_pairs={{0,16},{4,20},{8,24},{12,28},{16,0},{20,4},{24,8},{28,12},{1,17},{... | collective-permute-start | bytes 786440 | tf_op jit(solution)/shard_map/ppermute | solution.py:177
  7.5 20.1 %collective-permute-start.38 = (bf16[1024,128]{1,0:T(8,128)(2,1)S(1)}, bf16[1024,128]{1,0:T(8,128)(2,1)S(1)}, u32[]{:S(2)}, u32[]{:S(2)}) collective-permute-start(bf16[1024,128]{1,0:T(8,128)(2,1)S(1)} %get-tuple-element.86), channel_id=1, source_target_pairs={{0,24},{4,28},{8,16},{12,20},{16,8},{20,12},{24,0},{28,4},{1,25},{... | collective-permute-start | bytes 786440 | tf_op jit(solution)/shard_map/ppermute | solution.py:177
  8.2 24.2 %collective-permute-start.41 = (f32[1,4,512]{2,1,0:T(4,128)S(1)}, f32[1,4,512]{2,1,0:T(4,128)S(1)}, u32[]{:S(2)}, u32[]{:S(2)}) collective-permute-start(f32[1,4,512]{2,1,0:T(4,128)S(1)} %get-tuple-element.129), channel_id=1, source_target_pairs={{4,0},{8,4},{12,8},{16,12},{20,16},{24,20},{28,24},{5,1},{9,5},{13... | collective-permute-start | bytes 24584 | tf_op jit(solution)/shard_map/ppermute | solution.py:200
  10.4 22.0 %collective-permute-start.42 = (f32[1,4,512]{2,1,0:T(4,128)S(1)}, f32[1,4,512]{2,1,0:T(4,128)S(1)}, u32[]{:S(2)}, u32[]{:S(2)}) collective-permute-start(f32[1,4,512]{2,1,0:T(4,128)S(1)} %get-tuple-element.130), channel_id=1, source_target_pairs={{0,4},{4,8},{8,12},{12,16},{16,20},{20,24},{24,28},{1,5},{5,9},{9,... | collective-permute-start | bytes 24584 | tf_op jit(solution)/shard_map/ppermute | solution.py:199
  16.2 14.7 %collective-permute-start.43 = (f32[2,1,512]{2,1,0:T(1,128)S(1)}, f32[2,1,512]{2,1,0:T(1,128)S(1)}, u32[]{:S(2)}, u32[]{:S(2)}) collective-permute-start(f32[2,1,512]{2,1,0:T(1,128)S(1)} %get-tuple-element.131), channel_id=1, source_target_pairs={{1,0},{2,1},{3,2},{5,4},{6,5},{7,6},{9,8},{10,9},{11,10},{13,12},{... | collective-permute-start | bytes 12296 | tf_op jit(solution)/shard_map/ppermute | solution.py:200
  26.3 6.1 %collective-permute-start.44 = (f32[2,1,512]{2,1,0:T(1,128)S(1)}, f32[2,1,512]{2,1,0:T(1,128)S(1)}, u32[]{:S(2)}, u32[]{:S(2)}) collective-permute-start(f32[2,1,512]{2,1,0:T(1,128)S(1)} %get-tuple-element.132), channel_id=1, source_target_pairs={{0,1},{1,2},{2,3},{4,5},{5,6},{6,7},{8,9},{9,10},{10,11},{12,13},{... | collective-permute-start | bytes 12296 | tf_op jit(solution)/shard_map/ppermute | solution.py:199
  28.6 12.6 %collective-permute-start.40 = (bf16[384,768]{1,0:T(8,128)(2,1)}, bf16[384,768]{1,0:T(8,128)(2,1)S(1)}, u32[]{:S(2)}, u32[]{:S(2)}) collective-permute-start(bf16[384,768]{1,0:T(8,128)(2,1)} %h.1), channel_id=1, source_target_pairs={{0,1},{1,0},{2,3},{3,2},{4,5},{5,4},{6,7},{7,6},{8,9},{9,8},{10,11... | collective-permute-start | bytes 1769480 | tf_op jit(solution)/shard_map/ppermute | solution.py:182
  30.9 31.7 %collective-permute-start.39 = (bf16[4096,128]{1,0:T(8,128)(2,1)}, bf16[4096,128]{1,0:T(8,128)(2,1)S(1)}, u32[]{:S(2)}, u32[]{:S(2)}) collective-permute-start(bf16[4096,128]{1,0:T(8,128)(2,1)} %pad_maximum_fusion.5), channel_id=1, source_target_pairs={{0,4},{4,0},{8,12},{12,8},{16,20},{20,16},{24,28},{28,24},{1,5},{5... | collective-permute-start | bytes 3145736 | tf_op jit(solution)/shard_map/ppermute | solution.py:177
  33.4 30.2 %copy-start.10 = (s32[24,24]{1,0:T(8,128)S(1)}, s32[24,24]{1,0:T(8,128)}, u32[]{:S(2)}) copy-start(s32[24,24]{1,0:T(8,128)} %pmask.13) | copy-start | bytes 6916
  36.4 1.9 %collective-permute-start.45 = (f32[96,128]{1,0:T(8,128)S(1)}, f32[96,128]{1,0:T(8,128)S(1)}, u32[]{:S(2)}, u32[]{:S(2)}) collective-permute-start(f32[96,128]{1,0:T(8,128)S(1)} %get-tuple-element.126), channel_id=1, source_target_pairs={{0,1},{1,0},{2,3},{3,2},{4,5},{5,4},{6,7},{7,6},{8,9},{9,8},{10,11... | collective-permute-start | bytes 147464 | tf_op jit(solution)/shard_map/ppermute | solution.py:182
  36.4 4.6 %collective-permute-start.46 = (f32[96,128]{1,0:T(8,128)S(1)}, f32[96,128]{1,0:T(8,128)S(1)}, u32[]{:S(2)}, u32[]{:S(2)}) collective-permute-start(f32[96,128]{1,0:T(8,128)S(1)} %get-tuple-element.128), channel_id=1, source_target_pairs={{0,2},{1,3},{2,0},{3,1},{4,6},{5,7},{6,4},{7,5},{8,10},{9,11},{10,... | collective-permute-start | bytes 147464 | tf_op jit(solution)/shard_map/ppermute | solution.py:182
  36.8 4.3 %collective-permute-start.47 = (f32[96,128]{1,0:T(8,128)S(1)}, f32[96,128]{1,0:T(8,128)S(1)}, u32[]{:S(2)}, u32[]{:S(2)}) collective-permute-start(f32[96,128]{1,0:T(8,128)S(1)} %get-tuple-element.127), channel_id=1, source_target_pairs={{0,3},{1,2},{2,1},{3,0},{4,7},{5,6},{6,5},{7,4},{8,11},{9,10},{10,... | collective-permute-start | bytes 147464 | tf_op jit(solution)/shard_map/ppermute | solution.py:182
  42.7 13.6 %collective-permute-start.48 = (bf16[1888,128]{1,0:T(8,128)(2,1)S(1)}, bf16[1888,128]{1,0:T(8,128)(2,1)S(1)}, u32[]{:S(2)}, u32[]{:S(2)}) collective-permute-start(bf16[1888,128]{1,0:T(8,128)(2,1)S(1)} %shard_map.67.rest_0_), channel_id=1, source_target_pairs={{0,8},{4,12},{8,0},{12,4},{16,24},{20,28},{24,16},{28,20},{1,9},{5... | collective-permute-start | bytes 1449992 | tf_op jit(solution)/shard_map/ppermute | solution.py:177
  44.8 11.5 %collective-permute-start.49 = (bf16[1888,128]{1,0:T(8,128)(2,1)S(1)}, bf16[1888,128]{1,0:T(8,128)(2,1)}, u32[]{:S(2)}, u32[]{:S(2)}) collective-permute-start(bf16[1888,128]{1,0:T(8,128)(2,1)S(1)} %shard_map.67.rest_0_), channel_id=1, source_target_pairs={{8,16},{12,20},{16,8},{20,12},{9,17},{13,21},{17,9},{21,13},{10,18... | collective-permute-start | bytes 1449992 | tf_op jit(solution)/shard_map/ppermute | solution.py:186
  46.3 13.1 %collective-permute-start.50 = (bf16[1888,128]{1,0:T(8,128)(2,1)S(1)}, bf16[1888,128]{1,0:T(8,128)(2,1)}, u32[]{:S(2)}, u32[]{:S(2)}) collective-permute-start(bf16[1888,128]{1,0:T(8,128)(2,1)S(1)} %shard_map.67.rest_0_), channel_id=1, source_target_pairs={{0,2},{1,3},{2,0},{3,1},{4,6},{5,7},{6,4},{7,5},{8,10},{9,11},{10,... | collective-permute-start | bytes 1449992 | tf_op jit(solution)/shard_map/ppermute | solution.py:182
  59.3 6.3 %collective-permute-start.51 = (bf16[1888,128]{1,0:T(8,128)(2,1)S(1)}, bf16[1888,128]{1,0:T(8,128)(2,1)}, u32[]{:S(2)}, u32[]{:S(2)}) collective-permute-start(bf16[1888,128]{1,0:T(8,128)(2,1)S(1)} %shard_map.67.rest_0_), channel_id=1, source_target_pairs={{0,1},{1,0},{2,3},{3,2},{4,5},{5,4},{6,7},{7,6},{8,9},{9,8},{10,11... | collective-permute-start | bytes 1449992 | tf_op jit(solution)/shard_map/ppermute | solution.py:182
  59.3 6.3 %collective-permute-start.52 = (bf16[1888,128]{1,0:T(8,128)(2,1)}, bf16[1888,128]{1,0:T(8,128)(2,1)}, u32[]{:S(2)}, u32[]{:S(2)}) collective-permute-start(bf16[1888,128]{1,0:T(8,128)(2,1)} %collective-permute-done.50.rest_2_), channel_id=1, source_target_pairs={{0,1},{1,0},{2,3},{3,2},{4,5},{5,4},{6,7},{7,6},{8,9},{9,8},{10,11... | collective-permute-start | bytes 1449992 | tf_op jit(solution)/shard_map/ppermute | solution.py:182
  59.9 9.5 %collective-permute-start.54 = (bf16[1888,128]{1,0:T(8,128)(2,1)S(1)}, bf16[1888,128]{1,0:T(8,128)(2,1)}, u32[]{:S(2)}, u32[]{:S(2)}) collective-permute-start(bf16[1888,128]{1,0:T(8,128)(2,1)S(1)} %collective-permute-done.48.rest_0_), channel_id=1, source_target_pairs={{8,16},{12,20},{16,8},{20,12},{9,17},{13,21},{17,9},{21,13},{10,18... | collective-permute-start | bytes 1449992 | tf_op jit(solution)/shard_map/ppermute | solution.py:186
  61.3 15.6 %collective-permute-start.55 = (bf16[1888,128]{1,0:T(8,128)(2,1)}, bf16[1888,128]{1,0:T(8,128)(2,1)}, u32[]{:S(2)}, u32[]{:S(2)}) collective-permute-start(bf16[1888,128]{1,0:T(8,128)(2,1)} %collective-permute-done.49), channel_id=1, source_target_pairs={{8,0},{12,4},{16,24},{20,28},{9,1},{13,5},{17,25},{21,29},{10,2},{... | collective-permute-start | bytes 1449992 | tf_op jit(solution)/shard_map/ppermute | solution.py:186
  62.6 14.3 %collective-permute-start.56 = (bf16[1888,128]{1,0:T(8,128)(2,1)S(1)}, bf16[1888,128]{1,0:T(8,128)(2,1)}, u32[]{:S(2)}, u32[]{:S(2)}) collective-permute-start(bf16[1888,128]{1,0:T(8,128)(2,1)S(1)} %collective-permute-done.48.rest_0_), channel_id=1, source_target_pairs={{0,2},{1,3},{2,0},{3,1},{4,6},{5,7},{6,4},{7,5},{8,10},{9,11},{10,... | collective-permute-start | bytes 1449992 | tf_op jit(solution)/shard_map/ppermute | solution.py:182
  67.9 1.4 copy-start.4
  76.9 5.1 %collective-permute-start.57 = (bf16[1888,128]{1,0:T(8,128)(2,1)S(1)}, bf16[1888,128]{1,0:T(8,128)(2,1)S(1)}, u32[]{:S(2)}, u32[]{:S(2)}) collective-permute-start(bf16[1888,128]{1,0:T(8,128)(2,1)S(1)} %collective-permute-done.48.rest_0_), channel_id=1, source_target_pairs={{0,1},{1,0},{2,3},{3,2},{4,5},{5,4},{6,7},{7,6},{8,9},{9,8},{10,11... | collective-permute-start | bytes 1449992 | tf_op jit(solution)/shard_map/ppermute | solution.py:182
  76.9 5.1 %collective-permute-start.58 = (bf16[1888,128]{1,0:T(8,128)(2,1)}, bf16[1888,128]{1,0:T(8,128)(2,1)S(1)}, u32[]{:S(2)}, u32[]{:S(2)}) collective-permute-start(bf16[1888,128]{1,0:T(8,128)(2,1)} %collective-permute-done.56.rest_2_), channel_id=1, source_target_pairs={{0,1},{1,0},{2,3},{3,2},{4,5},{5,4},{6,7},{7,6},{8,9},{9,8},{10,11... | collective-permute-start | bytes 1449992 | tf_op jit(solution)/shard_map/ppermute | solution.py:182
  78.4 13.0 %collective-permute-start.61 = (bf16[1888,128]{1,0:T(8,128)(2,1)S(1)}, bf16[1888,128]{1,0:T(8,128)(2,1)S(1)}, u32[]{:S(2)}, u32[]{:S(2)}) collective-permute-start(bf16[1888,128]{1,0:T(8,128)(2,1)S(1)} %broadcast_select_fusion.3.rest_0_), channel_id=1, source_target_pairs={{0,2},{1,3},{2,0},{3,1},{4,6},{5,7},{6,4},{7,5},{8,10},{9,11},{10,... | collective-permute-start | bytes 1449992 | tf_op jit(solution)/shard_map/ppermute | solution.py:182
  79.5 14.8 %collective-permute-start.60 = (bf16[1888,128]{1,0:T(8,128)(2,1)}, bf16[1888,128]{1,0:T(8,128)(2,1)S(1)}, u32[]{:S(2)}, u32[]{:S(2)}) collective-permute-start(bf16[1888,128]{1,0:T(8,128)(2,1)} %collective-permute-done.54), channel_id=1, source_target_pairs={{8,0},{12,4},{16,24},{20,28},{9,1},{13,5},{17,25},{21,29},{10,2},{... | collective-permute-start | bytes 1449992 | tf_op jit(solution)/shard_map/ppermute | solution.py:186
  81.1 8.7 %collective-permute-start.53 = (bf16[384,384]{1,0:T(8,128)(2,1)S(1)}, bf16[384,384]{1,0:T(8,128)(2,1)S(1)}, u32[]{:S(2)}, u32[]{:S(2)}) collective-permute-start(bf16[384,384]{1,0:T(8,128)(2,1)S(1)} %shard_map.69.rest_0_.rest_1_), channel_id=1, source_target_pairs={{0,4},{4,0},{8,12},{12,8},{16,20},{20,16},{24,28},{28,24},{1,5},{5... | collective-permute-start | bytes 884744 | tf_op jit(solution)/shard_map/ppermute | solution.py:177
  94.3 2.4 %collective-permute-start.62 = (bf16[1888,128]{1,0:T(8,128)(2,1)S(1)}, bf16[1888,128]{1,0:T(8,128)(2,1)S(1)}, u32[]{:S(2)}, u32[]{:S(2)}) collective-permute-start(bf16[1888,128]{1,0:T(8,128)(2,1)S(1)} %broadcast_select_fusion.3.rest_0_), channel_id=1, source_target_pairs={{0,1},{1,0},{2,3},{3,2},{4,5},{5,4},{6,7},{7,6},{8,9},{9,8},{10,11... | collective-permute-start | bytes 1449992 | tf_op jit(solution)/shard_map/ppermute | solution.py:182
  94.3 2.5 %collective-permute-start.63 = (bf16[1888,128]{1,0:T(8,128)(2,1)S(1)}, bf16[1888,128]{1,0:T(8,128)(2,1)S(1)}, u32[]{:S(2)}, u32[]{:S(2)}) collective-permute-start(bf16[1888,128]{1,0:T(8,128)(2,1)S(1)} %collective-permute-done.61.rest_2_), channel_id=1, source_target_pairs={{0,1},{1,0},{2,3},{3,2},{4,5},{5,4},{6,7},{7,6},{8,9},{9,8},{10,11... | collective-permute-start | bytes 1449992 | tf_op jit(solution)/shard_map/ppermute | solution.py:182
  94.9 10.2 %collective-permute-start.65 = (bf16[1888,128]{1,0:T(8,128)(2,1)S(1)}, bf16[1888,128]{1,0:T(8,128)(2,1)S(1)}, u32[]{:S(2)}, u32[]{:S(2)}) collective-permute-start(bf16[1888,128]{1,0:T(8,128)(2,1)S(1)} %broadcast_select_fusion.2.rest_0_), channel_id=1, source_target_pairs={{0,1},{1,0},{2,3},{3,2},{4,5},{5,4},{6,7},{7,6},{8,9},{9,8},{10,11... | collective-permute-start | bytes 1449992 | tf_op jit(solution)/shard_map/ppermute | solution.py:182
  95.0 13.5 %collective-permute-start.66 = (bf16[1888,128]{1,0:T(8,128)(2,1)S(1)}, bf16[1888,128]{1,0:T(8,128)(2,1)S(1)}, u32[]{:S(2)}, u32[]{:S(2)}) collective-permute-start(bf16[1888,128]{1,0:T(8,128)(2,1)S(1)} %broadcast_select_fusion.2.rest_0_), channel_id=1, source_target_pairs={{0,2},{1,3},{2,0},{3,1},{4,6},{5,7},{6,4},{7,5},{8,10},{9,11},{10,... | collective-permute-start | bytes 1449992 | tf_op jit(solution)/shard_map/ppermute | solution.py:182
  96.0 9.1 %collective-permute-start.59 = (bf16[384,384]{1,0:T(8,128)(2,1)S(1)}, bf16[384,384]{1,0:T(8,128)(2,1)S(1)}, u32[]{:S(2)}, u32[]{:S(2)}) collective-permute-start(bf16[384,384]{1,0:T(8,128)(2,1)S(1)} %shard_map.71.rest_2_.rest_1_), channel_id=1, source_target_pairs={{0,4},{4,0},{8,12},{12,8},{16,20},{20,16},{24,28},{28,24},{1,5},{5... | collective-permute-start | bytes 884744 | tf_op jit(solution)/shard_map/ppermute | solution.py:177
  108.4 1.9 %collective-permute-start.67 = (bf16[1888,128]{1,0:T(8,128)(2,1)S(1)}, bf16[1888,128]{1,0:T(8,128)(2,1)S(1)}, u32[]{:S(2)}, u32[]{:S(2)}) collective-permute-start(bf16[1888,128]{1,0:T(8,128)(2,1)S(1)} %collective-permute-done.66.rest_2_), channel_id=1, source_target_pairs={{0,1},{1,0},{2,3},{3,2},{4,5},{5,4},{6,7},{7,6},{8,9},{9,8},{10,11... | collective-permute-start | bytes 1449992 | tf_op jit(solution)/shard_map/ppermute | solution.py:182
  108.4 9.8 %collective-permute-start.64 = (bf16[384,384]{1,0:T(8,128)(2,1)S(1)}, bf16[384,384]{1,0:T(8,128)(2,1)S(1)}, u32[]{:S(2)}, u32[]{:S(2)}) collective-permute-start(bf16[384,384]{1,0:T(8,128)(2,1)S(1)} %shard_map.73.rest_4_.rest_1_), channel_id=1, source_target_pairs={{0,4},{4,0},{8,12},{12,8},{16,20},{20,16},{24,28},{28,24},{1,5},{5... | collective-permute-start | bytes 884744 | tf_op jit(solution)/shard_map/ppermute | solution.py:177
  112.1 1.4 copy-start.6
  113.6 10.6 %collective-permute-start.68 = (bf16[384,384]{1,0:T(8,128)(2,1)S(1)}, bf16[384,384]{1,0:T(8,128)(2,1)S(1)}, u32[]{:S(2)}, u32[]{:S(2)}) collective-permute-start(bf16[384,384]{1,0:T(8,128)(2,1)S(1)} %shard_map.75.rest_6_.rest_1_), channel_id=1, source_target_pairs={{0,4},{4,0},{8,12},{12,8},{16,20},{20,16},{24,28},{28,24},{1,5},{5... | collective-permute-start | bytes 884744 | tf_op jit(solution)/shard_map/ppermute | solution.py:177
  114.4 10.6 %copy-start.7 = (bf16[384,3072]{1,0:T(8,128)(2,1)S(1)}, bf16[384,3072]{1,0:T(8,128)(2,1)}, u32[]{:S(2)}) copy-start(bf16[384,3072]{1,0:T(8,128)(2,1)} %copy-done.6) | copy-start | bytes 7077892
  132.4 12.4 %collective-permute-start.71 = (bf16[1024,128]{1,0:T(8,128)(2,1)}, bf16[1024,128]{1,0:T(8,128)(2,1)S(1)}, u32[]{:S(2)}, u32[]{:S(2)}) collective-permute-start(bf16[1024,128]{1,0:T(8,128)(2,1)} %shard_map.80), channel_id=1, source_target_pairs={{0,24},{4,28},{8,16},{12,20},{16,8},{20,12},{24,0},{28,4},{1,25},{... | collective-permute-start | bytes 786440 | tf_op jit(solution)/shard_map/ppermute | solution.py:177
  135.0 22.6 %collective-permute-start.70 = (bf16[1024,128]{1,0:T(8,128)(2,1)S(1)}, bf16[1024,128]{1,0:T(8,128)(2,1)}, u32[]{:S(2)}, u32[]{:S(2)}) collective-permute-start(bf16[1024,128]{1,0:T(8,128)(2,1)S(1)} %shard_map.79), channel_id=1, source_target_pairs={{0,16},{4,20},{8,24},{12,28},{16,0},{20,4},{24,8},{28,12},{1,17},{... | collective-permute-start | bytes 786440 | tf_op jit(solution)/shard_map/ppermute | solution.py:177
  135.0 22.6 %collective-permute-start.69 = (bf16[1024,128]{1,0:T(8,128)(2,1)S(1)}, bf16[1024,128]{1,0:T(8,128)(2,1)}, u32[]{:S(2)}, u32[]{:S(2)}) collective-permute-start(bf16[1024,128]{1,0:T(8,128)(2,1)S(1)} %shard_map.78), channel_id=1, source_target_pairs={{0,8},{4,12},{8,0},{12,4},{16,24},{20,28},{24,16},{28,20},{1,9},{5... | collective-permute-start | bytes 786440 | tf_op jit(solution)/shard_map/ppermute | solution.py:177
  140.8 1.7 %copy-start.5 = (bf16[384,3072]{1,0:T(8,128)(2,1)S(1)}, bf16[384,3072]{1,0:T(8,128)(2,1)}, u32[]{:S(2)}) copy-start(bf16[384,3072]{1,0:T(8,128)(2,1)} %copy-done.4) | copy-start | bytes 7077892

commit v6 on v5

--- a/solution.py
+++ b/solution.py
@@ -108,7 +108,7 @@
 
 
 def spread_kernel(s, cap, kb, jb, info, hmask, *rest):
-    packed, (dense, diagonal, slots) = rest[:-3], rest[-3:]
+    joined, packed, (dense, first, diagonal, slots) = rest[0], rest[1:-4], rest[-4:]
     row = info[0] ^ (2 * s)
     part = kb * BLK // 4
     for m in range(4):
@@ -130,6 +130,9 @@
         columns = pl.ds(pl.multiple_of((row * kb + k) * BLK, BLK), BLK)
         both = dense[rows, columns].astype(F32) + diagonal[k * BLK : (k + 1) * BLK, :].astype(F32)
         dense[rows, columns] = both.astype(BF16)
+    first[...] = lax.dot_general(
+        joined[...], dense[...], (((1,), (1,)), ((), ())), preferred_element_type=F32
+    ).astype(BF16)
 
 
 def integral_kernel(effective, basis, total):
@@ -142,12 +145,6 @@
                 weighted = (values.astype(F32) * effective[x, y : y + 1, :]).astype(BF16)
                 here = lax.dot_general(weighted, values, (((1,), (1,)), ((), ())), preferred_element_type=F32)
                 total[rows, :] = here if x + y == 0 else total[rows, :] + here
-
-
-def first_kernel(joined, dense, first):
-    first[...] = lax.dot_general(
-        joined[...], dense[...], (((1,), (1,)), ((), ())), preferred_element_type=F32
-    ).astype(BF16)
 
 
 def second_kernel(slots, cap, zs, kb, jb, info, pmask, joined, *rest):
@@ -267,15 +264,11 @@
         return call(
             functools.partial(spread_kernel, s, cap_h, kb, jb),
             [info, hmask],
-            [near, near_core, far, far_core],
-            [shape(side, order)],
+            [joined, near, near_core, far, far_core],
+            [shape(side, order), shape(wide, side)],
             scratch=[pltpu.VMEM((side, BLK), BF16), pltpu.VMEM((2 * cap_h * BLK, BLK), BF16)],
-        )[0]
-
-    def multiply(rows_of_g):
-        return call(
-            first_kernel, [], [joined, rows_of_g], [shape(wide, side)], flops=2 * side * order * wide
-        )[0]
+            flops=2 * side * order * wide,
+        )
 
     middle, outward = [(1, 2), (2, 1)], [(1, 0), (2, 3)]
     inner = (z == 1) | (z == 2)
@@ -292,8 +285,7 @@
     )
 
     dense, first, first_x = [None] * zs, [None] * zs, [None] * zs
-    dense[0] = spread(0, own, own_core, own_y, own_y_core)
-    first[0] = multiply(dense[0])
+    dense[0], first[0] = spread(0, own, own_core, own_y, own_y_core)
 
     done = (out_near, beside_y, first[0])
     beside, over, over_beside, out_near, beside_y = after(
@@ -303,8 +295,7 @@
     out_far, slot_2_y = along(over_beside, outward), swap_col(slot_2, 2)
     beside_core, beside_y_core = swap_col(beside, 1), swap_col(beside_y, 1)
     first_x[0] = swap_row(first[0], 1)
-    dense[1] = spread(1, beside, beside_core, beside_y, beside_y_core)
-    first[1] = multiply(dense[1])
+    dense[1], first[1] = spread(1, beside, beside_core, beside_y, beside_y_core)
 
     done = (out_far, slot_2_y, first[1], first_x[0])
     over, out_far, slot_2, slot_2_y = after(done, over, out_far, slot_2, slot_2_y)
@@ -312,14 +303,12 @@
     slot_3_y, slot_2_y_core = swap_col(slot_3, 2), swap_col(slot_2_y, 1)
     slot_2_core, slot_3_core = swap_col(slot_2, 1), swap_col(slot_3, 1)
     first_x[1] = swap_row(first[1], 1)
-    dense[2] = spread(2, slot_2, slot_2_core, slot_2_y, slot_2_y_core)
-    first[2] = multiply(dense[2])
+    dense[2], first[2] = spread(2, slot_2, slot_2_core, slot_2_y, slot_2_y_core)
     first_x[2] = swap_row(first[2], 1)
 
     (slot_3_y,) = after((first_x[1], first[2], slot_3_core), slot_3_y)
     slot_3_y_core = swap_col(slot_3_y, 1)
-    dense[3] = spread(3, slot_3, slot_3_core, slot_3_y, slot_3_y_core)
-    first[3] = multiply(dense[3])
+    dense[3], first[3] = spread(3, slot_3, slot_3_core, slot_3_y, slot_3_y_core)
     first_x[3] = swap_row(first[3], 1)
     (first_joined,) = call(
         functools.partial(join_kernel, zs, side),

time: 162 us -> 155 us (0.957)
  waiting for transfers between devices: 74.1 us -> 61.6 us
  Pallas kernels: 35 us -> 38.6 us
  local copies, waits for them, and re-layouts: 4.09 us -> 6.8 us
    ppermute x12, waiting for transfers between devices: 51.5 us -> 42.6 us  [swap_row(): return lax.ppermute(value, 'row', [(i, i ^ bits) for i in range(count)])]
    pallas_call x18 -> x14, Pallas kernels: 35 us -> 38.6 us  [call(): pl.pallas_call(body, out_shape=tuple(outs), in_specs=[SMEM_SPEC] * len(sc...]
    ppermute x4, waiting for transfers between devices: 10.4 us -> 6.84 us  [along(): lax.ppermute(value, 'row', [(2 * a + x, 2 * b + x) for a, b in pairs for...]
    unnamed x10 -> x12, local copies, waits for them, and re-layouts: 1.68 us -> 4.49 us
  transfers between devices with their start and end apart: 36 -> 36, of which waited for: 17 -> 17; matrix products, arithmetic and copies ran while one was open for 5% -> 5% of each run, Pallas kernels for 14% -> 20%
where the time goes in v6:
time: 155 us; the launch traced here: 154 us
  waiting for transfers between devices  61.6 us (40%)
  starting transfers between devices  40.6 us (26%)
  Pallas kernels  38.6 us (25%)
  local copies, waits for them, and re-layouts  6.8 us (4%)
  other arithmetic  4.86 us (3%)
  between operations  1.67 us (1%)
    ppermute x12, waiting for transfers between devices, swap_row(): return lax.ppermute(value, 'row', [(i, i ^ bits) for i in range(count)])  42.6 us
    pallas_call x14, Pallas kernels, call(): pl.pallas_call(body, out_shape=tuple(outs), in_specs=[SMEM_SPEC] * len(sc...  38.6 us
    ppermute x12, starting transfers between devices, swap_row(): return lax.ppermute(value, 'row', [(i, i ^ bits) for i in range(count)])  16.7 us
    ppermute x16, waiting for transfers between devices, swap_col(): return lax.ppermute(value, 'col', [(i, i ^ bits) for i in range(count)])  12.2 us
    ppermute x16, starting transfers between devices, swap_col(): return lax.ppermute(value, 'col', [(i, i ^ bits) for i in range(count)])  9.79 us
    ppermute x4, waiting for transfers between devices, along(): lax.ppermute(value, 'row', [(2 * a + x, 2 * b + x) for a, b in pairs for...  6.84 us
    ppermute x2, starting transfers between devices, beyond(): lax.ppermute(lax.slice_in_dim(potential, last, None, axis=dim), axis, for...  5.82 us
    ppermute x4, starting transfers between devices, along(): lax.ppermute(value, 'row', [(2 * a + x, 2 * b + x) for a, b in pairs for...  5.74 us
  transfers between devices with their start and end apart: 36, of which 17 were waited for; matrix products, arithmetic and copies ran while one was open for 5% of the time, Pallas kernels for 20%

profile of v6, /device:TPU:0, one launch (start us, length us, event | category | flops | bytes accessed | tf_op | source)
XLA Modules:
  0.0 154.2 jit_solution(9898650303674813148)
XLA Ops:
  0.1 1.8 %shard_map.64 = (bf16[1024,128]{1,0:T(8,128)(2,1)S(1)}, bf16[1024,128]{1,0:T(8,128)(2,1)S(1)}, bf16[1024,128]{1,0:T(8,128)(2,1)S(1)}, bf16[1024,128]{1,0:T(8,128)(2,1)S(1)}) custom-call(s32[2]{0:T(128)S(1)} %pad_add_fusion.1.info, s32[24,24]{1,0:T(8,128)} %pmask.13, bf16[2,384,768]{2,1,0:T(8,128)(2,1)} %p.3), custom_call_target="tpu_custom_call" | custom-call | bytes 2228224 | tf_op jit(solution)/shard_map/pallas_call | solution.py:24
  1.8 3.1 %collective-permute-start.36 = (bf16[1024,128]{1,0:T(8,128)(2,1)S(1)}, bf16[1024,128]{1,0:T(8,128)(2,1)S(1)}, u32[]{:S(2)}, u32[]{:S(2)}) collective-permute-start(bf16[1024,128]{1,0:T(8,128)(2,1)S(1)} %get-tuple-element.100), channel_id=1, source_target_pairs={{0,8},{4,12},{8,0},{12,4},{16,24},{20,28},{24,16},{28,20},{1,9},{5... | collective-permute-start | bytes 786440 | tf_op jit(solution)/shard_map/ppermute | solution.py:174
  4.9 2.6 %collective-permute-start.37 = (bf16[1024,128]{1,0:T(8,128)(2,1)S(1)}, bf16[1024,128]{1,0:T(8,128)(2,1)S(1)}, u32[]{:S(2)}, u32[]{:S(2)}) collective-permute-start(bf16[1024,128]{1,0:T(8,128)(2,1)S(1)} %get-tuple-element.101), channel_id=1, source_target_pairs={{0,16},{4,20},{8,24},{12,28},{16,0},{20,4},{24,8},{28,12},{1,17},{... | collective-permute-start | bytes 786440 | tf_op jit(solution)/shard_map/ppermute | solution.py:174
  8.2 1.3 collective-permute-start.41
  10.4 4.5 %collective-permute-start.42 = (f32[1,4,512]{2,1,0:T(4,128)S(1)}, f32[1,4,512]{2,1,0:T(4,128)S(1)}, u32[]{:S(2)}, u32[]{:S(2)}) collective-permute-start(f32[1,4,512]{2,1,0:T(4,128)S(1)} %get-tuple-element.154), channel_id=1, source_target_pairs={{0,4},{4,8},{8,12},{12,16},{16,20},{20,24},{24,28},{1,5},{5,9},{9,... | collective-permute-start | bytes 24584 | tf_op jit(solution)/shard_map/ppermute | solution.py:196
  15.0 1.2 collective-permute-done.36.rest_1_
  16.2 1.3 collective-permute-start.43
  17.5 8.8 %collective-permute-done.37.rest_2_ = bf16[1024,128]{1,0:T(8,128)(2,1)S(1)} collective-permute-done((bf16[1024,128]{1,0:T(8,128)(2,1)S(1)}, bf16[1024,128]{1,0:T(8,128)(2,1)S(1)}, u32[]{:S(2)}, u32[]{:S(2)}) %collective-permute-start.37) | collective-permute-done | bytes 262176 | tf_op jit(solution)/shard_map/ppermute | solution.py:174
  26.3 1.3 collective-permute-start.44
  28.6 2.3 %collective-permute-start.40 = (bf16[384,768]{1,0:T(8,128)(2,1)}, bf16[384,768]{1,0:T(8,128)(2,1)S(1)}, u32[]{:S(2)}, u32[]{:S(2)}) collective-permute-start(bf16[384,768]{1,0:T(8,128)(2,1)} %h.1), channel_id=1, source_target_pairs={{0,1},{1,0},{2,3},{3,2},{4,5},{5,4},{6,7},{7,6},{8,9},{9,8},{10,11... | collective-permute-start | bytes 1769480 | tf_op jit(solution)/shard_map/ppermute | solution.py:179
  30.9 1.5 collective-permute-start.39
  32.5 2.9 %shard_map.66 = f32[384,128]{1,0:T(8,128)S(1)} custom-call(f32[2,4,512]{2,1,0:T(4,128)S(1)} %fusion.12.effective, bf16[2,4,384,512]{3,2,1,0:T(8,128)(2,1)} %basis.1), custom_call_target="tpu_custom_call" | custom-call | flops 402653184 | bytes 107479040 | tf_op jit(solution)/shard_map/pallas_call | solution.py:24
  35.9 1.5 collective-permute-start.47
  37.4 2.7 %collective-permute-done.46 = f32[96,128]{1,0:T(8,128)S(1)} collective-permute-done((f32[96,128]{1,0:T(8,128)S(1)}, f32[96,128]{1,0:T(8,128)S(1)}, u32[]{:S(2)}, u32[]{:S(2)}) %collective-permute-start.46) | collective-permute-done | bytes 49184 | tf_op jit(solution)/shard_map/ppermute | solution.py:179
  40.3 1.5 shard_map.67.rest_1_
  41.8 2.1 %collective-permute-start.48 = (bf16[1888,128]{1,0:T(8,128)(2,1)S(1)}, bf16[1888,128]{1,0:T(8,128)(2,1)S(1)}, u32[]{:S(2)}, u32[]{:S(2)}) collective-permute-start(bf16[1888,128]{1,0:T(8,128)(2,1)S(1)} %shard_map.67.rest_1_), channel_id=1, source_target_pairs={{0,8},{4,12},{8,0},{12,4},{16,24},{20,28},{24,16},{28,20},{1,9},{5... | collective-permute-start | bytes 1449992 | tf_op jit(solution)/shard_map/ppermute | solution.py:174
  43.9 1.5 collective-permute-start.49
  46.1 9.3 %collective-permute-done.48.rest_1_ = bf16[1888,128]{1,0:T(8,128)(2,1)S(1)} collective-permute-done((bf16[1888,128]{1,0:T(8,128)(2,1)S(1)}, bf16[1888,128]{1,0:T(8,128)(2,1)S(1)}, u32[]{:S(2)}, u32[]{:S(2)}) %collective-permute-start.48) | collective-permute-done | bytes 483360 | tf_op jit(solution)/shard_map/ppermute | solution.py:174
  55.4 3.0 %collective-permute-done.50.rest_3_ = bf16[1888,128]{1,0:T(8,128)(2,1)} collective-permute-done((bf16[1888,128]{1,0:T(8,128)(2,1)S(1)}, bf16[1888,128]{1,0:T(8,128)(2,1)}, u32[]{:S(2)}, u32[]{:S(2)}) %collective-permute-start.50) | collective-permute-done | bytes 483360 | tf_op jit(solution)/shard_map/ppermute | solution.py:179
  59.0 1.4 collective-permute-start.54
  60.4 1.3 collective-permute-start.55
  61.7 1.1 collective-permute-start.56
  62.8 1.9 %shard_map.65.rest_0_ = bf16[384,3072]{1,0:T(8,128)(2,1)S(1)} custom-call(s32[2]{0:T(128)S(1)} %pad_add_fusion.1.info, s32[24,24]{1,0:T(8,128)S(1)} %copy-done.8, bf16[1024,128]{1,0:T(8,128)(2,1)S(1)} %get-tuple-element.99.rest_0_, bf16[1024,128]{1,0:T(8,128)(2,1)S(1)} %collective-permute-done.36.rest_1_, ...), custom_call_target="tpu_custom_call" | custom-call | bytes 4456448 | tf_op jit(solution)/shard_map/pallas_call | solution.py:24
  64.7 1.4 copy-done.5
  66.1 4.4 %shard_map.68 = (bf16[384,3072]{1,0:T(8,128)(2,1)S(1)}, bf16[384,384]{1,0:T(8,128)(2,1)S(1)}) custom-call(s32[2]{0:T(128)S(1)} %pad_add_fusion.1.info, s32[24,24]{1,0:T(8,128)S(1)} %copy-done.9, bf16[384,3072]{1,0:T(8,128)(2,1)} %copy-done.5, bf16[1888,128]{1,0:T(8,128)(2,1)S(1)} %shard_map.67.rest_1_, bf16[1888,128]{1,0:T(8,128)(2,1)} %collective-permute-done.51.rest_2_, ...), custom_call_target="tpu_custom_call" | custom-call | flops 905969664 | bytes 6946816 | tf_op jit(solution)/shard_map/pallas_call | solution.py:24
  70.5 1.4 copy-done.6
  71.9 4.0 %collective-permute-done.55 = bf16[1888,128]{1,0:T(8,128)(2,1)} collective-permute-done((bf16[1888,128]{1,0:T(8,128)(2,1)}, bf16[1888,128]{1,0:T(8,128)(2,1)}, u32[]{:S(2)}, u32[]{:S(2)}) %collective-permute-start.55) | collective-permute-done | bytes 483360 | tf_op jit(solution)/shard_map/ppermute | solution.py:183
  78.6 1.6 %collective-permute-start.60 = (bf16[1888,128]{1,0:T(8,128)(2,1)}, bf16[1888,128]{1,0:T(8,128)(2,1)S(1)}, u32[]{:S(2)}, u32[]{:S(2)}) collective-permute-start(bf16[1888,128]{1,0:T(8,128)(2,1)} %collective-permute-done.54), channel_id=1, source_target_pairs={{8,0},{12,4},{16,24},{20,28},{9,1},{13,5},{17,25},{21,29},{10,2},{... | collective-permute-start | bytes 1449992 | tf_op jit(solution)/shard_map/ppermute | solution.py:183
  81.0 4.1 %shard_map.69 = (bf16[384,3072]{1,0:T(8,128)(2,1)S(1)}, bf16[384,384]{1,0:T(8,128)(2,1)S(1)}) custom-call(s32[2]{0:T(128)S(1)} %pad_add_fusion.1.info, s32[24,24]{1,0:T(8,128)S(1)} %copy-done.9, bf16[384,3072]{1,0:T(8,128)(2,1)} %copy-done.5, bf16[1888,128]{1,0:T(8,128)(2,1)S(1)} %collective-permute-done.48.rest_1_, ...), custom_call_target="tpu_custom_call" | custom-call | flops 905969664 | bytes 6946816 | tf_op jit(solution)/shard_map/pallas_call | solution.py:24
  85.1 3.8 %collective-permute-done.53.rest_1_ = bf16[384,384]{1,0:T(8,128)(2,1)S(1)} collective-permute-done((bf16[384,384]{1,0:T(8,128)(2,1)S(1)}, bf16[384,384]{1,0:T(8,128)(2,1)S(1)}, u32[]{:S(2)}, u32[]{:S(2)}) %collective-permute-start.53) | collective-permute-done | bytes 294944 | tf_op jit(solution)/shard_map/ppermute | solution.py:174
  88.9 1.6 %collective-permute-done.61.rest_3_ = bf16[1888,128]{1,0:T(8,128)(2,1)S(1)} collective-permute-done((bf16[1888,128]{1,0:T(8,128)(2,1)S(1)}, bf16[1888,128]{1,0:T(8,128)(2,1)S(1)}, u32[]{:S(2)}, u32[]{:S(2)}) %collective-permute-start.61) | collective-permute-done | bytes 483360 | tf_op jit(solution)/shard_map/ppermute | solution.py:179
  90.6 2.8 %collective-permute-done.60 = bf16[1888,128]{1,0:T(8,128)(2,1)S(1)} collective-permute-done((bf16[1888,128]{1,0:T(8,128)(2,1)}, bf16[1888,128]{1,0:T(8,128)(2,1)S(1)}, u32[]{:S(2)}, u32[]{:S(2)}) %collective-permute-start.60) | collective-permute-done | bytes 483360 | tf_op jit(solution)/shard_map/ppermute | solution.py:183
  95.9 4.0 %shard_map.70 = (bf16[384,3072]{1,0:T(8,128)(2,1)S(1)}, bf16[384,384]{1,0:T(8,128)(2,1)S(1)}) custom-call(s32[2]{0:T(128)S(1)} %pad_add_fusion.1.info, s32[24,24]{1,0:T(8,128)S(1)} %copy-done.9, bf16[384,3072]{1,0:T(8,128)(2,1)} %copy-done.5, bf16[1888,128]{1,0:T(8,128)(2,1)S(1)} %broadcast_select_fusion.3.rest_1_, ...), custom_call_target="tpu_custom_call" | custom-call | flops 905969664 | bytes 6946816 | tf_op jit(solution)/shard_map/pallas_call | solution.py:24
  100.0 4.2 %collective-permute-done.59.rest_3_ = bf16[384,384]{1,0:T(8,128)(2,1)S(1)} collective-permute-done((bf16[384,384]{1,0:T(8,128)(2,1)S(1)}, bf16[384,384]{1,0:T(8,128)(2,1)S(1)}, u32[]{:S(2)}, u32[]{:S(2)}) %collective-permute-start.59) | collective-permute-done | bytes 294944 | tf_op jit(solution)/shard_map/ppermute | solution.py:174
  104.2 3.3 %collective-permute-done.66.rest_3_ = bf16[1888,128]{1,0:T(8,128)(2,1)S(1)} collective-permute-done((bf16[1888,128]{1,0:T(8,128)(2,1)S(1)}, bf16[1888,128]{1,0:T(8,128)(2,1)S(1)}, u32[]{:S(2)}, u32[]{:S(2)}) %collective-permute-start.66) | collective-permute-done | bytes 483360 | tf_op jit(solution)/shard_map/ppermute | solution.py:179
  108.3 1.1 collective-permute-done.67.rest_4_
  109.4 4.0 %shard_map.71 = (bf16[384,3072]{1,0:T(8,128)(2,1)S(1)}, bf16[384,384]{1,0:T(8,128)(2,1)S(1)}) custom-call(s32[2]{0:T(128)S(1)} %pad_add_fusion.1.info, s32[24,24]{1,0:T(8,128)S(1)} %copy-done.9, bf16[384,3072]{1,0:T(8,128)(2,1)} %copy-done.5, bf16[1888,128]{1,0:T(8,128)(2,1)S(1)} %broadcast_select_fusion.2.rest_1_, ...), custom_call_target="tpu_custom_call" | custom-call | flops 905969664 | bytes 6946816 | tf_op jit(solution)/shard_map/pallas_call | solution.py:24
  114.2 3.1 %collective-permute-done.64.rest_5_ = bf16[384,384]{1,0:T(8,128)(2,1)S(1)} collective-permute-done((bf16[384,384]{1,0:T(8,128)(2,1)S(1)}, bf16[384,384]{1,0:T(8,128)(2,1)S(1)}, u32[]{:S(2)}, u32[]{:S(2)}) %collective-permute-start.64) | collective-permute-done | bytes 294944 | tf_op jit(solution)/shard_map/ppermute | solution.py:174
  117.3 5.9 %collective-permute-done.68.rest_7_ = bf16[384,384]{1,0:T(8,128)(2,1)S(1)} collective-permute-done((bf16[384,384]{1,0:T(8,128)(2,1)S(1)}, bf16[384,384]{1,0:T(8,128)(2,1)S(1)}, u32[]{:S(2)}, u32[]{:S(2)}) %collective-permute-start.68) | collective-permute-done | bytes 294944 | tf_op jit(solution)/shard_map/ppermute | solution.py:174
  124.0 2.2 %shard_map.76 = bf16[1024,128]{1,0:T(8,128)(2,1)S(1)} custom-call(s32[2]{0:T(128)S(1)} %pad_add_fusion.1.info, s32[24,24]{1,0:T(8,128)S(1)} %copy-done.8, bf16[384,3072]{1,0:T(8,128)(2,1)S(1)} %shard_map.72.joined, bf16[384,3072]{1,0:T(8,128)(2,1)S(1)} %get-tuple-element.125.rest_0_, bf16[384,384]{1,0:T(8,128)(2,1)S(1)} %get-tuple-element.121.rest_6_.rest_1_), custom_call_target="tpu_custom_call" | custom-call | flops 905969664 | bytes 5275648 | tf_op jit(solution)/shard_map/pallas_call | solution.py:24
  126.3 2.6 %collective-permute-start.71 = (bf16[1024,128]{1,0:T(8,128)(2,1)S(1)}, bf16[1024,128]{1,0:T(8,128)(2,1)S(1)}, u32[]{:S(2)}, u32[]{:S(2)}) collective-permute-start(bf16[1024,128]{1,0:T(8,128)(2,1)S(1)} %shard_map.76), channel_id=1, source_target_pairs={{0,24},{4,28},{8,16},{12,20},{16,8},{20,12},{24,0},{28,4},{1,25},{... | collective-permute-start | bytes 786440 | tf_op jit(solution)/shard_map/ppermute | solution.py:174
  128.9 2.9 %shard_map.75 = bf16[1024,128]{1,0:T(8,128)(2,1)} custom-call(s32[2]{0:T(128)S(1)} %pad_add_fusion.1.info, s32[24,24]{1,0:T(8,128)S(1)} %copy-done.8, bf16[384,3072]{1,0:T(8,128)(2,1)S(1)} %shard_map.72.joined, bf16[384,3072]{1,0:T(8,128)(2,1)S(1)} %get-tuple-element.124.rest_0_, bf16[384,384]{1,0:T(8,128)(2,1)S(1)} %get-tuple-element.117.rest_4_.rest_1_), custom_call_target="tpu_custom_call" | custom-call | flops 905969664 | bytes 5275648 | tf_op jit(solution)/shard_map/pallas_call | solution.py:24
  131.8 2.9 %shard_map.74 = bf16[1024,128]{1,0:T(8,128)(2,1)} custom-call(s32[2]{0:T(128)S(1)} %pad_add_fusion.1.info, s32[24,24]{1,0:T(8,128)S(1)} %copy-done.8, bf16[384,3072]{1,0:T(8,128)(2,1)S(1)} %shard_map.72.joined, bf16[384,3072]{1,0:T(8,128)(2,1)S(1)} %get-tuple-element.123.rest_0_, bf16[384,384]{1,0:T(8,128)(2,1)S(1)} %get-tuple-element.111.rest_2_.rest_1_), custom_call_target="tpu_custom_call" | custom-call | flops 905969664 | bytes 5275648 | tf_op jit(solution)/shard_map/pallas_call | solution.py:24
  134.8 1.8 %collective-permute-start.69 = (bf16[1024,128]{1,0:T(8,128)(2,1)}, bf16[1024,128]{1,0:T(8,128)(2,1)}, u32[]{:S(2)}, u32[]{:S(2)}) collective-permute-start(bf16[1024,128]{1,0:T(8,128)(2,1)} %shard_map.74), channel_id=1, source_target_pairs={{0,8},{4,12},{8,0},{12,4},{16,24},{20,28},{24,16},{28,20},{1,9},{5... | collective-permute-start | bytes 786440 | tf_op jit(solution)/shard_map/ppermute | solution.py:174
  141.1 1.7 %copy-done.7 = bf16[384,3072]{1,0:T(8,128)(2,1)S(1)} copy-done((bf16[384,3072]{1,0:T(8,128)(2,1)S(1)}, bf16[384,3072]{1,0:T(8,128)(2,1)}, u32[]{:S(2)}) %copy-start.7) | copy-done | bytes 2359320
  142.8 2.2 %shard_map.73.rest_0_ = bf16[1024,128]{1,0:T(8,128)(2,1)S(1)} custom-call(s32[2]{0:T(128)S(1)} %pad_add_fusion.1.info, s32[24,24]{1,0:T(8,128)S(1)} %copy-done.8, bf16[384,3072]{1,0:T(8,128)(2,1)S(1)} %shard_map.72.joined, bf16[384,3072]{1,0:T(8,128)(2,1)S(1)} %copy-done.7, bf16[384,384]{1,0:T(8,128)(2,1)S(1)} %get-tuple-element.106.rest_0_.rest_1_), custom_call_target="tpu_custom_call" | custom-call | flops 905969664 | bytes 5275648 | tf_op jit(solution)/shard_map/pallas_call | solution.py:24
  145.0 6.2 %collective-permute-done.70.rest_2_ = bf16[1024,128]{1,0:T(8,128)(2,1)S(1)} collective-permute-done((bf16[1024,128]{1,0:T(8,128)(2,1)}, bf16[1024,128]{1,0:T(8,128)(2,1)S(1)}, u32[]{:S(2)}, u32[]{:S(2)}) %collective-permute-start.70) | collective-permute-done | bytes 262176 | tf_op jit(solution)/shard_map/ppermute | solution.py:174
  151.2 2.9 %shard_map.77 = bf16[2,384,768]{2,1,0:T(8,128)(2,1)} custom-call(s32[2]{0:T(128)S(1)} %pad_add_fusion.1.info, s32[24,24]{1,0:T(8,128)S(1)} %copy-done.8, bf16[2,384,768]{2,1,0:T(8,128)(2,1)} %p.3, bf16[1024,128]{1,0:T(8,128)(2,1)S(1)} %shard_map.73.rest_0_, bf16[1024,128]{1,0:T(8,128)(2,1)} %collective-permute-done.69.rest_1_, ...), custom_call_target="tpu_custom_call" | custom-call | bytes 3407872 | tf_op jit(solution)/shard_map/pallas_call | solution.py:24
  (66 shorter events, 16.3 us)
Async XLA Ops:
  0.0 32.4 %copy-start.11 = (f32[2,4,512]{2,1,0:T(4,128)S(1)}, f32[2,4,512]{2,1,0:T(4,128)}, u32[]{:S(2)}) copy-start(f32[2,4,512]{2,1,0:T(4,128)} %param.8) | copy-start | bytes 49156
  1.8 14.3 %collective-permute-start.36 = (bf16[1024,128]{1,0:T(8,128)(2,1)S(1)}, bf16[1024,128]{1,0:T(8,128)(2,1)S(1)}, u32[]{:S(2)}, u32[]{:S(2)}) collective-permute-start(bf16[1024,128]{1,0:T(8,128)(2,1)S(1)} %get-tuple-element.100), channel_id=1, source_target_pairs={{0,8},{4,12},{8,0},{12,4},{16,24},{20,28},{24,16},{28,20},{1,9},{5... | collective-permute-start | bytes 786440 | tf_op jit(solution)/shard_map/ppermute | solution.py:174
  4.9 21.4 %collective-permute-start.37 = (bf16[1024,128]{1,0:T(8,128)(2,1)S(1)}, bf16[1024,128]{1,0:T(8,128)(2,1)S(1)}, u32[]{:S(2)}, u32[]{:S(2)}) collective-permute-start(bf16[1024,128]{1,0:T(8,128)(2,1)S(1)} %get-tuple-element.101), channel_id=1, source_target_pairs={{0,16},{4,20},{8,24},{12,28},{16,0},{20,4},{24,8},{28,12},{1,17},{... | collective-permute-start | bytes 786440 | tf_op jit(solution)/shard_map/ppermute | solution.py:174
  7.5 20.1 %collective-permute-start.38 = (bf16[1024,128]{1,0:T(8,128)(2,1)S(1)}, bf16[1024,128]{1,0:T(8,128)(2,1)S(1)}, u32[]{:S(2)}, u32[]{:S(2)}) collective-permute-start(bf16[1024,128]{1,0:T(8,128)(2,1)S(1)} %get-tuple-element.102), channel_id=1, source_target_pairs={{0,24},{4,28},{8,16},{12,20},{16,8},{20,12},{24,0},{28,4},{1,25},{... | collective-permute-start | bytes 786440 | tf_op jit(solution)/shard_map/ppermute | solution.py:174
  8.2 24.2 %collective-permute-start.41 = (f32[1,4,512]{2,1,0:T(4,128)S(1)}, f32[1,4,512]{2,1,0:T(4,128)S(1)}, u32[]{:S(2)}, u32[]{:S(2)}) collective-permute-start(f32[1,4,512]{2,1,0:T(4,128)S(1)} %get-tuple-element.153), channel_id=1, source_target_pairs={{4,0},{8,4},{12,8},{16,12},{20,16},{24,20},{28,24},{5,1},{9,5},{13... | collective-permute-start | bytes 24584 | tf_op jit(solution)/shard_map/ppermute | solution.py:197
  10.4 22.0 %collective-permute-start.42 = (f32[1,4,512]{2,1,0:T(4,128)S(1)}, f32[1,4,512]{2,1,0:T(4,128)S(1)}, u32[]{:S(2)}, u32[]{:S(2)}) collective-permute-start(f32[1,4,512]{2,1,0:T(4,128)S(1)} %get-tuple-element.154), channel_id=1, source_target_pairs={{0,4},{4,8},{8,12},{12,16},{16,20},{20,24},{24,28},{1,5},{5,9},{9,... | collective-permute-start | bytes 24584 | tf_op jit(solution)/shard_map/ppermute | solution.py:196
  16.2 14.7 %collective-permute-start.43 = (f32[2,1,512]{2,1,0:T(1,128)S(1)}, f32[2,1,512]{2,1,0:T(1,128)S(1)}, u32[]{:S(2)}, u32[]{:S(2)}) collective-permute-start(f32[2,1,512]{2,1,0:T(1,128)S(1)} %get-tuple-element.155), channel_id=1, source_target_pairs={{1,0},{2,1},{3,2},{5,4},{6,5},{7,6},{9,8},{10,9},{11,10},{13,12},{... | collective-permute-start | bytes 12296 | tf_op jit(solution)/shard_map/ppermute | solution.py:197
  26.3 6.1 %collective-permute-start.44 = (f32[2,1,512]{2,1,0:T(1,128)S(1)}, f32[2,1,512]{2,1,0:T(1,128)S(1)}, u32[]{:S(2)}, u32[]{:S(2)}) collective-permute-start(f32[2,1,512]{2,1,0:T(1,128)S(1)} %get-tuple-element.156), channel_id=1, source_target_pairs={{0,1},{1,2},{2,3},{4,5},{5,6},{6,7},{8,9},{9,10},{10,11},{12,13},{... | collective-permute-start | bytes 12296 | tf_op jit(solution)/shard_map/ppermute | solution.py:196
  28.6 11.7 %copy-start.9 = (s32[24,24]{1,0:T(8,128)S(1)}, s32[24,24]{1,0:T(8,128)}, u32[]{:S(2)}) copy-start(s32[24,24]{1,0:T(8,128)} %hmask.9) | copy-start | bytes 6916
  28.6 11.7 %collective-permute-start.40 = (bf16[384,768]{1,0:T(8,128)(2,1)}, bf16[384,768]{1,0:T(8,128)(2,1)S(1)}, u32[]{:S(2)}, u32[]{:S(2)}) collective-permute-start(bf16[384,768]{1,0:T(8,128)(2,1)} %h.1), channel_id=1, source_target_pairs={{0,1},{1,0},{2,3},{3,2},{4,5},{5,4},{6,7},{7,6},{8,9},{9,8},{10,11... | collective-permute-start | bytes 1769480 | tf_op jit(solution)/shard_map/ppermute | solution.py:179
  30.9 30.8 %collective-permute-start.39 = (bf16[4096,128]{1,0:T(8,128)(2,1)}, bf16[4096,128]{1,0:T(8,128)(2,1)S(1)}, u32[]{:S(2)}, u32[]{:S(2)}) collective-permute-start(bf16[4096,128]{1,0:T(8,128)(2,1)} %pad_maximum_fusion.5), channel_id=1, source_target_pairs={{0,4},{4,0},{8,12},{12,8},{16,20},{20,16},{24,28},{28,24},{1,5},{5... | collective-permute-start | bytes 3145736 | tf_op jit(solution)/shard_map/ppermute | solution.py:174
  32.5 30.3 %copy-start.8 = (s32[24,24]{1,0:T(8,128)S(1)}, s32[24,24]{1,0:T(8,128)}, u32[]{:S(2)}) copy-start(s32[24,24]{1,0:T(8,128)} %pmask.13) | copy-start | bytes 6916
  35.4 1.9 %collective-permute-start.45 = (f32[96,128]{1,0:T(8,128)S(1)}, f32[96,128]{1,0:T(8,128)S(1)}, u32[]{:S(2)}, u32[]{:S(2)}) collective-permute-start(f32[96,128]{1,0:T(8,128)S(1)} %get-tuple-element.150), channel_id=1, source_target_pairs={{0,1},{1,0},{2,3},{3,2},{4,5},{5,4},{6,7},{7,6},{8,9},{9,8},{10,11... | collective-permute-start | bytes 147464 | tf_op jit(solution)/shard_map/ppermute | solution.py:179
  35.5 4.6 %collective-permute-start.46 = (f32[96,128]{1,0:T(8,128)S(1)}, f32[96,128]{1,0:T(8,128)S(1)}, u32[]{:S(2)}, u32[]{:S(2)}) collective-permute-start(f32[96,128]{1,0:T(8,128)S(1)} %get-tuple-element.152), channel_id=1, source_target_pairs={{0,2},{1,3},{2,0},{3,1},{4,6},{5,7},{6,4},{7,5},{8,10},{9,11},{10,... | collective-permute-start | bytes 147464 | tf_op jit(solution)/shard_map/ppermute | solution.py:179
  35.9 4.4 %collective-permute-start.47 = (f32[96,128]{1,0:T(8,128)S(1)}, f32[96,128]{1,0:T(8,128)S(1)}, u32[]{:S(2)}, u32[]{:S(2)}) collective-permute-start(f32[96,128]{1,0:T(8,128)S(1)} %get-tuple-element.151), channel_id=1, source_target_pairs={{0,3},{1,2},{2,1},{3,0},{4,7},{5,6},{6,5},{7,4},{8,11},{9,10},{10,... | collective-permute-start | bytes 147464 | tf_op jit(solution)/shard_map/ppermute | solution.py:179
  41.8 13.6 %collective-permute-start.48 = (bf16[1888,128]{1,0:T(8,128)(2,1)S(1)}, bf16[1888,128]{1,0:T(8,128)(2,1)S(1)}, u32[]{:S(2)}, u32[]{:S(2)}) collective-permute-start(bf16[1888,128]{1,0:T(8,128)(2,1)S(1)} %shard_map.67.rest_1_), channel_id=1, source_target_pairs={{0,8},{4,12},{8,0},{12,4},{16,24},{20,28},{24,16},{28,20},{1,9},{5... | collective-permute-start | bytes 1449992 | tf_op jit(solution)/shard_map/ppermute | solution.py:174
  43.9 11.6 %collective-permute-start.49 = (bf16[1888,128]{1,0:T(8,128)(2,1)S(1)}, bf16[1888,128]{1,0:T(8,128)(2,1)}, u32[]{:S(2)}, u32[]{:S(2)}) collective-permute-start(bf16[1888,128]{1,0:T(8,128)(2,1)S(1)} %shard_map.67.rest_1_), channel_id=1, source_target_pairs={{8,16},{12,20},{16,8},{20,12},{9,17},{13,21},{17,9},{21,13},{10,18... | collective-permute-start | bytes 1449992 | tf_op jit(solution)/shard_map/ppermute | solution.py:183
  45.3 13.1 %collective-permute-start.50 = (bf16[1888,128]{1,0:T(8,128)(2,1)S(1)}, bf16[1888,128]{1,0:T(8,128)(2,1)}, u32[]{:S(2)}, u32[]{:S(2)}) collective-permute-start(bf16[1888,128]{1,0:T(8,128)(2,1)S(1)} %shard_map.67.rest_1_), channel_id=1, source_target_pairs={{0,2},{1,3},{2,0},{3,1},{4,6},{5,7},{6,4},{7,5},{8,10},{9,11},{10,... | collective-permute-start | bytes 1449992 | tf_op jit(solution)/shard_map/ppermute | solution.py:179
  58.4 7.7 %collective-permute-start.51 = (bf16[1888,128]{1,0:T(8,128)(2,1)S(1)}, bf16[1888,128]{1,0:T(8,128)(2,1)}, u32[]{:S(2)}, u32[]{:S(2)}) collective-permute-start(bf16[1888,128]{1,0:T(8,128)(2,1)S(1)} %shard_map.67.rest_1_), channel_id=1, source_target_pairs={{0,1},{1,0},{2,3},{3,2},{4,5},{5,4},{6,7},{7,6},{8,9},{9,8},{10,11... | collective-permute-start | bytes 1449992 | tf_op jit(solution)/shard_map/ppermute | solution.py:179
  58.4 7.7 %collective-permute-start.52 = (bf16[1888,128]{1,0:T(8,128)(2,1)}, bf16[1888,128]{1,0:T(8,128)(2,1)}, u32[]{:S(2)}, u32[]{:S(2)}) collective-permute-start(bf16[1888,128]{1,0:T(8,128)(2,1)} %collective-permute-done.50.rest_3_), channel_id=1, source_target_pairs={{0,1},{1,0},{2,3},{3,2},{4,5},{5,4},{6,7},{7,6},{8,9},{9,8},{10,11... | collective-permute-start | bytes 1449992 | tf_op jit(solution)/shard_map/ppermute | solution.py:179
  59.0 13.0 %collective-permute-start.54 = (bf16[1888,128]{1,0:T(8,128)(2,1)S(1)}, bf16[1888,128]{1,0:T(8,128)(2,1)}, u32[]{:S(2)}, u32[]{:S(2)}) collective-permute-start(bf16[1888,128]{1,0:T(8,128)(2,1)S(1)} %collective-permute-done.48.rest_1_), channel_id=1, source_target_pairs={{8,16},{12,20},{16,8},{20,12},{9,17},{13,21},{17,9},{21,13},{10,18... | collective-permute-start | bytes 1449992 | tf_op jit(solution)/shard_map/ppermute | solution.py:183
  60.4 15.6 %collective-permute-start.55 = (bf16[1888,128]{1,0:T(8,128)(2,1)}, bf16[1888,128]{1,0:T(8,128)(2,1)}, u32[]{:S(2)}, u32[]{:S(2)}) collective-permute-start(bf16[1888,128]{1,0:T(8,128)(2,1)} %collective-permute-done.49), channel_id=1, source_target_pairs={{8,0},{12,4},{16,24},{20,28},{9,1},{13,5},{17,25},{21,29},{10,2},{... | collective-permute-start | bytes 1449992 | tf_op jit(solution)/shard_map/ppermute | solution.py:183
  61.7 14.3 %collective-permute-start.56 = (bf16[1888,128]{1,0:T(8,128)(2,1)S(1)}, bf16[1888,128]{1,0:T(8,128)(2,1)}, u32[]{:S(2)}, u32[]{:S(2)}) collective-permute-start(bf16[1888,128]{1,0:T(8,128)(2,1)S(1)} %collective-permute-done.48.rest_1_), channel_id=1, source_target_pairs={{0,2},{1,3},{2,0},{3,1},{4,6},{5,7},{6,4},{7,5},{8,10},{9,11},{10,... | collective-permute-start | bytes 1449992 | tf_op jit(solution)/shard_map/ppermute | solution.py:179
  64.7 1.4 copy-start.5
  70.5 1.4 copy-start.6
  75.9 5.1 %collective-permute-start.57 = (bf16[1888,128]{1,0:T(8,128)(2,1)S(1)}, bf16[1888,128]{1,0:T(8,128)(2,1)S(1)}, u32[]{:S(2)}, u32[]{:S(2)}) collective-permute-start(bf16[1888,128]{1,0:T(8,128)(2,1)S(1)} %collective-permute-done.48.rest_1_), channel_id=1, source_target_pairs={{0,1},{1,0},{2,3},{3,2},{4,5},{5,4},{6,7},{7,6},{8,9},{9,8},{10,11... | collective-permute-start | bytes 1449992 | tf_op jit(solution)/shard_map/ppermute | solution.py:179
  75.9 5.1 %collective-permute-start.58 = (bf16[1888,128]{1,0:T(8,128)(2,1)}, bf16[1888,128]{1,0:T(8,128)(2,1)S(1)}, u32[]{:S(2)}, u32[]{:S(2)}) collective-permute-start(bf16[1888,128]{1,0:T(8,128)(2,1)} %collective-permute-done.56.rest_3_), channel_id=1, source_target_pairs={{0,1},{1,0},{2,3},{3,2},{4,5},{5,4},{6,7},{7,6},{8,9},{9,8},{10,11... | collective-permute-start | bytes 1449992 | tf_op jit(solution)/shard_map/ppermute | solution.py:179
  77.5 13.0 %collective-permute-start.61 = (bf16[1888,128]{1,0:T(8,128)(2,1)S(1)}, bf16[1888,128]{1,0:T(8,128)(2,1)S(1)}, u32[]{:S(2)}, u32[]{:S(2)}) collective-permute-start(bf16[1888,128]{1,0:T(8,128)(2,1)S(1)} %broadcast_select_fusion.3.rest_1_), channel_id=1, source_target_pairs={{0,2},{1,3},{2,0},{3,1},{4,6},{5,7},{6,4},{7,5},{8,10},{9,11},{10,... | collective-permute-start | bytes 1449992 | tf_op jit(solution)/shard_map/ppermute | solution.py:179
  78.6 14.8 %collective-permute-start.60 = (bf16[1888,128]{1,0:T(8,128)(2,1)}, bf16[1888,128]{1,0:T(8,128)(2,1)S(1)}, u32[]{:S(2)}, u32[]{:S(2)}) collective-permute-start(bf16[1888,128]{1,0:T(8,128)(2,1)} %collective-permute-done.54), channel_id=1, source_target_pairs={{8,0},{12,4},{16,24},{20,28},{9,1},{13,5},{17,25},{21,29},{10,2},{... | collective-permute-start | bytes 1449992 | tf_op jit(solution)/shard_map/ppermute | solution.py:183
  80.2 8.7 %collective-permute-start.53 = (bf16[384,384]{1,0:T(8,128)(2,1)S(1)}, bf16[384,384]{1,0:T(8,128)(2,1)S(1)}, u32[]{:S(2)}, u32[]{:S(2)}) collective-permute-start(bf16[384,384]{1,0:T(8,128)(2,1)S(1)} %get-tuple-element.106.rest_0_.rest_1_), channel_id=1, source_target_pairs={{0,4},{4,0},{8,12},{12,8},{16,20},{20,16},{24,28},{28,24},{1,5},{5... | collective-permute-start | bytes 884744 | tf_op jit(solution)/shard_map/ppermute | solution.py:174
  93.4 2.4 %collective-permute-start.62 = (bf16[1888,128]{1,0:T(8,128)(2,1)S(1)}, bf16[1888,128]{1,0:T(8,128)(2,1)S(1)}, u32[]{:S(2)}, u32[]{:S(2)}) collective-permute-start(bf16[1888,128]{1,0:T(8,128)(2,1)S(1)} %broadcast_select_fusion.3.rest_1_), channel_id=1, source_target_pairs={{0,1},{1,0},{2,3},{3,2},{4,5},{5,4},{6,7},{7,6},{8,9},{9,8},{10,11... | collective-permute-start | bytes 1449992 | tf_op jit(solution)/shard_map/ppermute | solution.py:179
  93.4 2.5 %collective-permute-start.63 = (bf16[1888,128]{1,0:T(8,128)(2,1)S(1)}, bf16[1888,128]{1,0:T(8,128)(2,1)S(1)}, u32[]{:S(2)}, u32[]{:S(2)}) collective-permute-start(bf16[1888,128]{1,0:T(8,128)(2,1)S(1)} %collective-permute-done.61.rest_3_), channel_id=1, source_target_pairs={{0,1},{1,0},{2,3},{3,2},{4,5},{5,4},{6,7},{7,6},{8,9},{9,8},{10,11... | collective-permute-start | bytes 1449992 | tf_op jit(solution)/shard_map/ppermute | solution.py:179
  94.0 10.2 %collective-permute-start.65 = (bf16[1888,128]{1,0:T(8,128)(2,1)S(1)}, bf16[1888,128]{1,0:T(8,128)(2,1)S(1)}, u32[]{:S(2)}, u32[]{:S(2)}) collective-permute-start(bf16[1888,128]{1,0:T(8,128)(2,1)S(1)} %broadcast_select_fusion.2.rest_1_), channel_id=1, source_target_pairs={{0,1},{1,0},{2,3},{3,2},{4,5},{5,4},{6,7},{7,6},{8,9},{9,8},{10,11... | collective-permute-start | bytes 1449992 | tf_op jit(solution)/shard_map/ppermute | solution.py:179
  94.0 13.5 %collective-permute-start.66 = (bf16[1888,128]{1,0:T(8,128)(2,1)S(1)}, bf16[1888,128]{1,0:T(8,128)(2,1)S(1)}, u32[]{:S(2)}, u32[]{:S(2)}) collective-permute-start(bf16[1888,128]{1,0:T(8,128)(2,1)S(1)} %broadcast_select_fusion.2.rest_1_), channel_id=1, source_target_pairs={{0,2},{1,3},{2,0},{3,1},{4,6},{5,7},{6,4},{7,5},{8,10},{9,11},{10,... | collective-permute-start | bytes 1449992 | tf_op jit(solution)/shard_map/ppermute | solution.py:179
  95.1 9.1 %collective-permute-start.59 = (bf16[384,384]{1,0:T(8,128)(2,1)S(1)}, bf16[384,384]{1,0:T(8,128)(2,1)S(1)}, u32[]{:S(2)}, u32[]{:S(2)}) collective-permute-start(bf16[384,384]{1,0:T(8,128)(2,1)S(1)} %get-tuple-element.111.rest_2_.rest_1_), channel_id=1, source_target_pairs={{0,4},{4,0},{8,12},{12,8},{16,20},{20,16},{24,28},{28,24},{1,5},{5... | collective-permute-start | bytes 884744 | tf_op jit(solution)/shard_map/ppermute | solution.py:174
  107.5 1.9 %collective-permute-start.67 = (bf16[1888,128]{1,0:T(8,128)(2,1)S(1)}, bf16[1888,128]{1,0:T(8,128)(2,1)S(1)}, u32[]{:S(2)}, u32[]{:S(2)}) collective-permute-start(bf16[1888,128]{1,0:T(8,128)(2,1)S(1)} %collective-permute-done.66.rest_3_), channel_id=1, source_target_pairs={{0,1},{1,0},{2,3},{3,2},{4,5},{5,4},{6,7},{7,6},{8,9},{9,8},{10,11... | collective-permute-start | bytes 1449992 | tf_op jit(solution)/shard_map/ppermute | solution.py:179
  107.5 9.8 %collective-permute-start.64 = (bf16[384,384]{1,0:T(8,128)(2,1)S(1)}, bf16[384,384]{1,0:T(8,128)(2,1)S(1)}, u32[]{:S(2)}, u32[]{:S(2)}) collective-permute-start(bf16[384,384]{1,0:T(8,128)(2,1)S(1)} %get-tuple-element.117.rest_4_.rest_1_), channel_id=1, source_target_pairs={{0,4},{4,0},{8,12},{12,8},{16,20},{20,16},{24,28},{28,24},{1,5},{5... | collective-permute-start | bytes 884744 | tf_op jit(solution)/shard_map/ppermute | solution.py:174
  113.4 9.8 %collective-permute-start.68 = (bf16[384,384]{1,0:T(8,128)(2,1)S(1)}, bf16[384,384]{1,0:T(8,128)(2,1)S(1)}, u32[]{:S(2)}, u32[]{:S(2)}) collective-permute-start(bf16[384,384]{1,0:T(8,128)(2,1)S(1)} %get-tuple-element.121.rest_6_.rest_1_), channel_id=1, source_target_pairs={{0,4},{4,0},{8,12},{12,8},{16,20},{20,16},{24,28},{28,24},{1,5},{5... | collective-permute-start | bytes 884744 | tf_op jit(solution)/shard_map/ppermute | solution.py:174
  126.3 18.7 %collective-permute-start.71 = (bf16[1024,128]{1,0:T(8,128)(2,1)S(1)}, bf16[1024,128]{1,0:T(8,128)(2,1)S(1)}, u32[]{:S(2)}, u32[]{:S(2)}) collective-permute-start(bf16[1024,128]{1,0:T(8,128)(2,1)S(1)} %shard_map.76), channel_id=1, source_target_pairs={{0,24},{4,28},{8,16},{12,20},{16,8},{20,12},{24,0},{28,4},{1,25},{... | collective-permute-start | bytes 786440 | tf_op jit(solution)/shard_map/ppermute | solution.py:174
  131.8 19.4 %collective-permute-start.70 = (bf16[1024,128]{1,0:T(8,128)(2,1)}, bf16[1024,128]{1,0:T(8,128)(2,1)S(1)}, u32[]{:S(2)}, u32[]{:S(2)}) collective-permute-start(bf16[1024,128]{1,0:T(8,128)(2,1)} %shard_map.75), channel_id=1, source_target_pairs={{0,16},{4,20},{8,24},{12,28},{16,0},{20,4},{24,8},{28,12},{1,17},{... | collective-permute-start | bytes 786440 | tf_op jit(solution)/shard_map/ppermute | solution.py:174
  134.8 16.5 %collective-permute-start.69 = (bf16[1024,128]{1,0:T(8,128)(2,1)}, bf16[1024,128]{1,0:T(8,128)(2,1)}, u32[]{:S(2)}, u32[]{:S(2)}) collective-permute-start(bf16[1024,128]{1,0:T(8,128)(2,1)} %shard_map.74), channel_id=1, source_target_pairs={{0,8},{4,12},{8,0},{12,4},{16,24},{20,28},{24,16},{28,20},{1,9},{5... | collective-permute-start | bytes 786440 | tf_op jit(solution)/shard_map/ppermute | solution.py:174
  141.1 1.7 %copy-start.7 = (bf16[384,3072]{1,0:T(8,128)(2,1)S(1)}, bf16[384,3072]{1,0:T(8,128)(2,1)}, u32[]{:S(2)}) copy-start(bf16[384,3072]{1,0:T(8,128)(2,1)} %copy-done.6) | copy-start | bytes 7077892
